TPU v7x, 512 devices: a whole 4x4x16 slice. The times are simulated.
512 devices in a mesh: layer: 8 (over x_lo, y), ex: 64 (over z, x_hi, core).
Axes of the slice: x: 4 (x_hi: 2, x_lo: 2; x = x_hi * 2 + x_lo), y: 4, z: 16, core: 2. Of those that a mesh axis runs over, the one named last changes fastest.
Arguments:
- queries: bfloat16 [8, 512, 4096], P('layer', 'ex'), may hold values from -6 to 6
- fisher: bfloat16 [8, 4096, 4096], P('layer', None, 'ex'), may hold values from -0.2 to 3, as said below
- train_grads: bfloat16 [8, 24576, 4096], P('layer', 'ex'), may hold values from -0.09375 to 0.09375
Outputs:
- scores: float32 [512, 24576], P('layer', 'ex')
Inputs may be any that keep to these rules, and one draw needn't show every extreme that they name: fisher[l] is symmetric for every layer l.
All inputs are finite; a program needn't handle non-finite values.
Results may differ from a plain program's by a relative error of at most 0.0029.
Values may be sent and summed in bfloat16 or wider, within the bound.
No kernel may reach another device: no remote copies, remote signals or barrier semaphores. Data moves between devices by JAX's collectives and lax.ppermute only.
A program may use at most 64 MiB of HBM per device.

v0:
```python
import jax
import jax.numpy as jnp
from jax import lax
from jax.sharding import PartitionSpec as P


def on_device(queries, fisher, train_grads):
    fisher_cols = fisher[0]
    train_rows = train_grads[0]
    pre_block = jnp.dot(
        lax.all_gather(queries, "ex", axis=1, tiled=True)[0],
        fisher_cols,
        preferred_element_type=jnp.float32,
    ).astype(jnp.bfloat16)
    assembled = lax.all_gather(pre_block, "ex", axis=1, tiled=True)
    partial_value = lax.dot_general(
        assembled, train_rows, (((1,), (1,)), ((), ())), preferred_element_type=jnp.float32
    )
    summed = lax.psum(partial_value, "layer")
    row_count = partial_value.shape[0] // lax.axis_size("layer")
    return lax.dynamic_slice_in_dim(summed, lax.axis_index("layer") * row_count, row_count, 0)


def solution(mesh):
    in_specs = (P("layer", "ex", None), P("layer", None, "ex"), P("layer", "ex", None))
    out_specs = P("layer", "ex")
    return jax.shard_map(
        on_device, mesh=mesh, in_specs=in_specs, out_specs=out_specs, check_vma=False
    )
```

profile of v0, /device:TPU:1, one launch (start us, length us, event | category | flops | bytes accessed | tf_op | source)
XLA Modules:
  0.0 411.5 jit_solution(9188737300585717732)
XLA Ops:
  6.5 0.0 copy-start
  6.5 0.0 all-gather.3.cloned.1.call-start
  6.5 0.7 all-gather.3.cloned.1.call-update
  7.3 0.0 all-gather.5.cloned.1.call-start
  7.3 160.1 %all-gather.3.cloned.1.call-done = bf16[1,512,4096]{2,1,0:T(8,128)(2,1)} async-done(((bf16[1,8,4096]{2,1,0:T(8,128)(2,1)}), bf16[1,512,4096]{2,1,0:T(8,128)(2,1)}) %all-gather.3.cloned.1.call-update) | async-done | bytes 4194320 | tf_op jit(solution)/shard_map/all_gather | solution.py:11
  167.4 4.3 %fusion.4 = bf16[512,64]{0,1:T(8,128)(2,1)} fusion(bf16[1,512,4096]{2,1,0:T(8,128)(2,1)} %all-gather.3.cloned.1.call-done, bf16[1,4096,64]{1,2,0:T(8,128)(2,1)} %param.4), kind=kOutput, calls=%fused_computation.4 | convolution fusion | flops 268468224 | bytes 4784128 | tf_op jit(solution)/shard_map/dot_general | solution.py:10
  171.7 0.0 all-gather.5.cloned.1.call-update
  171.8 0.0 all-reduce.2.cloned.1.call-start
  171.8 145.6 %all-gather.5.cloned.1.call-done = bf16[512,4096]{0,1:T(8,128)(2,1)} async-done(((bf16[512,64]{0,1:T(8,128)(2,1)}), bf16[512,4096]{0,1:T(8,128)(2,1)}) %all-gather.5.cloned.1.call-update) | async-done | bytes 4194320 | tf_op jit(solution)/shard_map/all_gather | solution.py:15
  317.4 0.0 copy-done
  317.4 5.5 %fusion.2 = f32[512,384]{1,0:T(8,128)} fusion(bf16[512,4096]{0,1:T(8,128)(2,1)} %all-gather.5.cloned.1.call-done, bf16[1,384,4096]{2,1,0:T(8,128)(2,1)S(1)} %copy-done), kind=kOutput, calls=%fused_computation.2 | convolution fusion | flops 1610612736 | bytes 8126464 | tf_op jit(solution)/shard_map/dot_general | solution.py:16
  322.8 0.0 all-reduce.2.cloned.1.call-update
  322.9 80.5 %all-reduce.2.cloned.1.call-done = f32[512,384]{1,0:T(8,128)} async-done(((f32[512,384]{1,0:T(8,128)}), f32[512,384]{1,0:T(8,128)}) %all-reduce.2.cloned.1.call-update) | async-done | bytes 786448 | tf_op jit(solution)/shard_map/psum | solution.py:19
  403.4 1.5 constant_dynamic-slice_fusion
Async XLA Ops:
  6.5 310.9 %copy-start = (bf16[1,384,4096]{2,1,0:T(8,128)(2,1)S(1)}, bf16[1,384,4096]{2,1,0:T(8,128)(2,1)}, u32[]{:S(2)}) copy-start(bf16[1,384,4096]{2,1,0:T(8,128)(2,1)} %param.5) | copy-start | bytes 9437188
  6.5 160.9 %all-gather.3.cloned.1.call-start = ((), (), s32[]{:S(2)}) async-start(), calls=%async_computation | async-start | bytes 4259840 | tf_op jit(solution)/shard_map/all_gather | solution.py:11
  7.3 310.1 %all-gather.5.cloned.1.call-start = ((), (), s32[]{:S(2)}) async-start(), calls=%async_computation.1 | async-start | bytes 4259840 | tf_op jit(solution)/shard_map/all_gather | solution.py:15
  171.8 231.6 %all-reduce.2.cloned.1.call-start = ((), (), s32[]{:S(2)}) async-start(), calls=%async_computation.2 | async-start | bytes 1572864 | tf_op jit(solution)/shard_map/psum | solution.py:19
Sparse Core Ops, SparseCore 0:
  10.7 156.7 all-gather.2
  171.9 145.4 all-gather.4
  323.0 80.3 all-reduce.1
where the time goes:
time: 415 us; the launch traced here: 411 us
  waiting for transfers between devices  387 us (93%)
  between operations  13.1 us (3%)
  matrix products  9.78 us (2%)
    all_gather x1, waiting for transfers between devices, on_device(): lax.all_gather(queries, 'ex', axis=1, tiled=True)[0]  160 us
    all_gather x1, waiting for transfers between devices, on_device(): assembled = lax.all_gather(pre_block, 'ex', axis=1, tiled=True)  146 us
    psum x1, waiting for transfers between devices, on_device(): summed = lax.psum(partial_value, 'layer')  80.5 us
  transfers between devices with their start and end apart: 3, of which 3 were waited for; matrix products, arithmetic and copies ran while one was open for 0% of the time, Pallas kernels for 0%

commit v1 on v0

v1 whole, which is shorter than its diff:
```python
import jax
import jax.numpy as jnp
from jax import lax
from jax.sharding import Mesh, PartitionSpec as P

TOP = 14.0


def exponent_of(peak):
    return jnp.clip(jnp.floor(jnp.log2(jnp.maximum(peak, 1e-37))), -100.0, 100.0)


def on_device(queries, fisher, train_grads):
    width = queries.shape[2]
    fisher_slab = lax.all_gather(fisher[0].T, ("xh", "c"), axis=0, tiled=True)
    train_chip = lax.all_gather(train_grads[0], "c", axis=0, tiled=True)

    own = queries[0].astype(jnp.float32)
    exponent = exponent_of(jnp.max(jnp.abs(own), axis=1, keepdims=True))
    scaled = (own * jnp.exp2(TOP - exponent)).astype(jnp.float16)
    tail = jnp.broadcast_to(exponent, (own.shape[0], 128)).astype(jnp.float16)
    rows = lax.all_gather(jnp.concatenate([scaled, tail], axis=1), "z", axis=0, tiled=True)
    back = jnp.exp2(rows[:, width : width + 1].astype(jnp.float32) - TOP)
    pre = lax.dot_general(
        rows[:, :width].astype(jnp.bfloat16), fisher_slab, (((1,), (1,)), ((), ())),
        preferred_element_type=jnp.float32,
    )
    pre = (pre * back).astype(jnp.bfloat16)

    slots = lax.axis_size("z")
    pre = lax.all_gather(pre.reshape(slots, own.shape[0], -1), "xh", axis=1)
    pre = pre.reshape(-1, pre.shape[-1]).astype(jnp.float32)
    height, span = pre.shape
    exponent = exponent_of(jnp.max(jnp.abs(pre)))
    scaled = (pre * jnp.exp2(TOP - exponent)).astype(jnp.float16)
    tail = jnp.broadcast_to(exponent, (8, span)).astype(jnp.float16)
    blocks = lax.all_gather(jnp.concatenate([scaled, tail], axis=0), "z", axis=0)
    back = jnp.exp2(blocks[:, height : height + 1, :1].astype(jnp.float32) - TOP)
    whole = (blocks[:, :height].astype(jnp.float32) * back).astype(jnp.bfloat16)
    whole = jnp.swapaxes(whole, 0, 1).reshape(height, width)
    partial_value = lax.dot_general(
        whole, train_chip, (((1,), (1,)), ((), ())), preferred_element_type=jnp.float32
    )

    layers = lax.axis_size("layer")
    parts = lax.all_to_all(partial_value.reshape(layers, height // layers, -1), "layer", 0, 0)
    total = jnp.sum(parts, axis=0)
    group = own.shape[0]
    total = total.reshape(-1, group, 2, total.shape[-1] // 2)
    total = lax.all_to_all(total, "c", 2, 1)
    return total.reshape(-1, total.shape[-1])


def solution(mesh):
    layers, spread = mesh.devices.shape
    fine = Mesh(mesh.devices.reshape(layers, spread // 4, 2, 2), ("layer", "z", "xh", "c"))
    ex = ("z", "xh", "c")
    in_specs = (P("layer", ex, None), P("layer", None, ex), P("layer", ex, None))
    return jax.shard_map(
        on_device, mesh=fine, in_specs=in_specs, out_specs=P("layer", ex), check_vma=False
    )
```

time: 415 us -> 140 us (0.34)
  waiting for transfers between devices: 387 us -> 5.53 us
  blocking collectives: 0 us -> 106 us
    all_gather x2, waiting for transfers between devices: 306 us -> 4.13 us  [the longest x1 4.12 us: on_device(): fisher_slab = lax.all_gather(fisher[0].T, ('xh', 'c'), axis=0, tiled=True)]
    psum x1 -> x0, waiting for transfers between devices: 80.5 us -> none  [on_device(): summed = lax.psum(partial_value, 'layer')]
    all_gather x0 -> x3, blocking collectives: none -> 80.3 us  [the longest x1 38.1 us: on_device(): lax.all_gather(jnp.concatenate([scaled, tail], axis=0), 'z', axis=0)]
    all_to_all x0 -> x2, blocking collectives: none -> 26 us  [the longest x1 13.1 us: on_device(): lax.all_to_all(partial_value.reshape(layers, height // layers, -1), 'laye...]
  transfers between devices with their start and end apart: 3 -> 2, of which waited for: 3 -> 1; matrix products, arithmetic and copies ran while one was open for 0% -> 6% of each run, Pallas kernels for 0% -> 0%
where the time goes in v1:
time: 140 us
  blocking collectives  106 us (76%)
  between operations  14.2 us (10%)
  matrix products  7.68 us (5%)
  waiting for transfers between devices  5.53 us (4%)
  local copies, waits for them, and re-layouts  4.56 us (3%)
  other arithmetic  1.95 us (1%)
    all_gather x1, blocking collectives, on_device(): lax.all_gather(jnp.concatenate([scaled, tail], axis=0), 'z', axis=0)  38.1 us
    all_gather x1, blocking collectives, on_device(): lax.all_gather(jnp.concatenate([scaled, tail], axis=1), 'z', axis=0, tile...  36.9 us
    all_to_all x1, blocking collectives, on_device(): lax.all_to_all(partial_value.reshape(layers, height // layers, -1), 'laye...  13.1 us
    all_to_all x1, blocking collectives, on_device(): total = lax.all_to_all(total, 'c', 2, 1)  12.8 us
    all_gather x1, blocking collectives, on_device(): pre = lax.all_gather(pre.reshape(slots, own.shape[0], -1), 'xh', axis=1)  5.3 us
    dot_general x1, matrix products, on_device(): lax.dot_general(whole, train_chip, (((1,), (1,)), ((), ())), preferred_el...  5.25 us
    all_gather x1, waiting for transfers between devices, on_device(): fisher_slab = lax.all_gather(fisher[0].T, ('xh', 'c'), axis=0, tiled=True)  4.12 us
  transfers between devices with their start and end apart: 2, of which 1 were waited for; matrix products, arithmetic and copies ran while one was open for 6% of the time, Pallas kernels for 0%

profile of v1, /device:TPU:1, one launch (start us, length us, event | category | flops | bytes accessed | tf_op | source)
XLA Modules:
  0.0 140.3 jit_solution(16591718028564484924)
XLA Ops:
  6.5 0.0 copy-start
  6.5 0.0 all-gather.7.cloned.1.call-start
  6.5 0.7 all-gather.7.cloned.1.call-update
  7.3 0.0 all-gather.9.cloned.1.call-start
  7.3 0.7 all-gather.9.cloned.1.call-update
  8.0 0.0 copy-done
  8.0 0.1 fusion.7
  8.2 0.1 fusion.8
  8.3 0.1 broadcast_in_dim.2
  8.4 36.9 %all-gather.10 = f16[128,4224]{1,0:T(8,128)(2,1)S(1)} all-gather(f16[8,4224]{1,0:T(8,128)(2,1)S(1)} %pad_maximum_fusion), channel_id=1, replica_groups=mesh['layer'=8,'z'=16,'xh'=2,'c'=2] {'z'}, dimensions={0}, use_global_device_ids=true | all-gather | bytes 1148928 | tf_op jit(solution)/shard_map/all_gather | solution.py:22
  45.3 0.1 copy.28
  45.4 4.1 %all-gather.7.cloned.1.call-done = bf16[256,4096]{1,0:T(8,128)(2,1)} async-done(((bf16[64,4096]{1,0:T(8,128)(2,1)}), bf16[256,4096]{1,0:T(8,128)(2,1)}) %all-gather.7.cloned.1.call-update) | async-done | bytes 2097168 | tf_op jit(solution)/shard_map/all_gather | solution.py:15
  49.5 2.4 %fusion.4 = bf16[16,1,8,256]{3,2,1,0:T(8,128)(2,1)S(1)} fusion(bf16[256,4096]{1,0:T(8,128)(2,1)} %all-gather.7.cloned.1.call-done, f16[128,4224]{1,0:T(8,128)(2,1)S(1)} %all-gather.10, f32[128]{0:T(128)S(1)} %bitcast.33), kind=kOutput, calls=%fused_computation.6 | convolution fusion | flops 269025280 | bytes 3211776 | tf_op jit(solution)/shard_map/dot_general | solution.py:24
  51.9 5.3 %all_gather.20 = bf16[16,2,8,256]{3,2,1,0:T(8,128)(2,1)S(1)} all-gather(bf16[16,1,8,256]{3,2,1,0:T(8,128)(2,1)S(1)} %fusion.4), channel_id=1, replica_groups=mesh['layer'=8,'z'=16,'xh'=2,'c'=2] {'xh'}, dimensions={1}, use_global_device_ids=true | all-gather | bytes 196608 | tf_op jit(solution)/shard_map/all_gather | solution.py:31
  57.2 0.6 fusion.5
  58.7 38.1 %all-gather.11 = f16[4224,256]{1,0:T(8,128)(2,1)S(1)} all-gather(f16[264,256]{1,0:T(8,128)(2,1)S(1)} %concatenate.7), channel_id=2, replica_groups=mesh['layer'=8,'z'=16,'xh'=2,'c'=2] {'z'}, dimensions={0}, use_global_device_ids=true | all-gather | bytes 2297856 | tf_op jit(solution)/shard_map/all_gather | solution.py:37
  96.7 0.1 copy.27
  96.8 1.0 fusion.2
  97.8 1.2 copy.23
  99.0 2.4 %dot_general.9 = bf16[8,32,4096]{2,1,0:T(8,128)(2,1)} reshape(bf16[256,16,256]{2,1,0:T(8,128)(2,1)S(1)} %copy.23) | data formatting | bytes 4194304 | tf_op jit(solution)/shard_map/dot_general | solution.py:41
  101.4 0.0 all-gather.9.cloned.1.call-done
  101.4 5.3 %fusion = f32[8,32,768]{2,1,0:T(8,128)S(1)} fusion(bf16[8,32,4096]{2,1,0:T(8,128)(2,1)} %dot_general.9, bf16[1,768,4096]{2,1,0:T(8,128)(2,1)} %all-gather.9.cloned.1.call-done), kind=kOutput, calls=%fused_computation | convolution fusion | flops 1610612736 | bytes 9175040 | tf_op jit(solution)/shard_map/dot_general | solution.py:41
  106.7 13.1 %all_to_all.20 = f32[8,32,768]{2,1,0:T(8,128)S(1)} all-to-all(f32[8,32,768]{2,1,0:T(8,128)S(1)} %fusion), channel_id=1, replica_groups=mesh['layer'=8,'z'=16,'xh'=2,'c'=2] {'layer'}, dimensions={0} | all-to-all | bytes 1572864 | tf_op jit(solution)/shard_map/all_to_all | solution.py:46
  119.9 0.1 broadcast_in_dim_reshape.3
  119.9 12.8 %all_to_all.21 = f32[4,1,8,2,384]{4,2,0,1,3:T(8,128)S(1)} all-to-all(f32[4,1,8,2,384]{4,2,0,1,3:T(8,128)S(1)} %copy.24), channel_id=1, replica_groups=mesh['layer'=8,'z'=16,'xh'=2,'c'=2] {'c'}, dimensions={3} | all-to-all | bytes 196608 | tf_op jit(solution)/shard_map/all_to_all | solution.py:50
  132.8 0.6 copy.25
  (9 shorter events, 0.2 us)
Async XLA Ops:
  6.5 1.5 %copy-start = (bf16[1,8,4096]{2,1,0:T(8,128)(2,1)S(1)}, bf16[1,8,4096]{2,1,0:T(8,128)(2,1)}, u32[]{:S(2)}) copy-start(bf16[1,8,4096]{2,1,0:T(8,128)(2,1)} %param.3) | copy-start | bytes 196612
  6.5 43.0 %all-gather.7.cloned.1.call-start = ((), (), s32[]{:S(2)}) async-start(), calls=%async_computation.2 | async-start | bytes 2621440 | tf_op jit(solution)/shard_map/all_gather | solution.py:15
  7.3 94.1 %all-gather.9.cloned.1.call-start = ((), (), s32[]{:S(2)}) async-start(), calls=%async_computation.3 | async-start | bytes 9437184 | tf_op jit(solution)/shard_map/all_gather | solution.py:16
Sparse Core Ops, SparseCore 0:
  9.5 39.9 all-gather.6
  51.6 27.7 all-gather.8

commit v2 on v1

--- a/solution.py
+++ b/solution.py
@@ -4,6 +4,7 @@
 from jax.sharding import Mesh, PartitionSpec as P
 
 TOP = 14.0
+SWAP = [(0, 1), (1, 0)]
 
 
 def exponent_of(peak):
@@ -12,8 +13,16 @@
 
 def on_device(queries, fisher, train_grads):
     width = queries.shape[2]
-    fisher_slab = lax.all_gather(fisher[0].T, ("xh", "c"), axis=0, tiled=True)
-    train_chip = lax.all_gather(train_grads[0], "c", axis=0, tiled=True)
+    mine = fisher[0].T
+    fisher_slab = jnp.concatenate(
+        [
+            mine,
+            lax.ppermute(mine, "c", SWAP),
+            lax.ppermute(mine, "xh", SWAP),
+            lax.ppermute(mine, ("xh", "c"), [(0, 3), (3, 0), (1, 2), (2, 1)]),
+        ]
+    )
+    train_other = lax.ppermute(train_grads[0], "c", SWAP)
 
     own = queries[0].astype(jnp.float32)
     exponent = exponent_of(jnp.max(jnp.abs(own), axis=1, keepdims=True))
@@ -26,9 +35,15 @@
         preferred_element_type=jnp.float32,
     )
     pre = (pre * back).astype(jnp.bfloat16)
+    first_chip, first_core = lax.axis_index("xh") == 0, lax.axis_index("c") == 0
+    pre = pre.reshape(-1, 2, 2, pre.shape[-1] // 4)
+    pre = jnp.where(first_core, pre, pre[:, :, ::-1])
+    pre = jnp.where(first_chip, pre, pre[:, ::-1]).reshape(pre.shape[0], -1)
 
     slots = lax.axis_size("z")
-    pre = lax.all_gather(pre.reshape(slots, own.shape[0], -1), "xh", axis=1)
+    pre = pre.reshape(slots, 1, own.shape[0], -1)
+    got = lax.ppermute(pre, "xh", SWAP)
+    pre = jnp.where(first_chip, jnp.concatenate([pre, got], axis=1), jnp.concatenate([got, pre], axis=1))
     pre = pre.reshape(-1, pre.shape[-1]).astype(jnp.float32)
     height, span = pre.shape
     exponent = exponent_of(jnp.max(jnp.abs(pre)))
@@ -38,17 +53,16 @@
     back = jnp.exp2(blocks[:, height : height + 1, :1].astype(jnp.float32) - TOP)
     whole = (blocks[:, :height].astype(jnp.float32) * back).astype(jnp.bfloat16)
     whole = jnp.swapaxes(whole, 0, 1).reshape(height, width)
-    partial_value = lax.dot_general(
-        whole, train_chip, (((1,), (1,)), ((), ())), preferred_element_type=jnp.float32
-    )
+    by_own = lax.dot_general(whole, train_grads[0], (((1,), (1,)), ((), ())), preferred_element_type=jnp.float32)
+    by_other = lax.dot_general(whole, train_other, (((1,), (1,)), ((), ())), preferred_element_type=jnp.float32)
 
-    layers = lax.axis_size("layer")
-    parts = lax.all_to_all(partial_value.reshape(layers, height // layers, -1), "layer", 0, 0)
-    total = jnp.sum(parts, axis=0)
-    group = own.shape[0]
-    total = total.reshape(-1, group, 2, total.shape[-1] // 2)
-    total = lax.all_to_all(total, "c", 2, 1)
-    return total.reshape(-1, total.shape[-1])
+    layers, group = lax.axis_size("layer"), own.shape[0]
+    parts = jnp.concatenate([by_own, by_other], axis=1).reshape(layers, height // layers, -1)
+    total = jnp.sum(lax.all_to_all(parts, "layer", 0, 0), axis=0)
+    keep, give = jnp.split(total.reshape(-1, 1, group, total.shape[-1]), 2, axis=-1)
+    got = lax.ppermute(give, "c", SWAP)
+    both = jnp.where(first_core, jnp.concatenate([keep, got], axis=1), jnp.concatenate([got, keep], axis=1))
+    return both.reshape(-1, both.shape[-1])
 
 
 def solution(mesh):

time: 140 us -> 139 us (level)
  starting transfers between devices: 0.04 us -> 37.8 us
  blocking collectives: 106 us -> 78.9 us
  between operations: 14.2 us -> 0.95 us
  other arithmetic: 1.95 us -> 5.76 us
  waiting for transfers between devices: 5.53 us -> 3.34 us
    ppermute x0 -> x6, starting transfers between devices: none -> 37.8 us  [the longest x1 15.9 us: on_device(): got = lax.ppermute(give, 'c', SWAP)]
    all_to_all x2 -> x1, blocking collectives: 26 us -> 12.7 us  [on_device(): total = jnp.sum(lax.all_to_all(parts, 'layer', 0, 0), axis=0)]
    all_gather x1, blocking collectives: 36.9 us -> 30.4 us  [on_device(): lax.all_gather(jnp.concatenate([scaled, tail], axis=1), 'z', axis=0, tile...]
    all_gather x1 -> x0, blocking collectives: 5.3 us -> none  [on_device(): pre = lax.all_gather(pre.reshape(slots, own.shape[0], -1), 'xh', axis=1)]
    all_gather x2 -> x0, waiting for transfers between devices: 4.13 us -> none  [the longest x1 4.12 us: on_device(): fisher_slab = lax.all_gather(fisher[0].T, ('xh', 'c'), axis=0, tiled=True)]
    ppermute x0 -> x6, waiting for transfers between devices: none -> 3.34 us  [the longest x1 2.46 us: on_device(): got = lax.ppermute(pre, 'xh', SWAP)]
    dot_general x1 -> x0, local copies, waits for them, and re-layouts: 2.39 us -> none  [on_device(): lax.dot_general(whole, train_chip, (((1,), (1,)), ((), ())), preferred_el...]
    all_gather x1, blocking collectives: 38.1 us -> 35.8 us  [on_device(): lax.all_gather(jnp.concatenate([scaled, tail], axis=0), 'z', axis=0)]
  transfers between devices with their start and end apart: 2 -> 6, of which waited for: 1 -> 2; matrix products, arithmetic and copies ran while one was open for 6% -> 10% of each run, Pallas kernels for 0% -> 0%
where the time goes in v2:
time: 139 us
  blocking collectives  78.9 us (57%)
  starting transfers between devices  37.8 us (27%)
  matrix products  8.27 us (6%)
  other arithmetic  5.76 us (4%)
  local copies, waits for them, and re-layouts  3.54 us (3%)
  waiting for transfers between devices  3.34 us (2%)
    all_gather x1, blocking collectives, on_device(): lax.all_gather(jnp.concatenate([scaled, tail], axis=0), 'z', axis=0)  35.8 us
    all_gather x1, blocking collectives, on_device(): lax.all_gather(jnp.concatenate([scaled, tail], axis=1), 'z', axis=0, tile...  30.4 us
    ppermute x1, starting transfers between devices, on_device(): got = lax.ppermute(give, 'c', SWAP)  15.9 us
    all_to_all x1, blocking collectives, on_device(): total = jnp.sum(lax.all_to_all(parts, 'layer', 0, 0), axis=0)  12.7 us
    ppermute x1, starting transfers between devices, on_device(): lax.ppermute(mine, 'c', SWAP)  8.78 us
    ppermute x1, starting transfers between devices, on_device(): lax.ppermute(mine, ('xh', 'c'), [(0, 3), (3, 0), (1, 2), (2, 1)])  5.05 us
    ppermute x1, starting transfers between devices, on_device(): got = lax.ppermute(pre, 'xh', SWAP)  4.04 us
    dot_general x1, matrix products, on_device(): lax.dot_general(whole, train_grads[0], (((1,), (1,)), ((), ())), preferre...  3.18 us
  transfers between devices with their start and end apart: 6, of which 2 were waited for; matrix products, arithmetic and copies ran while one was open for 10% of the time, Pallas kernels for 0%

profile of v2, /device:TPU:1, one launch (start us, length us, event | category | flops | bytes accessed | tf_op | source)
XLA Modules:
  0.0 138.5 jit_solution(16410027224827943311)
XLA Ops:
  0.0 8.8 %collective-permute-start = (bf16[64,4096]{1,0:T(8,128)(2,1)}, bf16[64,4096]{1,0:T(8,128)(2,1)S(1)}, u32[]{:S(2)}, u32[]{:S(2)}) collective-permute-start(bf16[64,4096]{1,0:T(8,128)(2,1)} %bitcast.35), channel_id=1, source_target_pairs={{0,1},{1,0},{2,3},{3,2},{4,5},{5,4},{6,7},{7,6},{8,9},{9,8},{10,11... | collective-permute-start | bytes 1572872 | tf_op jit(solution)/shard_map/ppermute | solution.py:20
  8.8 1.9 %collective-permute-start.1 = (bf16[64,4096]{1,0:T(8,128)(2,1)}, bf16[64,4096]{1,0:T(8,128)(2,1)S(1)}, u32[]{:S(2)}, u32[]{:S(2)}) collective-permute-start(bf16[64,4096]{1,0:T(8,128)(2,1)} %bitcast.36), channel_id=1, source_target_pairs={{0,2},{2,0},{1,3},{3,1},{4,6},{6,4},{5,7},{7,5},{8,10},{10,8},{9,1... | collective-permute-start | bytes 1572872 | tf_op jit(solution)/shard_map/ppermute | solution.py:21
  10.7 5.0 %collective-permute-start.2 = (bf16[64,4096]{1,0:T(8,128)(2,1)}, bf16[64,4096]{1,0:T(8,128)(2,1)S(1)}, u32[]{:S(2)}, u32[]{:S(2)}) collective-permute-start(bf16[64,4096]{1,0:T(8,128)(2,1)} %bitcast.37), channel_id=1, source_target_pairs={{0,3},{3,0},{1,2},{2,1},{4,7},{7,4},{5,6},{6,5},{8,11},{11,8},{9,1... | collective-permute-start | bytes 1572872 | tf_op jit(solution)/shard_map/ppermute | solution.py:22
  15.8 2.1 %collective-permute-start.4 = (bf16[384,4096]{1,0:T(8,128)(2,1)}, bf16[384,4096]{1,0:T(8,128)(2,1)}, u32[]{:S(2)}, u32[]{:S(2)}) collective-permute-start(bf16[384,4096]{1,0:T(8,128)(2,1)} %bitcast.34), channel_id=1, source_target_pairs={{0,1},{1,0},{2,3},{3,2},{4,5},{5,4},{6,7},{7,6},{8,9},{9,8},{10,11... | collective-permute-start | bytes 9437192 | tf_op jit(solution)/shard_map/ppermute | solution.py:25
  17.9 1.0 fusion.17
  18.9 0.9 fusion.18
  19.8 0.1 broadcast_in_dim.2
  19.9 30.4 %all-gather.3 = f16[128,4224]{1,0:T(8,128)(2,1)S(1)} all-gather(f16[8,4224]{1,0:T(8,128)(2,1)S(1)} %pad_maximum_fusion.1), channel_id=1, replica_groups=mesh['layer'=8,'z'=16,'xh'=2,'c'=2] {'z'}, dimensions={0}, use_global_device_ids=true | all-gather | bytes 1148928 | tf_op jit(solution)/shard_map/all_gather | solution.py:31
  50.4 0.1 copy.26
  50.4 0.0 collective-permute-done
  50.4 0.0 collective-permute-done.1
  50.4 0.0 collective-permute-done.2
  50.5 1.9 %fusion.12 = bf16[128,256]{1,0:T(8,128)(2,1)S(1)} fusion(bf16[64,4096]{1,0:T(8,128)(2,1)S(1)} %collective-permute-done.2, bf16[64,4096]{1,0:T(8,128)(2,1)S(1)} %collective-permute-done.1, bf16[64,4096]{1,0:T(8,128)(2,1)S(1)} %collective-permute-done, bf16[64,4096]{1,0:T(8,128)(2,1)} %bitcast.38, f16[128,4224]{1,0:T(8,128)(2,1)S(1)} %all-gather.3, ...), kind=kOutput, calls=%fused_computation.11 | convolution fusion | flops 277413888 | bytes 3211776 | tf_op jit(solution)/shard_map/dot_general | solution.py:33
  52.4 0.1 copy.19
  52.5 0.1 copy.20
  52.7 0.1 reshape_reshape.3
  52.8 4.0 %collective-permute-start.3 = (bf16[16,1,8,256]{3,2,0,1:T(8,128)(2,1)S(1)}, bf16[16,1,8,256]{3,2,0,1:T(8,128)(2,1)S(1)}, u32[]{:S(2)}, u32[]{:S(2)}) collective-permute-start(bf16[16,1,8,256]{3,2,0,1:T(8,128)(2,1)S(1)} %reshape_reshape.3), channel_id=1, source_target_pairs={{0,2},{2,0},{1,3},{3,1},{4,6},{6,4},{5,7},{7,5},{8,10},{10,8},{9,1... | collective-permute-start | bytes 196616 | tf_op jit(solution)/shard_map/ppermute | solution.py:45
  56.9 2.5 %collective-permute-done.3 = bf16[16,1,8,256]{3,2,0,1:T(8,128)(2,1)S(1)} collective-permute-done((bf16[16,1,8,256]{3,2,0,1:T(8,128)(2,1)S(1)}, bf16[16,1,8,256]{3,2,0,1:T(8,128)(2,1)S(1)}, u32[]{:S(2)}, u32[]{:S(2)}) %collective-permute-start.3) | collective-permute-done | bytes 65568 | tf_op jit(solution)/shard_map/ppermute | solution.py:45
  59.3 0.6 fusion.15
  60.8 35.8 %all-gather.4 = f16[4224,256]{1,0:T(8,128)(2,1)S(1)} all-gather(f16[264,256]{1,0:T(8,128)(2,1)S(1)} %concatenate.28), channel_id=2, replica_groups=mesh['layer'=8,'z'=16,'xh'=2,'c'=2] {'z'}, dimensions={0}, use_global_device_ids=true | all-gather | bytes 2297856 | tf_op jit(solution)/shard_map/all_gather | solution.py:52
  96.6 0.1 copy.25
  96.7 2.3 %fusion = bf16[256,16,256]{2,0,1:T(8,128)(2,1)} fusion(f16[16,264,256]{2,1,0:T(8,128)(2,1)S(1)} %bitcast.26, f32[16]{0:T(128)S(1)} %exponential_bitcast_fusion), kind=kLoop, calls=%fused_computation.1 | loop fusion | flops 3145728 | bytes 4194368 | tf_op jit(solution)/shard_map/transpose | solution.py:55
  99.1 2.8 %copy.23 = bf16[256,16,256]{0,2,1:T(8,128)(2,1)S(1)} copy(bf16[256,16,256]{2,0,1:T(8,128)(2,1)} %fusion) | data formatting | bytes 4194304 | tf_op jit(solution)/shard_map/transpose | solution.py:55
  101.9 3.2 %fusion.20 = f32[256,384]{1,0:T(8,128)S(1)} fusion(bf16[256,4096]{0,1:T(8,128)(2,1)S(1)} %bitcast.28, bf16[1,384,4096]{2,1,0:T(8,128)(2,1)} %param.5), kind=kOutput, calls=%fused_computation.32 | convolution fusion | flops 805306368 | bytes 5636096 | tf_op jit(solution)/shard_map/dot_general | solution.py:56
  105.1 0.0 collective-permute-done.4
  105.1 3.2 %fusion.24 = f32[256,384]{1,0:T(8,128)S(1)} fusion(bf16[256,4096]{0,1:T(8,128)(2,1)S(1)} %bitcast.29, bf16[384,4096]{1,0:T(8,128)(2,1)} %collective-permute-done.4), kind=kOutput, calls=%fused_computation.36 | convolution fusion | flops 805306368 | bytes 5636096 | tf_op jit(solution)/shard_map/dot_general | solution.py:57
  108.3 0.1 pad_maximum_fusion
  108.4 12.7 %all_to_all.5 = f32[8,32,768]{2,1,0:T(8,128)S(1)} all-to-all(f32[8,32,768]{2,1,0:T(8,128)S(1)} %bitcast.27), channel_id=1, replica_groups=mesh['layer'=8,'z'=16,'xh'=2,'c'=2] {'layer'}, dimensions={0} | all-to-all | bytes 1572864 | tf_op jit(solution)/shard_map/all_to_all | solution.py:61
  121.1 15.9 %collective-permute-start.5 = (f32[4,1,8,384]{3,2,1,0:T(8,128)S(1)}, f32[4,1,8,384]{3,2,1,0:T(8,128)S(1)}, u32[]{:S(2)}, u32[]{:S(2)}) collective-permute-start(f32[4,1,8,384]{3,2,1,0:T(8,128)S(1)} %get-tuple-element.6), channel_id=1, source_target_pairs={{0,1},{1,0},{2,3},{3,2},{4,5},{5,4},{6,7},{7,6},{8,9},{9,8},{10,11... | collective-permute-start | bytes 147464 | tf_op jit(solution)/shard_map/ppermute | solution.py:63
  137.0 0.9 collective-permute-done.5
  137.9 0.6 maximum_select_fusion.1
  (12 shorter events, 0.3 us)
Async XLA Ops:
  0.0 50.4 %collective-permute-start = (bf16[64,4096]{1,0:T(8,128)(2,1)}, bf16[64,4096]{1,0:T(8,128)(2,1)S(1)}, u32[]{:S(2)}, u32[]{:S(2)}) collective-permute-start(bf16[64,4096]{1,0:T(8,128)(2,1)} %bitcast.35), channel_id=1, source_target_pairs={{0,1},{1,0},{2,3},{3,2},{4,5},{5,4},{6,7},{7,6},{8,9},{9,8},{10,11... | collective-permute-start | bytes 1572872 | tf_op jit(solution)/shard_map/ppermute | solution.py:20
  8.8 41.7 %collective-permute-start.1 = (bf16[64,4096]{1,0:T(8,128)(2,1)}, bf16[64,4096]{1,0:T(8,128)(2,1)S(1)}, u32[]{:S(2)}, u32[]{:S(2)}) collective-permute-start(bf16[64,4096]{1,0:T(8,128)(2,1)} %bitcast.36), channel_id=1, source_target_pairs={{0,2},{2,0},{1,3},{3,1},{4,6},{6,4},{5,7},{7,5},{8,10},{10,8},{9,1... | collective-permute-start | bytes 1572872 | tf_op jit(solution)/shard_map/ppermute | solution.py:21
  10.7 39.7 %collective-permute-start.2 = (bf16[64,4096]{1,0:T(8,128)(2,1)}, bf16[64,4096]{1,0:T(8,128)(2,1)S(1)}, u32[]{:S(2)}, u32[]{:S(2)}) collective-permute-start(bf16[64,4096]{1,0:T(8,128)(2,1)} %bitcast.37), channel_id=1, source_target_pairs={{0,3},{3,0},{1,2},{2,1},{4,7},{7,4},{5,6},{6,5},{8,11},{11,8},{9,1... | collective-permute-start | bytes 1572872 | tf_op jit(solution)/shard_map/ppermute | solution.py:22
  15.8 89.4 %collective-permute-start.4 = (bf16[384,4096]{1,0:T(8,128)(2,1)}, bf16[384,4096]{1,0:T(8,128)(2,1)}, u32[]{:S(2)}, u32[]{:S(2)}) collective-permute-start(bf16[384,4096]{1,0:T(8,128)(2,1)} %bitcast.34), channel_id=1, source_target_pairs={{0,1},{1,0},{2,3},{3,2},{4,5},{5,4},{6,7},{7,6},{8,9},{9,8},{10,11... | collective-permute-start | bytes 9437192 | tf_op jit(solution)/shard_map/ppermute | solution.py:25
  52.8 6.5 %collective-permute-start.3 = (bf16[16,1,8,256]{3,2,0,1:T(8,128)(2,1)S(1)}, bf16[16,1,8,256]{3,2,0,1:T(8,128)(2,1)S(1)}, u32[]{:S(2)}, u32[]{:S(2)}) collective-permute-start(bf16[16,1,8,256]{3,2,0,1:T(8,128)(2,1)S(1)} %reshape_reshape.3), channel_id=1, source_target_pairs={{0,2},{2,0},{1,3},{3,1},{4,6},{6,4},{5,7},{7,5},{8,10},{10,8},{9,1... | collective-permute-start | bytes 196616 | tf_op jit(solution)/shard_map/ppermute | solution.py:45
  121.1 16.7 %collective-permute-start.5 = (f32[4,1,8,384]{3,2,1,0:T(8,128)S(1)}, f32[4,1,8,384]{3,2,1,0:T(8,128)S(1)}, u32[]{:S(2)}, u32[]{:S(2)}) collective-permute-start(f32[4,1,8,384]{3,2,1,0:T(8,128)S(1)} %get-tuple-element.6), channel_id=1, source_target_pairs={{0,1},{1,0},{2,3},{3,2},{4,5},{5,4},{6,7},{7,6},{8,9},{9,8},{10,11... | collective-permute-start | bytes 147464 | tf_op jit(solution)/shard_map/ppermute | solution.py:63

commit v3 on v0

v3 whole, which is shorter than its diff:
```python
import functools

import jax
import jax.numpy as jnp
from jax import lax
from jax.experimental import pallas as pl
from jax.experimental.pallas import tpu as pltpu
from jax.sharding import Mesh, PartitionSpec as P

TOP = 14.0
AXES = ("layer", "z", "xh", "c")
SWAP = [(0, 1), (1, 0)]
CYCLE = [(1, 0), (0, 2), (2, 3), (3, 1)]
CROSS = [(1, 2), (2, 1)]
NT = (((1,), (1,)), ((), ()))


def exponent_of(peak):
    return jnp.clip(jnp.floor(jnp.log2(jnp.maximum(peak, 1e-37))), -100.0, 100.0)


def gather_z(x, groups):
    return lax.all_gather(x, AXES, axis=0, axis_index_groups=groups)


def add_blocks(total, blocks, train, side):
    for z in range(0, blocks.shape[0], 2):
        first = pl.multiple_of((2 * z + side) * 128, 128)
        second = pl.multiple_of((2 * z + 3 - side) * 128, 128)
        left = jnp.concatenate([blocks[z], blocks[z + 1]], axis=1)
        right = jnp.concatenate([train[:, pl.ds(first, 128)], train[:, pl.ds(second, 128)]], axis=1)
        total = total + lax.dot_general(left, right, NT, preferred_element_type=jnp.float32)
    return total


def side_of():
    return lax.rem(lax.axis_index("c") + lax.axis_index("z"), 2)


def first_kernel(own, train, out):
    out[...] = add_blocks(jnp.zeros(out.shape, jnp.float32), own, train, side_of())


def second_kernel(begun, own, other, train, train_got, out):
    side, chip = side_of(), lax.axis_index("xh")
    layers, _, rows, _ = out.shape
    here = add_blocks(begun[...], other, train, 1 - side)
    for layer in range(layers):
        out[layer, chip] = here[layer * rows : (layer + 1) * rows]
    there = add_blocks(jnp.zeros(begun.shape, jnp.float32), own, train_got, side)
    there = add_blocks(there, other, train_got, 1 - side)
    for layer in range(layers):
        out[layer, 1 - chip] = there[layer * rows : (layer + 1) * rows]


def in_vmem(kernel, out_shape, *operands):
    flops = 2 * sum(x.size for x in operands[:1]) * operands[-1].shape[0]
    spec = pl.BlockSpec(memory_space=pltpu.VMEM)
    return pl.pallas_call(
        kernel,
        out_shape=out_shape,
        in_specs=[spec] * len(operands),
        out_specs=spec,
        compiler_params=pltpu.CompilerParams(vmem_limit_bytes=40 * 2**20),
        cost_estimate=pl.CostEstimate(flops=flops, bytes_accessed=2**20, transcendentals=0),
    )(*operands)


def on_device(groups, queries, fisher, train_grads):
    width, group = queries.shape[2], queries.shape[1]
    layers, slots = lax.axis_size("layer"), lax.axis_size("z")
    chip, core, side = lax.axis_index("xh"), lax.axis_index("c"), side_of()
    train = train_grads[0]

    mine = fisher[0].T
    cycled = lax.ppermute(mine, ("xh", "c"), CYCLE)
    crossed = lax.ppermute(mine, ("xh", "c"), CROSS)
    train_got = lax.ppermute(train, "xh", SWAP)

    wide = queries[0].astype(jnp.float32)
    exponent = exponent_of(jnp.max(jnp.abs(wide), axis=1, keepdims=True))
    scaled = (wide * jnp.exp2(TOP - exponent)).astype(jnp.float16)
    tail = jnp.broadcast_to(exponent, (group, 128)).astype(jnp.float16)
    rows = gather_z(jnp.concatenate([scaled, tail], axis=1), groups).reshape(slots * group, width + 128)
    rows_got = lax.ppermute(rows, "c", SWAP)

    kept = jnp.where(chip == core, mine, crossed)
    low = jnp.where(chip == 0, kept, cycled)
    high = jnp.where(chip == 0, cycled, kept)
    columns = jnp.concatenate([low, high], axis=0)

    def product(part):
        back = jnp.exp2(part[:, width : width + 1].astype(jnp.float32) - TOP)
        value = lax.dot_general(part[:, :width].astype(jnp.bfloat16), columns, NT, preferred_element_type=jnp.float32)
        return (value * back).astype(jnp.bfloat16).reshape(slots, 1, group, columns.shape[0])

    near, far = product(rows), product(rows_got)
    flip = (lax.broadcasted_iota(jnp.int32, (slots, 1, 1, 1), 0) + side) % 2 == 0
    pre = jnp.concatenate([jnp.where(flip, near, far), jnp.where(flip, far, near)], axis=1)
    height, span = slots * 2 * group, columns.shape[0]
    pre = pre.reshape(height, span).astype(jnp.float32)

    exponent = exponent_of(jnp.max(jnp.abs(pre)))
    scaled = (pre * jnp.exp2(TOP - exponent)).astype(jnp.float16)
    tail = jnp.broadcast_to(exponent, (8, span)).astype(jnp.float16)
    blocks = gather_z(jnp.concatenate([scaled, tail], axis=0), groups)
    back = jnp.exp2(blocks[:, height : height + 1, :1].astype(jnp.float32) - TOP)
    own = (blocks[:, :height].astype(jnp.float32) * back).astype(jnp.bfloat16)
    other = lax.ppermute(own, "c", SWAP)
    begun = in_vmem(first_kernel, jax.ShapeDtypeStruct((height, train.shape[0]), jnp.float32), own, train)
    parts_shape = jax.ShapeDtypeStruct((layers, 2, height // layers, train.shape[0]), jnp.float32)
    parts = in_vmem(second_kernel, parts_shape, begun, own, other, train, train_got)

    parts = lax.all_to_all(parts.reshape(2 * layers, height // layers, -1), ("layer", "xh"), 0, 0)
    total = jnp.sum(parts.reshape(layers, 2, -1, 2 * group, parts.shape[-1]), axis=0)
    return jnp.swapaxes(total, 0, 1).reshape(-1, parts.shape[-1])


def solution(mesh):
    layers, spread = mesh.devices.shape
    slots = spread // 4
    fine = Mesh(mesh.devices.reshape(layers, slots, 2, 2), AXES)
    groups = [
        [layer * spread + 4 * z + 2 * chip + (side + z) % 2 for z in range(slots)]
        for layer in range(layers)
        for chip in range(2)
        for side in range(2)
    ]
    ex = ("z", "xh", "c")
    in_specs = (P("layer", ex, None), P("layer", None, ex), P("layer", ex, None))
    return jax.shard_map(
        functools.partial(on_device, groups),
        mesh=fine,
        in_specs=in_specs,
        out_specs=P("layer", ex),
        check_vma=False,
    )
```

time: 415 us -> 152 us (0.37)
  waiting for transfers between devices: 387 us -> 27.4 us
  blocking collectives: 0 us -> 90.2 us
  starting transfers between devices: 0.08 us -> 16.9 us
  between operations: 13.1 us -> 0.91 us
  matrix products: 9.78 us -> 2.24 us
  other arithmetic: 0 us -> 5.98 us
  Pallas kernels: 0 us -> 4.51 us
    all_gather x2 -> x0, waiting for transfers between devices: 306 us -> none  [the longest x1 160 us: on_device(): lax.all_gather(queries, 'ex', axis=1, tiled=True)[0]]
    psum x1 -> x0, waiting for transfers between devices: 80.5 us -> none  [on_device(): summed = lax.psum(partial_value, 'layer')]
    all_gather x0 -> x2, blocking collectives: none -> 73.4 us  [gather_z(): return lax.all_gather(x, AXES, axis=0, axis_index_groups=groups)]
    ppermute x0 -> x5, waiting for transfers between devices: none -> 27.4 us  [the longest x1 25.6 us: on_device(): train_got = lax.ppermute(train, 'xh', SWAP)]
    ppermute x0 -> x5, starting transfers between devices: none -> 16.9 us  [the longest x1 8.78 us: on_device(): cycled = lax.ppermute(mine, ('xh', 'c'), CYCLE)]
    all_to_all x0 -> x1, blocking collectives: none -> 16.8 us  [on_device(): lax.all_to_all(parts.reshape(2 * layers, height // layers, -1), ('layer',...]
    dot_general x2, matrix products: 9.78 us -> 2.24 us  [product(): lax.dot_general(part[:, :width].astype(jnp.bfloat16), columns, NT, prefer...]
    pallas_call x0 -> x2, Pallas kernels: none -> 4.51 us  [in_vmem(): pl.pallas_call(kernel, out_shape=out_shape, in_specs=[spec] * len(operand...]
  transfers between devices with their start and end apart: 3 -> 5, of which waited for: 3 -> 2; matrix products, arithmetic and copies ran while one was open for 0% -> 7% of each run, Pallas kernels for 0% -> 1%
where the time goes in v3:
time: 152 us
  blocking collectives  90.2 us (59%)
  waiting for transfers between devices  27.4 us (18%)
  starting transfers between devices  16.9 us (11%)
  other arithmetic  5.98 us (4%)
  Pallas kernels  4.51 us (3%)
  local copies, waits for them, and re-layouts  3.4 us (2%)
  matrix products  2.24 us (1%)
    all_gather x2, blocking collectives, gather_z(): return lax.all_gather(x, AXES, axis=0, axis_index_groups=groups)  73.4 us
    ppermute x1, waiting for transfers between devices, on_device(): train_got = lax.ppermute(train, 'xh', SWAP)  25.6 us
    all_to_all x1, blocking collectives, on_device(): lax.all_to_all(parts.reshape(2 * layers, height // layers, -1), ('layer',...  16.8 us
    ppermute x1, starting transfers between devices, on_device(): cycled = lax.ppermute(mine, ('xh', 'c'), CYCLE)  8.78 us
    pallas_call x2, Pallas kernels, in_vmem(): pl.pallas_call(kernel, out_shape=out_shape, in_specs=[spec] * len(operand...  4.51 us
  transfers between devices with their start and end apart: 5, of which 2 were waited for; matrix products, arithmetic and copies ran while one was open for 7% of the time, Pallas kernels for 1%

profile of v3, /device:TPU:1, one launch (start us, length us, event | category | flops | bytes accessed | tf_op | source)
XLA Modules:
  0.0 151.6 jit_solution(5859036928296292287)
XLA Ops:
  0.0 8.8 %collective-permute-start.1 = (bf16[64,4096]{1,0:T(8,128)(2,1)}, bf16[64,4096]{1,0:T(8,128)(2,1)}, u32[]{:S(2)}, u32[]{:S(2)}) collective-permute-start(bf16[64,4096]{1,0:T(8,128)(2,1)} %bitcast.31), channel_id=1, source_target_pairs={{1,0},{0,2},{2,3},{3,1},{5,4},{4,6},{6,7},{7,5},{9,8},{8,10},{10,1... | collective-permute-start | bytes 1572872 | tf_op jit(solution)/shard_map/ppermute | solution.py:76
  8.8 1.9 %collective-permute-start = (bf16[64,4096]{1,0:T(8,128)(2,1)}, bf16[64,4096]{1,0:T(8,128)(2,1)}, u32[]{:S(2)}, u32[]{:S(2)}) collective-permute-start(bf16[64,4096]{1,0:T(8,128)(2,1)} %bitcast.32), channel_id=1, source_target_pairs={{1,2},{2,1},{5,6},{6,5},{9,10},{10,9},{13,14},{14,13},{17,18},{18,... | collective-permute-start | bytes 1572872 | tf_op jit(solution)/shard_map/ppermute | solution.py:77
  10.7 1.0 fusion.6
  11.7 0.9 fusion.7
  12.6 0.1 broadcast_in_dim.19
  12.7 0.0 copy-start
  12.7 39.6 %all-gather.4 = f16[128,4224]{1,0:T(8,128)(2,1)} all-gather(f16[8,4224]{1,0:T(8,128)(2,1)S(1)} %pad_maximum_fusion.3), channel_id=2, replica_groups={{0,5,8,13,16,21,24,29,32,37,40,45,48,53,56,61},{1,4,9,12,17,20,25,28,33..., dimensions={0}, use_global_device_ids=true | all-gather | bytes 1148928 | tf_op jit(solution)/shard_map/all_gather | solution.py:23
  52.3 2.6 %copy.12 = f16[128,4224]{0,1:T(8,128)(2,1)} copy(f16[128,4224]{1,0:T(8,128)(2,1)} %all-gather.4) | data formatting | bytes 2162688 | tf_op jit(solution)/shard_map/all_gather | solution.py:23
  54.9 2.3 %collective-permute-start.2 = (f16[128,4224]{0,1:T(8,128)(2,1)}, f16[128,4224]{0,1:T(8,128)(2,1)}, u32[]{:S(2)}, u32[]{:S(2)}) collective-permute-start(f16[128,4224]{0,1:T(8,128)(2,1)} %copy.12), channel_id=1, source_target_pairs={{0,1},{1,0},{2,3},{3,2},{4,5},{5,4},{6,7},{7,6},{8,9},{9,8},{10,11... | collective-permute-start | bytes 3244040 | tf_op jit(solution)/shard_map/ppermute | solution.py:85
  57.2 0.0 copy-done
  57.3 1.9 %collective-permute-start.4 = (bf16[384,4096]{1,0:T(8,128)(2,1)S(1)}, bf16[384,4096]{1,0:T(8,128)(2,1)}, u32[]{:S(2)}, u32[]{:S(2)}) collective-permute-start(bf16[384,4096]{1,0:T(8,128)(2,1)S(1)} %bitcast.24), channel_id=1, source_target_pairs={{0,2},{2,0},{1,3},{3,1},{4,6},{6,4},{5,7},{7,5},{8,10},{10,8},{9,1... | collective-permute-start | bytes 9437192 | tf_op jit(solution)/shard_map/ppermute | solution.py:78
  59.2 0.7 fusion.21
  59.9 0.0 collective-permute-done.1
  59.9 0.0 collective-permute-done
  59.9 1.5 broadcast_select_fusion.2
  61.4 0.0 collective-permute-done.2
  61.4 0.7 fusion.17
  62.1 0.0 copy-start.1
  62.1 1.8 %fusion.2 = bf16[16,1,8,128]{3,2,0,1:T(8,128)(2,1)S(1)} fusion(f16[128,4224]{0,1:T(8,128)(2,1)} %collective-permute-done.2, bf16[64,4096]{1,0:T(8,128)(2,1)S(1)} %get-tuple-element.6, bf16[64,4096]{1,0:T(8,128)(2,1)S(1)} %get-tuple-element.5, f32[128]{0:T(128)S(1)} %fusion.17), kind=kOutput, calls=%fused_computation.5 | convolution fusion | flops 136871936 | bytes 2130432 | tf_op jit(solution)/shard_map/dot_general | solution.py:94
  63.9 0.0 copy-done.1
  63.9 0.4 broadcast_select_fusion.4
  64.3 0.6 fusion.4
  65.8 33.9 %all-gather.5 = f16[4224,128]{1,0:T(8,128)(2,1)S(1)} all-gather(f16[264,128]{1,0:T(8,128)(2,1)S(1)} %concatenate.15), channel_id=3, replica_groups={{0,5,8,13,16,21,24,29,32,37,40,45,48,53,56,61},{1,4,9,12,17,20,25,28,33..., dimensions={0}, use_global_device_ids=true | all-gather | bytes 1148928 | tf_op jit(solution)/shard_map/all_gather | solution.py:23
  99.6 0.2 fusion.11
  99.9 0.3 multiply_convert_fusion.own
  100.2 2.0 %collective-permute-start.3 = (bf16[16,256,128]{2,1,0:T(8,128)(2,1)S(1)}, bf16[16,256,128]{2,1,0:T(8,128)(2,1)S(1)}, u32[]{:S(2)}, u32[]{:S(2)}) collective-permute-start(bf16[16,256,128]{2,1,0:T(8,128)(2,1)S(1)} %multiply_convert_fusion.own), channel_id=1, source_target_pairs={{0,1},{1,0},{2,3},{3,2},{4,5},{5,4},{6,7},{7,6},{8,9},{9,8},{10,11... | collective-permute-start | bytes 3145736 | tf_op jit(solution)/shard_map/ppermute | solution.py:109
  102.2 0.8 shard_map.37.begun
  102.9 1.8 %collective-permute-done.3.other = bf16[16,256,128]{2,1,0:T(8,128)(2,1)S(1)} collective-permute-done((bf16[16,256,128]{2,1,0:T(8,128)(2,1)S(1)}, bf16[16,256,128]{2,1,0:T(8,128)(2,1)S(1)}, u32[]{:S(2)}, u32[]{:S(2)}) %collective-permute-start.3) | collective-permute-done | bytes 1048608 | tf_op jit(solution)/shard_map/ppermute | solution.py:109
  104.7 25.6 %collective-permute-done.4.train_got = bf16[384,4096]{1,0:T(8,128)(2,1)} collective-permute-done((bf16[384,4096]{1,0:T(8,128)(2,1)S(1)}, bf16[384,4096]{1,0:T(8,128)(2,1)}, u32[]{:S(2)}, u32[]{:S(2)}) %collective-permute-start.4) | collective-permute-done | bytes 3145760 | tf_op jit(solution)/shard_map/ppermute | solution.py:78
  130.3 3.7 %shard_map.38 = f32[8,2,32,384]{3,2,1,0:T(8,128)S(1)} custom-call(f32[256,384]{1,0:T(8,128)S(1)} %shard_map.37.begun, bf16[16,256,128]{2,1,0:T(8,128)(2,1)S(1)} %multiply_convert_fusion.own, bf16[16,256,128]{2,1,0:T(8,128)(2,1)S(1)} %collective-permute-done.3.other, bf16[384,4096]{1,0:T(8,128)(2,1)S(1)} %bitcast.26, ...), custom_call_target="tpu_custom_call" | custom-call | flops 75497472 | bytes 1048576 | tf_op jit(solution)/shard_map/pallas_call | solution.py:59
  134.1 16.8 %all_to_all.5 = f32[16,32,384]{2,1,0:T(8,128)S(1)} all-to-all(f32[16,32,384]{2,1,0:T(8,128)S(1)} %bitcast.27), channel_id=1, replica_groups=mesh['layer'=8,'z'=16,'xh'=2,'c'=2] {'layer','xh'}, dimensions={0} | all-to-all | bytes 1572864 | tf_op jit(solution)/shard_map/all_to_all | solution.py:114
  150.9 0.6 copy.15
  (7 shorter events, 0.2 us)
Async XLA Ops:
  0.0 59.9 %collective-permute-start.1 = (bf16[64,4096]{1,0:T(8,128)(2,1)}, bf16[64,4096]{1,0:T(8,128)(2,1)}, u32[]{:S(2)}, u32[]{:S(2)}) collective-permute-start(bf16[64,4096]{1,0:T(8,128)(2,1)} %bitcast.31), channel_id=1, source_target_pairs={{1,0},{0,2},{2,3},{3,1},{5,4},{4,6},{6,7},{7,5},{9,8},{8,10},{10,1... | collective-permute-start | bytes 1572872 | tf_op jit(solution)/shard_map/ppermute | solution.py:76
  8.8 51.1 %collective-permute-start = (bf16[64,4096]{1,0:T(8,128)(2,1)}, bf16[64,4096]{1,0:T(8,128)(2,1)}, u32[]{:S(2)}, u32[]{:S(2)}) collective-permute-start(bf16[64,4096]{1,0:T(8,128)(2,1)} %bitcast.32), channel_id=1, source_target_pairs={{1,2},{2,1},{5,6},{6,5},{9,10},{10,9},{13,14},{14,13},{17,18},{18,... | collective-permute-start | bytes 1572872 | tf_op jit(solution)/shard_map/ppermute | solution.py:77
  12.7 44.5 %copy-start = (bf16[1,384,4096]{2,1,0:T(8,128)(2,1)S(1)}, bf16[1,384,4096]{2,1,0:T(8,128)(2,1)}, u32[]{:S(2)}) copy-start(bf16[1,384,4096]{2,1,0:T(8,128)(2,1)} %param.5) | copy-start | bytes 9437188
  54.9 6.4 %collective-permute-start.2 = (f16[128,4224]{0,1:T(8,128)(2,1)}, f16[128,4224]{0,1:T(8,128)(2,1)}, u32[]{:S(2)}, u32[]{:S(2)}) collective-permute-start(f16[128,4224]{0,1:T(8,128)(2,1)} %copy.12), channel_id=1, source_target_pairs={{0,1},{1,0},{2,3},{3,2},{4,5},{5,4},{6,7},{7,6},{8,9},{9,8},{10,11... | collective-permute-start | bytes 3244040 | tf_op jit(solution)/shard_map/ppermute | solution.py:85
  57.3 73.1 %collective-permute-start.4 = (bf16[384,4096]{1,0:T(8,128)(2,1)S(1)}, bf16[384,4096]{1,0:T(8,128)(2,1)}, u32[]{:S(2)}, u32[]{:S(2)}) collective-permute-start(bf16[384,4096]{1,0:T(8,128)(2,1)S(1)} %bitcast.24), channel_id=1, source_target_pairs={{0,2},{2,0},{1,3},{3,1},{4,6},{6,4},{5,7},{7,5},{8,10},{10,8},{9,1... | collective-permute-start | bytes 9437192 | tf_op jit(solution)/shard_map/ppermute | solution.py:78
  62.1 1.8 %copy-start.1 = (f16[128,4224]{1,0:T(8,128)(2,1)S(1)}, f16[128,4224]{1,0:T(8,128)(2,1)}, u32[]{:S(2)}) copy-start(f16[128,4224]{1,0:T(8,128)(2,1)} %all-gather.4) | copy-start | bytes 3244036
  100.2 4.6 %collective-permute-start.3 = (bf16[16,256,128]{2,1,0:T(8,128)(2,1)S(1)}, bf16[16,256,128]{2,1,0:T(8,128)(2,1)S(1)}, u32[]{:S(2)}, u32[]{:S(2)}) collective-permute-start(bf16[16,256,128]{2,1,0:T(8,128)(2,1)S(1)} %multiply_convert_fusion.own), channel_id=1, source_target_pairs={{0,1},{1,0},{2,3},{3,2},{4,5},{5,4},{6,7},{7,6},{8,9},{9,8},{10,11... | collective-permute-start | bytes 3145736 | tf_op jit(solution)/shard_map/ppermute | solution.py:109

commit v4 on v3

v4 whole, which is shorter than its diff:
```python
import functools

import jax
import jax.numpy as jnp
from jax import lax
from jax.experimental import pallas as pl
from jax.experimental.pallas import tpu as pltpu
from jax.sharding import Mesh, PartitionSpec as P

TOP = 14.0
AXES = ("layer", "z", "xh", "c")
SWAP = [(0, 1), (1, 0)]
CYCLE = [(1, 0), (0, 2), (2, 3), (3, 1)]
CROSS = [(1, 2), (2, 1)]
NT = (((1,), (1,)), ((), ()))


def exponent_of(peak):
    return jnp.clip(jnp.floor(jnp.log2(jnp.maximum(peak, 1e-37))), -100.0, 100.0)


def gather_z(x, groups):
    return lax.all_gather(x, AXES, axis=0, axis_index_groups=groups)


def add_blocks(total, blocks, train, side, begin=0):
    for z in range(0, train.shape[1] // 256, 2):
        first = pl.multiple_of((2 * z + side) * 128, 128)
        second = pl.multiple_of((2 * z + 3 - side) * 128, 128)
        left = jnp.concatenate([blocks[begin + z], blocks[begin + z + 1]], axis=1)
        right = jnp.concatenate([train[:, pl.ds(first, 128)], train[:, pl.ds(second, 128)]], axis=1)
        total = total + lax.dot_general(left, right, NT, preferred_element_type=jnp.float32)
    return total


def side_of():
    return lax.rem(lax.axis_index("c") + lax.axis_index("z"), 2)


def columns_of(mine, cycled, crossed):
    chip, core = lax.axis_index("xh"), lax.axis_index("c")
    kept = jnp.where(chip == core, mine[...], crossed[...])
    low = jnp.where(chip == 0, kept, cycled[...])
    high = jnp.where(chip == 0, cycled[...], kept)
    return jnp.concatenate([low, high], axis=0)


def rounded_product(rows, columns):
    value = lax.dot_general(rows[...], columns, NT, preferred_element_type=jnp.float32)
    return value.astype(jnp.bfloat16).astype(jnp.float32)


def near_kernel(rows, mine, cycled, crossed, out):
    out[...] = rounded_product(rows, columns_of(mine, cycled, crossed))


def chunk_kernel(near, rows, mine, cycled, crossed, out, order):
    side = side_of()
    far = rounded_product(rows, columns_of(mine, cycled, crossed))
    height = order.shape[0]
    group = out.shape[0] - height
    for z in range(height // (2 * group)):
        first = lax.rem(side + z, 2)
        piece = slice(z * group, (z + 1) * group)
        order[pl.ds(pl.multiple_of((2 * z + first) * group, group), group)] = near[piece]
        order[pl.ds(pl.multiple_of((2 * z + 1 - first) * group, group), group)] = far[piece]
    value = order[...]
    peak = jnp.max(jnp.max(jnp.abs(value), axis=0, keepdims=True), axis=1, keepdims=True)
    exponent = exponent_of(peak)
    tail = jnp.broadcast_to(exponent, (group, out.shape[1]))
    out[...] = jnp.concatenate([value * jnp.exp2(TOP - exponent), tail], axis=0)


def first_kernel(own, train, out):
    out[...] = add_blocks(jnp.zeros(out.shape, jnp.float32), own, train, side_of())


def second_kernel(begun, own, other, train, early, late, out):
    side, chip = side_of(), lax.axis_index("xh")
    layers, _, rows, _ = out.shape
    here = add_blocks(begun[...], other, train, 1 - side)
    for layer in range(layers):
        out[layer, chip] = here[layer * rows : (layer + 1) * rows]
    there = jnp.zeros(begun.shape, jnp.float32)
    for piece, begin in ((early, 0), (late, early.shape[1] // 256)):
        there = add_blocks(there, own, piece, side, begin)
        there = add_blocks(there, other, piece, 1 - side, begin)
    for layer in range(layers):
        out[layer, 1 - chip] = there[layer * rows : (layer + 1) * rows]


def in_vmem(kernel, out_shape, *operands, scratch=()):
    flops = 2 * operands[0].size * operands[1].shape[0]
    spec = pl.BlockSpec(memory_space=pltpu.VMEM)
    return pl.pallas_call(
        kernel,
        out_shape=out_shape,
        in_specs=[spec] * len(operands),
        out_specs=spec,
        scratch_shapes=scratch,
        compiler_params=pltpu.CompilerParams(vmem_limit_bytes=40 * 2**20),
        cost_estimate=pl.CostEstimate(flops=flops, bytes_accessed=2**20, transcendentals=0),
    )(*operands)


def on_device(groups, queries, fisher, train_grads):
    width, group = queries.shape[2], queries.shape[1]
    layers, slots = lax.axis_size("layer"), lax.axis_size("z")
    train = train_grads[0]
    cut = 256 * (slots * 3 // 16 * 2 or 2)

    mine = fisher[0].T
    cycled = lax.ppermute(mine, ("xh", "c"), CYCLE)
    crossed = lax.ppermute(mine, ("xh", "c"), CROSS)
    early = lax.ppermute(train[:, :cut], "xh", SWAP)
    late = lax.ppermute(train[:, cut:], "xh", SWAP)

    wide = queries[0].astype(jnp.float32)
    exponent = exponent_of(jnp.max(jnp.abs(wide), axis=1, keepdims=True))
    scaled = (wide * jnp.exp2(TOP - exponent)).astype(jnp.float16)
    tail = jnp.broadcast_to(exponent, (group, 128)).astype(jnp.float16)
    rows = gather_z(jnp.concatenate([scaled, tail], axis=1), groups).reshape(slots * group, width + 128)
    rows, cycled, crossed = lax.optimization_barrier((rows, cycled, crossed))
    blocks_of_fisher = (mine, cycled, crossed)
    back = jnp.exp2(rows[:, width : width + 1].astype(jnp.float32) - TOP)
    rows = (rows[:, :width].astype(jnp.float32) * back).astype(jnp.bfloat16)
    rows_got = lax.ppermute(rows, "c", SWAP)

    height, span = slots * 2 * group, 2 * mine.shape[0]
    near = in_vmem(near_kernel, jax.ShapeDtypeStruct((height // 2, span), jnp.float32), rows, *blocks_of_fisher)
    chunk = in_vmem(
        chunk_kernel,
        jax.ShapeDtypeStruct((height + group, span), jnp.float32),
        near,
        rows_got,
        *blocks_of_fisher,
        scratch=[pltpu.VMEM((height, span), jnp.float32)],
    )
    chunk, early = lax.optimization_barrier((chunk, early))
    blocks = gather_z(chunk.astype(jnp.float16), groups)
    back = jnp.exp2(blocks[:, height : height + 1, :1].astype(jnp.float32) - TOP)
    own = (blocks[:, :height].astype(jnp.float32) * back).astype(jnp.bfloat16)
    other = lax.ppermute(own, "c", SWAP)
    begun = in_vmem(first_kernel, jax.ShapeDtypeStruct((height, train.shape[0]), jnp.float32), own, train)
    parts_shape = jax.ShapeDtypeStruct((layers, 2, height // layers, train.shape[0]), jnp.float32)
    parts = in_vmem(second_kernel, parts_shape, begun, own, other, train, early, late)

    parts = lax.all_to_all(parts.reshape(2 * layers, height // layers, -1), ("layer", "xh"), 0, 0)
    total = jnp.sum(parts.reshape(layers, 2, -1, 2 * group, parts.shape[-1]), axis=0)
    return jnp.swapaxes(total, 0, 1).reshape(-1, parts.shape[-1])


def solution(mesh):
    layers, spread = mesh.devices.shape
    slots = spread // 4
    fine = Mesh(mesh.devices.reshape(layers, slots, 2, 2), AXES)
    groups = [
        [layer * spread + 4 * z + 2 * chip + (side + z) % 2 for z in range(slots)]
        for layer in range(layers)
        for chip in range(2)
        for side in range(2)
    ]
    ex = ("z", "xh", "c")
    in_specs = (P("layer", ex, None), P("layer", None, ex), P("layer", ex, None))
    return jax.shard_map(
        functools.partial(on_device, groups),
        mesh=fine,
        in_specs=in_specs,
        out_specs=P("layer", ex),
        check_vma=False,
    )
```

time: 152 us -> 126 us (0.83)
  waiting for transfers between devices: 27.4 us -> 5.32 us
  starting transfers between devices: 16.9 us -> 24.6 us
  other arithmetic: 5.98 us -> 1.24 us
  matrix products: 2.24 us -> 0 us
    ppermute x1 -> x2, waiting for transfers between devices: 25.6 us -> 5.31 us  [the longest x1 5.31 us: on_device(): late = lax.ppermute(train[:, cut:], 'xh', SWAP)]
    ppermute x1 -> x2, starting transfers between devices: 1.92 us -> 8.5 us  [the longest x1 4.88 us: on_device(): late = lax.ppermute(train[:, cut:], 'xh', SWAP)]
    ppermute x1, starting transfers between devices: 8.78 us -> 3.44 us  [on_device(): cycled = lax.ppermute(mine, ('xh', 'c'), CYCLE)]
    ppermute x1, starting transfers between devices: 1.92 us -> 6.16 us  [on_device(): crossed = lax.ppermute(mine, ('xh', 'c'), CROSS)]
    all_gather x2, blocking collectives: 73.4 us -> 69.5 us  [gather_z(): return lax.all_gather(x, AXES, axis=0, axis_index_groups=groups)]
    all_gather x1 -> x0, local copies, waits for them, and re-layouts: 2.63 us -> none  [gather_z(): return lax.all_gather(x, AXES, axis=0, axis_index_groups=groups)]
    all_to_all x1, blocking collectives: 16.8 us -> 19.3 us  [on_device(): lax.all_to_all(parts.reshape(2 * layers, height // layers, -1), ('layer',...]
    dot_general x2 -> x0, matrix products: 2.24 us -> none  [product(): lax.dot_general(part[:, :width].astype(jnp.bfloat16), columns, NT, prefer...]
  transfers between devices with their start and end apart: 5 -> 6, of which waited for: 2 -> 1; matrix products, arithmetic and copies ran while one was open for 7% -> 2% of each run, Pallas kernels for 1% -> 1%
where the time goes in v4:
time: 126 us
  blocking collectives  88.7 us (70%)
  starting transfers between devices  24.6 us (20%)
  waiting for transfers between devices  5.32 us (4%)
  Pallas kernels  3.66 us (3%)
  local copies, waits for them, and re-layouts  2.23 us (2%)
    all_gather x2, blocking collectives, gather_z(): return lax.all_gather(x, AXES, axis=0, axis_index_groups=groups)  69.5 us
    all_to_all x1, blocking collectives, on_device(): lax.all_to_all(parts.reshape(2 * layers, height // layers, -1), ('layer',...  19.3 us
    ppermute x1, starting transfers between devices, on_device(): crossed = lax.ppermute(mine, ('xh', 'c'), CROSS)  6.16 us
    ppermute x1, waiting for transfers between devices, on_device(): late = lax.ppermute(train[:, cut:], 'xh', SWAP)  5.31 us
    ppermute x1, starting transfers between devices, on_device(): late = lax.ppermute(train[:, cut:], 'xh', SWAP)  4.88 us
    ppermute x1, starting transfers between devices, on_device(): rows_got = lax.ppermute(rows, 'c', SWAP)  4.5 us
    pallas_call x4, Pallas kernels, in_vmem(): pl.pallas_call(kernel, out_shape=out_shape, in_specs=[spec] * len(operand...  3.66 us
    ppermute x1, starting transfers between devices, on_device(): early = lax.ppermute(train[:, :cut], 'xh', SWAP)  3.61 us
  transfers between devices with their start and end apart: 6, of which 1 were waited for; matrix products, arithmetic and copies ran while one was open for 2% of the time, Pallas kernels for 1%

profile of v4, /device:TPU:1, one launch (start us, length us, event | category | flops | bytes accessed | tf_op | source)
XLA Modules:
  0.0 126.0 jit_solution(1092780102699062000)
XLA Ops:
  0.0 0.0 copy-start.2
  0.0 6.2 %collective-permute-start.1 = (bf16[64,4096]{1,0:T(8,128)(2,1)}, bf16[64,4096]{1,0:T(8,128)(2,1)S(1)}, u32[]{:S(2)}, u32[]{:S(2)}) collective-permute-start(bf16[64,4096]{1,0:T(8,128)(2,1)} %bitcast.18), channel_id=1, source_target_pairs={{1,2},{2,1},{5,6},{6,5},{9,10},{10,9},{13,14},{14,13},{17,18},{18,... | collective-permute-start | bytes 1572872 | tf_op jit(solution)/shard_map/ppermute | solution.py:114
  6.2 3.4 %collective-permute-start = (bf16[64,4096]{1,0:T(8,128)(2,1)}, bf16[64,4096]{1,0:T(8,128)(2,1)S(1)}, u32[]{:S(2)}, u32[]{:S(2)}) collective-permute-start(bf16[64,4096]{1,0:T(8,128)(2,1)} %bitcast.19), channel_id=1, source_target_pairs={{1,0},{0,2},{2,3},{3,1},{5,4},{4,6},{6,7},{7,5},{9,8},{8,10},{10,1... | collective-permute-start | bytes 1572872 | tf_op jit(solution)/shard_map/ppermute | solution.py:113
  9.6 1.3 %slice.24 = bf16[384,1536]{1,0:T(8,128)(2,1)S(1)} slice(bf16[384,4096]{1,0:T(8,128)(2,1)} %bitcast.13), slice={[0:384], [0:1536]} | slice | bytes 2359296 | tf_op jit(solution)/shard_map/slice | solution.py:115
  11.0 0.0 copy-start
  11.0 3.6 %collective-permute-start.3 = (bf16[384,1536]{1,0:T(8,128)(2,1)S(1)}, bf16[384,1536]{1,0:T(8,128)(2,1)S(1)}, u32[]{:S(2)}, u32[]{:S(2)}) collective-permute-start(bf16[384,1536]{1,0:T(8,128)(2,1)S(1)} %slice.24), channel_id=1, source_target_pairs={{0,2},{2,0},{1,3},{3,1},{4,6},{6,4},{5,7},{7,5},{8,10},{10,8},{9,1... | collective-permute-start | bytes 3538952 | tf_op jit(solution)/shard_map/ppermute | solution.py:115
  14.6 0.0 copy-done.2
  14.6 0.1 fusion
  14.8 0.1 fusion.1
  14.9 0.1 broadcast_in_dim.2
  15.0 36.2 %all-gather.4 = f16[128,4224]{1,0:T(8,128)(2,1)S(1)} all-gather(f16[8,4224]{1,0:T(8,128)(2,1)S(1)} %pad_maximum_fusion), channel_id=2, replica_groups={{0,5,8,13,16,21,24,29,32,37,40,45,48,53,56,61},{1,4,9,12,17,20,25,28,33..., dimensions={0}, use_global_device_ids=true | all-gather | bytes 1148928 | tf_op jit(solution)/shard_map/all_gather | solution.py:23
  51.2 0.0 collective-permute-done.1.crossed
  51.2 0.0 collective-permute-done.cycled
  51.2 0.1 exponential_reduce_fusion
  51.3 0.3 multiply_convert_fusion.1.rows
  51.6 0.0 copy-start.1
  51.6 4.5 %collective-permute-start.2 = (bf16[128,4096]{1,0:T(8,128)(2,1)S(1)}, bf16[128,4096]{1,0:T(8,128)(2,1)S(1)}, u32[]{:S(2)}, u32[]{:S(2)}) collective-permute-start(bf16[128,4096]{1,0:T(8,128)(2,1)S(1)} %multiply_convert_fusion.1.rows), channel_id=1, source_target_pairs={{0,1},{1,0},{2,3},{3,2},{4,5},{5,4},{6,7},{7,6},{8,9},{9,8},{10,11... | collective-permute-start | bytes 3145736 | tf_op jit(solution)/shard_map/ppermute | solution.py:127
  56.1 0.0 copy-done
  56.1 0.1 slice.27
  56.3 4.9 %collective-permute-start.5 = (bf16[384,2560]{1,0:T(8,128)(2,1)S(1)}, bf16[384,2560]{1,0:T(8,128)(2,1)S(1)}, u32[]{:S(2)}, u32[]{:S(2)}) collective-permute-start(bf16[384,2560]{1,0:T(8,128)(2,1)S(1)} %slice.27), channel_id=1, source_target_pairs={{0,2},{2,0},{1,3},{3,1},{4,6},{6,4},{5,7},{7,5},{8,10},{10,8},{9,1... | collective-permute-start | bytes 5898248 | tf_op jit(solution)/shard_map/ppermute | solution.py:116
  61.2 0.0 copy-done.1
  61.2 0.5 shard_map.37.near
  61.7 0.0 collective-permute-done.2.rows
  61.7 0.6 shard_map.38
  62.3 0.0 collective-permute-done.3.early
  62.3 33.2 %all-gather.5 = f16[4224,128]{1,0:T(8,128)(2,1)S(1)} all-gather(f16[264,128]{1,0:T(8,128)(2,1)S(1)} %convert_element_type.41), channel_id=3, replica_groups={{0,5,8,13,16,21,24,29,32,37,40,45,48,53,56,61},{1,4,9,12,17,20,25,28,33..., dimensions={0}, use_global_device_ids=true | all-gather | bytes 1148928 | tf_op jit(solution)/shard_map/all_gather | solution.py:23
  95.5 0.2 fusion.5
  95.7 0.3 multiply_convert_fusion.own
  96.1 2.0 %collective-permute-start.4 = (bf16[16,256,128]{2,1,0:T(8,128)(2,1)S(1)}, bf16[16,256,128]{2,1,0:T(8,128)(2,1)S(1)}, u32[]{:S(2)}, u32[]{:S(2)}) collective-permute-start(bf16[16,256,128]{2,1,0:T(8,128)(2,1)S(1)} %multiply_convert_fusion.own), channel_id=1, source_target_pairs={{0,1},{1,0},{2,3},{3,2},{4,5},{5,4},{6,7},{7,6},{8,9},{9,8},{10,11... | collective-permute-start | bytes 3145736 | tf_op jit(solution)/shard_map/ppermute | solution.py:143
  98.1 0.8 shard_map.39.begun
  98.9 5.3 %collective-permute-done.5.late = bf16[384,2560]{1,0:T(8,128)(2,1)S(1)} collective-permute-done((bf16[384,2560]{1,0:T(8,128)(2,1)S(1)}, bf16[384,2560]{1,0:T(8,128)(2,1)S(1)}, u32[]{:S(2)}, u32[]{:S(2)}) %collective-permute-start.5) | collective-permute-done | bytes 1966112 | tf_op jit(solution)/shard_map/ppermute | solution.py:116
  104.2 0.0 collective-permute-done.4.other
  104.2 1.8 %shard_map.40 = f32[8,2,32,384]{3,2,1,0:T(8,128)S(1)} custom-call(f32[256,384]{1,0:T(8,128)S(1)} %shard_map.39.begun, bf16[16,256,128]{2,1,0:T(8,128)(2,1)S(1)} %multiply_convert_fusion.own, bf16[16,256,128]{2,1,0:T(8,128)(2,1)S(1)} %collective-permute-done.4.other, bf16[384,4096]{1,0:T(8,128)(2,1)S(1)} %bitcast.16, ...), custom_call_target="tpu_custom_call" | custom-call | flops 3145728 | bytes 1048576 | tf_op jit(solution)/shard_map/pallas_call | solution.py:95
  106.0 19.3 %all_to_all.5 = f32[16,32,384]{2,1,0:T(8,128)S(1)} all-to-all(f32[16,32,384]{2,1,0:T(8,128)S(1)} %bitcast.17), channel_id=1, replica_groups=mesh['layer'=8,'z'=16,'xh'=2,'c'=2] {'layer','xh'}, dimensions={0} | all-to-all | bytes 1572864 | tf_op jit(solution)/shard_map/all_to_all | solution.py:148
  125.3 0.6 copy.5
  (4 shorter events, 0.1 us)
Async XLA Ops:
  0.0 14.6 %copy-start.2 = (bf16[1,8,4096]{2,1,0:T(8,128)(2,1)S(1)}, bf16[1,8,4096]{2,1,0:T(8,128)(2,1)}, u32[]{:S(2)}) copy-start(bf16[1,8,4096]{2,1,0:T(8,128)(2,1)} %param.3) | copy-start | bytes 196612
  0.0 51.2 %collective-permute-start.1 = (bf16[64,4096]{1,0:T(8,128)(2,1)}, bf16[64,4096]{1,0:T(8,128)(2,1)S(1)}, u32[]{:S(2)}, u32[]{:S(2)}) collective-permute-start(bf16[64,4096]{1,0:T(8,128)(2,1)} %bitcast.18), channel_id=1, source_target_pairs={{1,2},{2,1},{5,6},{6,5},{9,10},{10,9},{13,14},{14,13},{17,18},{18,... | collective-permute-start | bytes 1572872 | tf_op jit(solution)/shard_map/ppermute | solution.py:114
  6.2 45.0 %collective-permute-start = (bf16[64,4096]{1,0:T(8,128)(2,1)}, bf16[64,4096]{1,0:T(8,128)(2,1)S(1)}, u32[]{:S(2)}, u32[]{:S(2)}) collective-permute-start(bf16[64,4096]{1,0:T(8,128)(2,1)} %bitcast.19), channel_id=1, source_target_pairs={{1,0},{0,2},{2,3},{3,1},{5,4},{4,6},{6,7},{7,5},{9,8},{8,10},{10,1... | collective-permute-start | bytes 1572872 | tf_op jit(solution)/shard_map/ppermute | solution.py:113
  11.0 45.2 %copy-start = (bf16[1,384,4096]{2,1,0:T(8,128)(2,1)S(1)}, bf16[1,384,4096]{2,1,0:T(8,128)(2,1)}, u32[]{:S(2)}) copy-start(bf16[1,384,4096]{2,1,0:T(8,128)(2,1)} %param.5) | copy-start | bytes 9437188
  11.0 51.3 %collective-permute-start.3 = (bf16[384,1536]{1,0:T(8,128)(2,1)S(1)}, bf16[384,1536]{1,0:T(8,128)(2,1)S(1)}, u32[]{:S(2)}, u32[]{:S(2)}) collective-permute-start(bf16[384,1536]{1,0:T(8,128)(2,1)S(1)} %slice.24), channel_id=1, source_target_pairs={{0,2},{2,0},{1,3},{3,1},{4,6},{6,4},{5,7},{7,5},{8,10},{10,8},{9,1... | collective-permute-start | bytes 3538952 | tf_op jit(solution)/shard_map/ppermute | solution.py:115
  51.6 9.6 %copy-start.1 = (bf16[1,4096,64]{1,2,0:T(8,128)(2,1)S(1)}, bf16[1,4096,64]{1,2,0:T(8,128)(2,1)}, u32[]{:S(2)}) copy-start(bf16[1,4096,64]{1,2,0:T(8,128)(2,1)} %param.4) | copy-start | bytes 1572868
  51.6 10.0 %collective-permute-start.2 = (bf16[128,4096]{1,0:T(8,128)(2,1)S(1)}, bf16[128,4096]{1,0:T(8,128)(2,1)S(1)}, u32[]{:S(2)}, u32[]{:S(2)}) collective-permute-start(bf16[128,4096]{1,0:T(8,128)(2,1)S(1)} %multiply_convert_fusion.1.rows), channel_id=1, source_target_pairs={{0,1},{1,0},{2,3},{3,2},{4,5},{5,4},{6,7},{7,6},{8,9},{9,8},{10,11... | collective-permute-start | bytes 3145736 | tf_op jit(solution)/shard_map/ppermute | solution.py:127
  56.3 47.9 %collective-permute-start.5 = (bf16[384,2560]{1,0:T(8,128)(2,1)S(1)}, bf16[384,2560]{1,0:T(8,128)(2,1)S(1)}, u32[]{:S(2)}, u32[]{:S(2)}) collective-permute-start(bf16[384,2560]{1,0:T(8,128)(2,1)S(1)} %slice.27), channel_id=1, source_target_pairs={{0,2},{2,0},{1,3},{3,1},{4,6},{6,4},{5,7},{7,5},{8,10},{10,8},{9,1... | collective-permute-start | bytes 5898248 | tf_op jit(solution)/shard_map/ppermute | solution.py:116
  96.1 8.1 %collective-permute-start.4 = (bf16[16,256,128]{2,1,0:T(8,128)(2,1)S(1)}, bf16[16,256,128]{2,1,0:T(8,128)(2,1)S(1)}, u32[]{:S(2)}, u32[]{:S(2)}) collective-permute-start(bf16[16,256,128]{2,1,0:T(8,128)(2,1)S(1)} %multiply_convert_fusion.own), channel_id=1, source_target_pairs={{0,1},{1,0},{2,3},{3,2},{4,5},{5,4},{6,7},{7,6},{8,9},{9,8},{10,11... | collective-permute-start | bytes 3145736 | tf_op jit(solution)/shard_map/ppermute | solution.py:143

commit v5 on v4

v5 whole, which is shorter than its diff:
```python
import functools

import jax
import jax.numpy as jnp
from jax import lax
from jax.experimental import pallas as pl
from jax.experimental.pallas import tpu as pltpu
from jax.sharding import Mesh, PartitionSpec as P

TOP = 14.0
AXES = ("layer", "z", "xh", "c")
SWAP = [(0, 1), (1, 0)]
NT = (((1,), (1,)), ((), ()))


def exponent_of(peak):
    return jnp.clip(jnp.floor(jnp.log2(jnp.maximum(peak, 1e-37))), -100.0, 100.0)


def gather_z(x, groups):
    return lax.all_gather(x, AXES, axis=0, axis_index_groups=groups)


def side_of():
    return lax.rem(lax.axis_index("c") + lax.axis_index("z"), 2)


def columns_of(mine, got):
    first = lax.axis_index("xh") == 0
    return jnp.concatenate([jnp.where(first, mine[...], got[...]), jnp.where(first, got[...], mine[...])], axis=0)


def rounded_product(rows, columns):
    value = lax.dot_general(rows[...], columns, NT, preferred_element_type=jnp.float32)
    return value.astype(jnp.bfloat16).astype(jnp.float32)


def near_kernel(rows, mine, got, out):
    out[...] = rounded_product(rows, columns_of(mine, got))


def chunk_kernel(near, rows, mine, got, out, order):
    side = side_of()
    far = rounded_product(rows, columns_of(mine, got))
    height = order.shape[0]
    group = out.shape[0] - height
    for z in range(height // (2 * group)):
        first = lax.rem(side + z, 2)
        piece = slice(z * group, (z + 1) * group)
        order[pl.ds(pl.multiple_of((2 * z + first) * group, group), group)] = near[piece]
        order[pl.ds(pl.multiple_of((2 * z + 1 - first) * group, group), group)] = far[piece]
    value = order[...]
    peak = jnp.max(jnp.max(jnp.abs(value), axis=0, keepdims=True), axis=1, keepdims=True)
    exponent = exponent_of(peak)
    tail = jnp.broadcast_to(exponent, (group, out.shape[1]))
    out[...] = jnp.concatenate([value * jnp.exp2(TOP - exponent), tail], axis=0)


def score_kernel(own, other, train, early, late, out):
    side, chip = side_of(), lax.axis_index("xh")
    layers, _, rows, count = out.shape
    half = own.shape[2] // 2
    here = jnp.zeros((own.shape[1], count), jnp.float32)
    there = here
    for z in range(own.shape[0]):
        mixed = lax.rem(side + z, 2) == 0
        one = jnp.where(mixed, own[z], other[z])
        two = jnp.where(mixed, other[z], own[z])
        left = jnp.concatenate([one[:, :half], two[:, :half], one[:, half:], two[:, half:]], axis=1)
        span = left.shape[1]
        piece, begin = (early, z * span) if z * span < early.shape[1] else (late, z * span - early.shape[1])
        right = train[:, z * span : (z + 1) * span]
        here = here + lax.dot_general(left, right, NT, preferred_element_type=jnp.float32)
        right = piece[:, begin : begin + span]
        there = there + lax.dot_general(left, right, NT, preferred_element_type=jnp.float32)
    for layer in range(layers):
        out[layer, chip] = here[layer * rows : (layer + 1) * rows].astype(out.dtype)
        out[layer, 1 - chip] = there[layer * rows : (layer + 1) * rows].astype(out.dtype)


def in_vmem(kernel, out_shape, *operands, scratch=()):
    flops = 2 * operands[0].size * operands[1].shape[0]
    spec = pl.BlockSpec(memory_space=pltpu.VMEM)
    return pl.pallas_call(
        kernel,
        out_shape=out_shape,
        in_specs=[spec] * len(operands),
        out_specs=spec,
        scratch_shapes=scratch,
        compiler_params=pltpu.CompilerParams(vmem_limit_bytes=40 * 2**20),
        cost_estimate=pl.CostEstimate(flops=flops, bytes_accessed=2**20, transcendentals=0),
    )(*operands)


def on_device(groups, queries, fisher, train_grads):
    width, group = queries.shape[2], queries.shape[1]
    layers, slots = lax.axis_size("layer"), lax.axis_size("z")
    train = train_grads[0]
    cut = 4 * fisher.shape[2] * (slots * 7 // 16)

    mine = fisher[0].T
    fisher_got = lax.ppermute(mine, "xh", SWAP)
    early = lax.ppermute(train[:, :cut], "xh", SWAP)
    late = lax.ppermute(train[:, cut:], "xh", SWAP)

    wide = queries[0].astype(jnp.float32)
    exponent = exponent_of(jnp.max(jnp.abs(wide), axis=1, keepdims=True))
    scaled = (wide * jnp.exp2(TOP - exponent)).astype(jnp.float16)
    tail = jnp.broadcast_to(exponent, (group, 128)).astype(jnp.float16)
    rows = gather_z(jnp.concatenate([scaled, tail], axis=1), groups).reshape(slots * group, width + 128)
    rows, fisher_got = lax.optimization_barrier((rows, fisher_got))
    back = jnp.exp2(rows[:, width : width + 1].astype(jnp.float32) - TOP)
    rows = (rows[:, :width].astype(jnp.float32) * back).astype(jnp.bfloat16)
    rows_got = lax.ppermute(rows, "c", SWAP)

    height, span = slots * 2 * group, 2 * mine.shape[0]
    near = in_vmem(near_kernel, jax.ShapeDtypeStruct((height // 2, span), jnp.float32), rows, mine, fisher_got)
    chunk = in_vmem(
        chunk_kernel,
        jax.ShapeDtypeStruct((height + group, span), jnp.float32),
        near,
        rows_got,
        mine,
        fisher_got,
        scratch=[pltpu.VMEM((height, span), jnp.float32)],
    )
    chunk, early = lax.optimization_barrier((chunk, early))
    blocks = gather_z(chunk.astype(jnp.float16), groups)
    back = jnp.exp2(blocks[:, height : height + 1, :1].astype(jnp.float32) - TOP)
    own = (blocks[:, :height].astype(jnp.float32) * back).astype(jnp.bfloat16)
    other = lax.ppermute(own, "c", SWAP)
    parts_shape = jax.ShapeDtypeStruct((layers, 2, height // layers, train.shape[0]), jnp.float32)
    parts = in_vmem(score_kernel, parts_shape, own, other, train, early, late)

    parts = lax.all_to_all(parts.reshape(2 * layers, height // layers, -1), ("layer", "xh"), 0, 0)
    total = jnp.sum(parts.reshape(layers, 2, -1, 2 * group, parts.shape[-1]), axis=0)
    return jnp.swapaxes(total, 0, 1).reshape(-1, parts.shape[-1])


def solution(mesh):
    layers, spread = mesh.devices.shape
    slots = spread // 4
    fine = Mesh(mesh.devices.reshape(layers, slots, 2, 2), AXES)
    groups = [
        [layer * spread + 4 * z + 2 * chip + (side + z) % 2 for z in range(slots)]
        for layer in range(layers)
        for chip in range(2)
        for side in range(2)
    ]
    ex = ("z", "xh", "c")
    in_specs = (P("layer", ex, None), P("layer", None, ex), P("layer", ex, None))
    return jax.shard_map(
        functools.partial(on_device, groups),
        mesh=fine,
        in_specs=in_specs,
        out_specs=P("layer", ex),
        check_vma=False,
    )
```

time: 126 us -> 119 us (0.944)
  starting transfers between devices: 24.6 us -> 16.6 us
  blocking collectives: 88.7 us -> 92.3 us
  waiting for transfers between devices: 5.32 us -> 2.63 us
    all_gather x2, blocking collectives: 69.5 us -> 74.5 us  [gather_z(): return lax.all_gather(x, AXES, axis=0, axis_index_groups=groups)]
    ppermute x1, waiting for transfers between devices: 5.31 us -> 1.29 us  [on_device(): late = lax.ppermute(train[:, cut:], 'xh', SWAP)]
    ppermute x2 -> x1, starting transfers between devices: 9.6 us -> 5.6 us  [on_device(): fisher_got = lax.ppermute(mine, 'xh', SWAP)]
    ppermute x1, starting transfers between devices: 4.5 us -> 2.05 us  [on_device(): rows_got = lax.ppermute(rows, 'c', SWAP)]
    ppermute x1, starting transfers between devices: 3.61 us -> 1.92 us  [on_device(): early = lax.ppermute(train[:, :cut], 'xh', SWAP)]
    all_to_all x1, blocking collectives: 19.3 us -> 17.7 us  [on_device(): lax.all_to_all(parts.reshape(2 * layers, height // layers, -1), ('layer',...]
    ppermute x1, waiting for transfers between devices: 0.01 us -> 1.34 us  [on_device(): other = lax.ppermute(own, 'c', SWAP)]
    pallas_call x4 -> x3, Pallas kernels: 3.66 us -> 3.45 us  [in_vmem(): pl.pallas_call(kernel, out_shape=out_shape, in_specs=[spec] * len(operand...]
  transfers between devices with their start and end apart: 6 -> 5, of which waited for: 1 -> 2; matrix products, arithmetic and copies ran while one was open for 2% -> 2% of each run, Pallas kernels for 1% -> 1%
where the time goes in v5:
time: 119 us
  blocking collectives  92.3 us (78%)
  starting transfers between devices  16.6 us (14%)
  Pallas kernels  3.45 us (3%)
  waiting for transfers between devices  2.63 us (2%)
  local copies, waits for them, and re-layouts  2.31 us (2%)
  other arithmetic  1.23 us (1%)
    all_gather x2, blocking collectives, gather_z(): return lax.all_gather(x, AXES, axis=0, axis_index_groups=groups)  74.5 us
    all_to_all x1, blocking collectives, on_device(): lax.all_to_all(parts.reshape(2 * layers, height // layers, -1), ('layer',...  17.7 us
    ppermute x1, starting transfers between devices, on_device(): fisher_got = lax.ppermute(mine, 'xh', SWAP)  5.6 us
    ppermute x1, starting transfers between devices, on_device(): late = lax.ppermute(train[:, cut:], 'xh', SWAP)  5.14 us
    pallas_call x3, Pallas kernels, in_vmem(): pl.pallas_call(kernel, out_shape=out_shape, in_specs=[spec] * len(operand...  3.45 us
  transfers between devices with their start and end apart: 5, of which 2 were waited for; matrix products, arithmetic and copies ran while one was open for 2% of the time, Pallas kernels for 1%

profile of v5, /device:TPU:1, one launch (start us, length us, event | category | flops | bytes accessed | tf_op | source)
XLA Modules:
  0.0 118.7 jit_solution(17453008607340003321)
XLA Ops:
  0.0 0.0 copy-start.2
  0.0 5.6 %collective-permute-start = (bf16[64,4096]{1,0:T(8,128)(2,1)}, bf16[64,4096]{1,0:T(8,128)(2,1)S(1)}, u32[]{:S(2)}, u32[]{:S(2)}) collective-permute-start(bf16[64,4096]{1,0:T(8,128)(2,1)} %bitcast.17), channel_id=1, source_target_pairs={{0,2},{2,0},{1,3},{3,1},{4,6},{6,4},{5,7},{7,5},{8,10},{10,8},{9,1... | collective-permute-start | bytes 1572872 | tf_op jit(solution)/shard_map/ppermute | solution.py:102
  5.6 1.4 %slice.24 = bf16[384,1792]{1,0:T(8,128)(2,1)S(1)} slice(bf16[384,4096]{1,0:T(8,128)(2,1)} %bitcast.13), slice={[0:384], [0:1792]} | slice | bytes 2752512 | tf_op jit(solution)/shard_map/slice | solution.py:103
  7.0 1.9 %collective-permute-start.2 = (bf16[384,1792]{1,0:T(8,128)(2,1)S(1)}, bf16[384,1792]{1,0:T(8,128)(2,1)S(1)}, u32[]{:S(2)}, u32[]{:S(2)}) collective-permute-start(bf16[384,1792]{1,0:T(8,128)(2,1)S(1)} %slice.24), channel_id=1, source_target_pairs={{0,2},{2,0},{1,3},{3,1},{4,6},{6,4},{5,7},{7,5},{8,10},{10,8},{9,1... | collective-permute-start | bytes 4128776 | tf_op jit(solution)/shard_map/ppermute | solution.py:103
  9.0 0.0 copy-done.2
  9.0 0.1 fusion
  9.1 0.0 copy-start
  9.1 0.1 fusion.1
  9.2 0.1 broadcast_in_dim.2
  9.3 40.9 %all-gather.4 = f16[128,4224]{1,0:T(8,128)(2,1)S(1)} all-gather(f16[8,4224]{1,0:T(8,128)(2,1)S(1)} %pad_maximum_fusion), channel_id=2, replica_groups={{0,5,8,13,16,21,24,29,32,37,40,45,48,53,56,61},{1,4,9,12,17,20,25,28,33..., dimensions={0}, use_global_device_ids=true | all-gather | bytes 1148928 | tf_op jit(solution)/shard_map/all_gather | solution.py:21
  50.2 0.0 collective-permute-done.got
  50.2 0.1 exponential_reduce_fusion
  50.4 0.3 multiply_convert_fusion.1.rows
  50.7 0.0 copy-start.1
  50.7 2.1 %collective-permute-start.1 = (bf16[128,4096]{1,0:T(8,128)(2,1)S(1)}, bf16[128,4096]{1,0:T(8,128)(2,1)S(1)}, u32[]{:S(2)}, u32[]{:S(2)}) collective-permute-start(bf16[128,4096]{1,0:T(8,128)(2,1)S(1)} %multiply_convert_fusion.1.rows), channel_id=1, source_target_pairs={{0,1},{1,0},{2,3},{3,2},{4,5},{5,4},{6,7},{7,6},{8,9},{9,8},{10,11... | collective-permute-start | bytes 3145736 | tf_op jit(solution)/shard_map/ppermute | solution.py:114
  52.7 0.0 copy-done
  52.7 0.1 slice.27
  52.9 5.1 %collective-permute-start.4 = (bf16[384,2304]{1,0:T(8,128)(2,1)S(1)}, bf16[384,2304]{1,0:T(8,128)(2,1)S(1)}, u32[]{:S(2)}, u32[]{:S(2)}) collective-permute-start(bf16[384,2304]{1,0:T(8,128)(2,1)S(1)} %slice.27), channel_id=1, source_target_pairs={{0,2},{2,0},{1,3},{3,1},{4,6},{6,4},{5,7},{7,5},{8,10},{10,8},{9,1... | collective-permute-start | bytes 5308424 | tf_op jit(solution)/shard_map/ppermute | solution.py:104
  58.0 0.0 copy-done.1
  58.0 0.5 shard_map.37.near
  58.5 0.0 collective-permute-done.1.rows
  58.5 0.6 shard_map.38
  59.1 0.0 collective-permute-done.2.early
  59.2 33.6 %all-gather.5 = f16[4224,128]{1,0:T(8,128)(2,1)S(1)} all-gather(f16[264,128]{1,0:T(8,128)(2,1)S(1)} %convert_element_type.41), channel_id=3, replica_groups={{0,5,8,13,16,21,24,29,32,37,40,45,48,53,56,61},{1,4,9,12,17,20,25,28,33..., dimensions={0}, use_global_device_ids=true | all-gather | bytes 1148928 | tf_op jit(solution)/shard_map/all_gather | solution.py:21
  92.8 0.2 fusion.5
  93.0 0.3 multiply_convert_fusion.own
  93.3 1.9 %collective-permute-start.3 = (bf16[16,256,128]{2,1,0:T(8,128)(2,1)S(1)}, bf16[16,256,128]{2,1,0:T(8,128)(2,1)S(1)}, u32[]{:S(2)}, u32[]{:S(2)}) collective-permute-start(bf16[16,256,128]{2,1,0:T(8,128)(2,1)S(1)} %multiply_convert_fusion.own), channel_id=1, source_target_pairs={{0,1},{1,0},{2,3},{3,2},{4,5},{5,4},{6,7},{7,6},{8,9},{9,8},{10,11... | collective-permute-start | bytes 3145736 | tf_op jit(solution)/shard_map/ppermute | solution.py:131
  95.3 1.3 %collective-permute-done.4.late = bf16[384,2304]{1,0:T(8,128)(2,1)S(1)} collective-permute-done((bf16[384,2304]{1,0:T(8,128)(2,1)S(1)}, bf16[384,2304]{1,0:T(8,128)(2,1)S(1)}, u32[]{:S(2)}, u32[]{:S(2)}) %collective-permute-start.4) | collective-permute-done | bytes 1769504 | tf_op jit(solution)/shard_map/ppermute | solution.py:104
  96.5 1.3 %collective-permute-done.3.other = bf16[16,256,128]{2,1,0:T(8,128)(2,1)S(1)} collective-permute-done((bf16[16,256,128]{2,1,0:T(8,128)(2,1)S(1)}, bf16[16,256,128]{2,1,0:T(8,128)(2,1)S(1)}, u32[]{:S(2)}, u32[]{:S(2)}) %collective-permute-start.3) | collective-permute-done | bytes 1048608 | tf_op jit(solution)/shard_map/ppermute | solution.py:131
  97.9 2.4 %shard_map.39 = f32[8,2,32,384]{3,2,1,0:T(8,128)S(1)} custom-call(bf16[16,256,128]{2,1,0:T(8,128)(2,1)S(1)} %multiply_convert_fusion.own, bf16[16,256,128]{2,1,0:T(8,128)(2,1)S(1)} %collective-permute-done.3.other, bf16[384,4096]{1,0:T(8,128)(2,1)S(1)} %bitcast.15, bf16[384,1792]{1,0:T(8,128)(2,1)S(1)} %collective-permute-done.2.early, ...), custom_call_target="tpu_custom_call" | custom-call | flops 16777216 | bytes 1048576 | tf_op jit(solution)/shard_map/pallas_call | solution.py:84
  100.3 17.7 %all_to_all.5 = f32[16,32,384]{2,1,0:T(8,128)S(1)} all-to-all(f32[16,32,384]{2,1,0:T(8,128)S(1)} %bitcast.16), channel_id=1, replica_groups=mesh['layer'=8,'z'=16,'xh'=2,'c'=2] {'layer','xh'}, dimensions={0} | all-to-all | bytes 1572864 | tf_op jit(solution)/shard_map/all_to_all | solution.py:135
  118.1 0.6 copy.5
  (4 shorter events, 0.1 us)
Async XLA Ops:
  0.0 9.0 %copy-start.2 = (bf16[1,8,4096]{2,1,0:T(8,128)(2,1)S(1)}, bf16[1,8,4096]{2,1,0:T(8,128)(2,1)}, u32[]{:S(2)}) copy-start(bf16[1,8,4096]{2,1,0:T(8,128)(2,1)} %param.3) | copy-start | bytes 196612
  0.0 50.2 %collective-permute-start = (bf16[64,4096]{1,0:T(8,128)(2,1)}, bf16[64,4096]{1,0:T(8,128)(2,1)S(1)}, u32[]{:S(2)}, u32[]{:S(2)}) collective-permute-start(bf16[64,4096]{1,0:T(8,128)(2,1)} %bitcast.17), channel_id=1, source_target_pairs={{0,2},{2,0},{1,3},{3,1},{4,6},{6,4},{5,7},{7,5},{8,10},{10,8},{9,1... | collective-permute-start | bytes 1572872 | tf_op jit(solution)/shard_map/ppermute | solution.py:102
  7.0 52.1 %collective-permute-start.2 = (bf16[384,1792]{1,0:T(8,128)(2,1)S(1)}, bf16[384,1792]{1,0:T(8,128)(2,1)S(1)}, u32[]{:S(2)}, u32[]{:S(2)}) collective-permute-start(bf16[384,1792]{1,0:T(8,128)(2,1)S(1)} %slice.24), channel_id=1, source_target_pairs={{0,2},{2,0},{1,3},{3,1},{4,6},{6,4},{5,7},{7,5},{8,10},{10,8},{9,1... | collective-permute-start | bytes 4128776 | tf_op jit(solution)/shard_map/ppermute | solution.py:103
  9.1 43.6 %copy-start = (bf16[1,384,4096]{2,1,0:T(8,128)(2,1)S(1)}, bf16[1,384,4096]{2,1,0:T(8,128)(2,1)}, u32[]{:S(2)}) copy-start(bf16[1,384,4096]{2,1,0:T(8,128)(2,1)} %param.5) | copy-start | bytes 9437188
  50.7 7.4 %copy-start.1 = (bf16[1,4096,64]{1,2,0:T(8,128)(2,1)S(1)}, bf16[1,4096,64]{1,2,0:T(8,128)(2,1)}, u32[]{:S(2)}) copy-start(bf16[1,4096,64]{1,2,0:T(8,128)(2,1)} %param.4) | copy-start | bytes 1572868
  50.7 7.8 %collective-permute-start.1 = (bf16[128,4096]{1,0:T(8,128)(2,1)S(1)}, bf16[128,4096]{1,0:T(8,128)(2,1)S(1)}, u32[]{:S(2)}, u32[]{:S(2)}) collective-permute-start(bf16[128,4096]{1,0:T(8,128)(2,1)S(1)} %multiply_convert_fusion.1.rows), channel_id=1, source_target_pairs={{0,1},{1,0},{2,3},{3,2},{4,5},{5,4},{6,7},{7,6},{8,9},{9,8},{10,11... | collective-permute-start | bytes 3145736 | tf_op jit(solution)/shard_map/ppermute | solution.py:114
  52.9 43.7 %collective-permute-start.4 = (bf16[384,2304]{1,0:T(8,128)(2,1)S(1)}, bf16[384,2304]{1,0:T(8,128)(2,1)S(1)}, u32[]{:S(2)}, u32[]{:S(2)}) collective-permute-start(bf16[384,2304]{1,0:T(8,128)(2,1)S(1)} %slice.27), channel_id=1, source_target_pairs={{0,2},{2,0},{1,3},{3,1},{4,6},{6,4},{5,7},{7,5},{8,10},{10,8},{9,1... | collective-permute-start | bytes 5308424 | tf_op jit(solution)/shard_map/ppermute | solution.py:104
  93.3 4.6 %collective-permute-start.3 = (bf16[16,256,128]{2,1,0:T(8,128)(2,1)S(1)}, bf16[16,256,128]{2,1,0:T(8,128)(2,1)S(1)}, u32[]{:S(2)}, u32[]{:S(2)}) collective-permute-start(bf16[16,256,128]{2,1,0:T(8,128)(2,1)S(1)} %multiply_convert_fusion.own), channel_id=1, source_target_pairs={{0,1},{1,0},{2,3},{3,2},{4,5},{5,4},{6,7},{7,6},{8,9},{9,8},{10,11... | collective-permute-start | bytes 3145736 | tf_op jit(solution)/shard_map/ppermute | solution.py:131

commit v6 on v5

--- a/solution.py
+++ b/solution.py
@@ -56,7 +56,7 @@
     out[...] = jnp.concatenate([value * jnp.exp2(TOP - exponent), tail], axis=0)
 
 
-def score_kernel(own, other, train, early, late, out):
+def score_kernel(own, other, train, got, out):
     side, chip = side_of(), lax.axis_index("xh")
     layers, _, rows, count = out.shape
     half = own.shape[2] // 2
@@ -68,10 +68,9 @@
         two = jnp.where(mixed, other[z], own[z])
         left = jnp.concatenate([one[:, :half], two[:, :half], one[:, half:], two[:, half:]], axis=1)
         span = left.shape[1]
-        piece, begin = (early, z * span) if z * span < early.shape[1] else (late, z * span - early.shape[1])
         right = train[:, z * span : (z + 1) * span]
         here = here + lax.dot_general(left, right, NT, preferred_element_type=jnp.float32)
-        right = piece[:, begin : begin + span]
+        right = got[:, z * span : (z + 1) * span]
         there = there + lax.dot_general(left, right, NT, preferred_element_type=jnp.float32)
     for layer in range(layers):
         out[layer, chip] = here[layer * rows : (layer + 1) * rows].astype(out.dtype)
@@ -96,12 +95,10 @@
     width, group = queries.shape[2], queries.shape[1]
     layers, slots = lax.axis_size("layer"), lax.axis_size("z")
     train = train_grads[0]
-    cut = 4 * fisher.shape[2] * (slots * 7 // 16)
 
     mine = fisher[0].T
     fisher_got = lax.ppermute(mine, "xh", SWAP)
-    early = lax.ppermute(train[:, :cut], "xh", SWAP)
-    late = lax.ppermute(train[:, cut:], "xh", SWAP)
+    train_got = lax.ppermute(train, "xh", SWAP)
 
     wide = queries[0].astype(jnp.float32)
     exponent = exponent_of(jnp.max(jnp.abs(wide), axis=1, keepdims=True))
@@ -124,13 +121,12 @@
         fisher_got,
         scratch=[pltpu.VMEM((height, span), jnp.float32)],
     )
-    chunk, early = lax.optimization_barrier((chunk, early))
     blocks = gather_z(chunk.astype(jnp.float16), groups)
     back = jnp.exp2(blocks[:, height : height + 1, :1].astype(jnp.float32) - TOP)
     own = (blocks[:, :height].astype(jnp.float32) * back).astype(jnp.bfloat16)
     other = lax.ppermute(own, "c", SWAP)
     parts_shape = jax.ShapeDtypeStruct((layers, 2, height // layers, train.shape[0]), jnp.float32)
-    parts = in_vmem(score_kernel, parts_shape, own, other, train, early, late)
+    parts = in_vmem(score_kernel, parts_shape, own, other, train, train_got)
 
     parts = lax.all_to_all(parts.reshape(2 * layers, height // layers, -1), ("layer", "xh"), 0, 0)
     total = jnp.sum(parts.reshape(layers, 2, -1, 2 * group, parts.shape[-1]), axis=0)

time: 119 us -> 117 us (0.983)
  starting transfers between devices: 16.6 us -> 11.7 us
  waiting for transfers between devices: 2.63 us -> 4.42 us
  other arithmetic: 1.23 us -> 2.92 us
  local copies, waits for them, and re-layouts: 2.31 us -> 0.73 us
    ppermute x2 -> x1, starting transfers between devices: 7.06 us -> 1.92 us  [on_device(): train_got = lax.ppermute(train, 'xh', SWAP)]
    ppermute x1, waiting for transfers between devices: 0.01 us -> 2.15 us  [on_device(): rows_got = lax.ppermute(rows, 'c', SWAP)]
    all_to_all x1, blocking collectives: 17.7 us -> 19.5 us  [on_device(): lax.all_to_all(parts.reshape(2 * layers, height // layers, -1), ('layer',...]
    slice x2 -> x0, local copies, waits for them, and re-layouts: 1.57 us -> none  [the longest x1 1.43 us: on_device(): early = lax.ppermute(train[:, :cut], 'xh', SWAP)]
    ppermute x2 -> x1, waiting for transfers between devices: 1.29 us -> 0.01 us  [on_device(): train_got = lax.ppermute(train, 'xh', SWAP)]
  transfers between devices with their start and end apart: 5 -> 4, of which waited for: 2 -> 2; matrix products, arithmetic and copies ran while one was open for 2% -> 3% of each run, Pallas kernels for 1% -> 1%
where the time goes in v6:
time: 117 us
  blocking collectives  93.3 us (80%)
  starting transfers between devices  11.7 us (10%)
  waiting for transfers between devices  4.42 us (4%)
  Pallas kernels  3.45 us (3%)
  other arithmetic  2.92 us (2%)
    all_gather x2, blocking collectives, gather_z(): return lax.all_gather(x, AXES, axis=0, axis_index_groups=groups)  73.8 us
    all_to_all x1, blocking collectives, on_device(): lax.all_to_all(parts.reshape(2 * layers, height // layers, -1), ('layer',...  19.5 us
    ppermute x1, starting transfers between devices, on_device(): fisher_got = lax.ppermute(mine, 'xh', SWAP)  5.6 us
    pallas_call x3, Pallas kernels, in_vmem(): pl.pallas_call(kernel, out_shape=out_shape, in_specs=[spec] * len(operand...  3.45 us
  transfers between devices with their start and end apart: 4, of which 2 were waited for; matrix products, arithmetic and copies ran while one was open for 3% of the time, Pallas kernels for 1%

profile of v6, /device:TPU:1, one launch (start us, length us, event | category | flops | bytes accessed | tf_op | source)
XLA Modules:
  0.0 116.7 jit_solution(6292201650575665221)
XLA Ops:
  0.0 0.0 copy-start.1
  0.0 5.6 %collective-permute-start = (bf16[64,4096]{1,0:T(8,128)(2,1)}, bf16[64,4096]{1,0:T(8,128)(2,1)S(1)}, u32[]{:S(2)}, u32[]{:S(2)}) collective-permute-start(bf16[64,4096]{1,0:T(8,128)(2,1)} %bitcast.16), channel_id=1, source_target_pairs={{0,2},{2,0},{1,3},{3,1},{4,6},{6,4},{5,7},{7,5},{8,10},{10,8},{9,1... | collective-permute-start | bytes 1572872 | tf_op jit(solution)/shard_map/ppermute | solution.py:100
  5.6 1.9 %collective-permute-start.3 = (bf16[384,4096]{1,0:T(8,128)(2,1)}, bf16[384,4096]{1,0:T(8,128)(2,1)S(1)}, u32[]{:S(2)}, u32[]{:S(2)}) collective-permute-start(bf16[384,4096]{1,0:T(8,128)(2,1)} %bitcast.14), channel_id=1, source_target_pairs={{0,2},{2,0},{1,3},{3,1},{4,6},{6,4},{5,7},{7,5},{8,10},{10,8},{9,1... | collective-permute-start | bytes 9437192 | tf_op jit(solution)/shard_map/ppermute | solution.py:101
  7.5 1.0 fusion
  8.5 0.9 fusion.1
  9.5 0.1 broadcast_in_dim.2
  9.6 41.1 %all-gather.4 = f16[128,4224]{1,0:T(8,128)(2,1)S(1)} all-gather(f16[8,4224]{1,0:T(8,128)(2,1)S(1)} %pad_maximum_fusion), channel_id=2, replica_groups={{0,5,8,13,16,21,24,29,32,37,40,45,48,53,56,61},{1,4,9,12,17,20,25,28,33..., dimensions={0}, use_global_device_ids=true | all-gather | bytes 1148928 | tf_op jit(solution)/shard_map/all_gather | solution.py:21
  50.6 0.0 collective-permute-done.got
  50.6 0.1 exponential_reduce_fusion
  50.8 0.3 multiply_convert_fusion.1.rows
  51.0 1.9 %collective-permute-start.1 = (bf16[128,4096]{1,0:T(8,128)(2,1)S(1)}, bf16[128,4096]{1,0:T(8,128)(2,1)S(1)}, u32[]{:S(2)}, u32[]{:S(2)}) collective-permute-start(bf16[128,4096]{1,0:T(8,128)(2,1)S(1)} %multiply_convert_fusion.1.rows), channel_id=1, source_target_pairs={{0,1},{1,0},{2,3},{3,2},{4,5},{5,4},{6,7},{7,6},{8,9},{9,8},{10,11... | collective-permute-start | bytes 3145736 | tf_op jit(solution)/shard_map/ppermute | solution.py:111
  53.0 0.0 copy-done.1
  53.0 0.5 shard_map.37.near
  53.5 2.1 %collective-permute-done.1.rows = bf16[128,4096]{1,0:T(8,128)(2,1)S(1)} collective-permute-done((bf16[128,4096]{1,0:T(8,128)(2,1)S(1)}, bf16[128,4096]{1,0:T(8,128)(2,1)S(1)}, u32[]{:S(2)}, u32[]{:S(2)}) %collective-permute-start.1) | collective-permute-done | bytes 1048608 | tf_op jit(solution)/shard_map/ppermute | solution.py:111
  55.6 0.6 shard_map.38
  56.2 0.0 copy-start
  56.2 32.7 %all-gather.5 = f16[4224,128]{1,0:T(8,128)(2,1)S(1)} all-gather(f16[264,128]{1,0:T(8,128)(2,1)S(1)} %convert_element_type.41), channel_id=3, replica_groups={{0,5,8,13,16,21,24,29,32,37,40,45,48,53,56,61},{1,4,9,12,17,20,25,28,33..., dimensions={0}, use_global_device_ids=true | all-gather | bytes 1148928 | tf_op jit(solution)/shard_map/all_gather | solution.py:21
  89.0 0.2 fusion.5
  89.2 0.3 multiply_convert_fusion.own
  89.5 2.3 %collective-permute-start.2 = (bf16[16,256,128]{2,1,0:T(8,128)(2,1)S(1)}, bf16[16,256,128]{2,1,0:T(8,128)(2,1)S(1)}, u32[]{:S(2)}, u32[]{:S(2)}) collective-permute-start(bf16[16,256,128]{2,1,0:T(8,128)(2,1)S(1)} %multiply_convert_fusion.own), channel_id=1, source_target_pairs={{0,1},{1,0},{2,3},{3,2},{4,5},{5,4},{6,7},{7,6},{8,9},{9,8},{10,11... | collective-permute-start | bytes 3145736 | tf_op jit(solution)/shard_map/ppermute | solution.py:127
  91.8 2.3 %collective-permute-done.2.other = bf16[16,256,128]{2,1,0:T(8,128)(2,1)S(1)} collective-permute-done((bf16[16,256,128]{2,1,0:T(8,128)(2,1)S(1)}, bf16[16,256,128]{2,1,0:T(8,128)(2,1)S(1)}, u32[]{:S(2)}, u32[]{:S(2)}) %collective-permute-start.2) | collective-permute-done | bytes 1048608 | tf_op jit(solution)/shard_map/ppermute | solution.py:127
  94.1 0.0 collective-permute-done.3.got
  94.1 0.0 copy-done
  94.1 2.4 %shard_map.39 = f32[8,2,32,384]{3,2,1,0:T(8,128)S(1)} custom-call(bf16[16,256,128]{2,1,0:T(8,128)(2,1)S(1)} %multiply_convert_fusion.own, bf16[16,256,128]{2,1,0:T(8,128)(2,1)S(1)} %collective-permute-done.2.other, bf16[384,4096]{1,0:T(8,128)(2,1)S(1)} %bitcast.15, bf16[384,4096]{1,0:T(8,128)(2,1)S(1)} %collective-permute-done.3.got), custom_call_target="tpu_custom_call" | custom-call | flops 16777216 | bytes 1048576 | tf_op jit(solution)/shard_map/pallas_call | solution.py:83
  96.5 19.5 %all_to_all.5 = f32[16,32,384]{2,1,0:T(8,128)S(1)} all-to-all(f32[16,32,384]{2,1,0:T(8,128)S(1)} %bitcast.13), channel_id=1, replica_groups=mesh['layer'=8,'z'=16,'xh'=2,'c'=2] {'layer','xh'}, dimensions={0} | all-to-all | bytes 1572864 | tf_op jit(solution)/shard_map/all_to_all | solution.py:131
  116.0 0.6 copy.5
  (4 shorter events, 0.1 us)
Async XLA Ops:
  0.0 53.0 %copy-start.1 = (bf16[1,4096,64]{1,2,0:T(8,128)(2,1)S(1)}, bf16[1,4096,64]{1,2,0:T(8,128)(2,1)}, u32[]{:S(2)}) copy-start(bf16[1,4096,64]{1,2,0:T(8,128)(2,1)} %param.4) | copy-start | bytes 1572868
  0.0 50.6 %collective-permute-start = (bf16[64,4096]{1,0:T(8,128)(2,1)}, bf16[64,4096]{1,0:T(8,128)(2,1)S(1)}, u32[]{:S(2)}, u32[]{:S(2)}) collective-permute-start(bf16[64,4096]{1,0:T(8,128)(2,1)} %bitcast.16), channel_id=1, source_target_pairs={{0,2},{2,0},{1,3},{3,1},{4,6},{6,4},{5,7},{7,5},{8,10},{10,8},{9,1... | collective-permute-start | bytes 1572872 | tf_op jit(solution)/shard_map/ppermute | solution.py:100
  5.6 88.5 %collective-permute-start.3 = (bf16[384,4096]{1,0:T(8,128)(2,1)}, bf16[384,4096]{1,0:T(8,128)(2,1)S(1)}, u32[]{:S(2)}, u32[]{:S(2)}) collective-permute-start(bf16[384,4096]{1,0:T(8,128)(2,1)} %bitcast.14), channel_id=1, source_target_pairs={{0,2},{2,0},{1,3},{3,1},{4,6},{6,4},{5,7},{7,5},{8,10},{10,8},{9,1... | collective-permute-start | bytes 9437192 | tf_op jit(solution)/shard_map/ppermute | solution.py:101
  51.0 4.6 %collective-permute-start.1 = (bf16[128,4096]{1,0:T(8,128)(2,1)S(1)}, bf16[128,4096]{1,0:T(8,128)(2,1)S(1)}, u32[]{:S(2)}, u32[]{:S(2)}) collective-permute-start(bf16[128,4096]{1,0:T(8,128)(2,1)S(1)} %multiply_convert_fusion.1.rows), channel_id=1, source_target_pairs={{0,1},{1,0},{2,3},{3,2},{4,5},{5,4},{6,7},{7,6},{8,9},{9,8},{10,11... | collective-permute-start | bytes 3145736 | tf_op jit(solution)/shard_map/ppermute | solution.py:111
  56.2 37.9 %copy-start = (bf16[1,384,4096]{2,1,0:T(8,128)(2,1)S(1)}, bf16[1,384,4096]{2,1,0:T(8,128)(2,1)}, u32[]{:S(2)}) copy-start(bf16[1,384,4096]{2,1,0:T(8,128)(2,1)} %param.5) | copy-start | bytes 9437188
  89.5 4.6 %collective-permute-start.2 = (bf16[16,256,128]{2,1,0:T(8,128)(2,1)S(1)}, bf16[16,256,128]{2,1,0:T(8,128)(2,1)S(1)}, u32[]{:S(2)}, u32[]{:S(2)}) collective-permute-start(bf16[16,256,128]{2,1,0:T(8,128)(2,1)S(1)} %multiply_convert_fusion.own), channel_id=1, source_target_pairs={{0,1},{1,0},{2,3},{3,2},{4,5},{5,4},{6,7},{7,6},{8,9},{9,8},{10,11... | collective-permute-start | bytes 3145736 | tf_op jit(solution)/shard_map/ppermute | solution.py:127

commit v7 on v6

--- a/solution.py
+++ b/solution.py
@@ -125,11 +125,12 @@
     back = jnp.exp2(blocks[:, height : height + 1, :1].astype(jnp.float32) - TOP)
     own = (blocks[:, :height].astype(jnp.float32) * back).astype(jnp.bfloat16)
     other = lax.ppermute(own, "c", SWAP)
-    parts_shape = jax.ShapeDtypeStruct((layers, 2, height // layers, train.shape[0]), jnp.float32)
+    parts_shape = jax.ShapeDtypeStruct((layers, 2, height // layers, train.shape[0]), jnp.bfloat16)
     parts = in_vmem(score_kernel, parts_shape, own, other, train, train_got)
 
     parts = lax.all_to_all(parts.reshape(2 * layers, height // layers, -1), ("layer", "xh"), 0, 0)
-    total = jnp.sum(parts.reshape(layers, 2, -1, 2 * group, parts.shape[-1]), axis=0)
+    parts = parts.reshape(layers, 2, -1, 2 * group, parts.shape[-1])
+    total = jnp.sum(parts.astype(jnp.float32), axis=0)
     return jnp.swapaxes(total, 0, 1).reshape(-1, parts.shape[-1])
 
 

time: 117 us -> 113 us (0.966)
  blocking collectives: 93.3 us -> 88.6 us
    all_to_all x1, blocking collectives: 19.5 us -> 14.7 us  [on_device(): lax.all_to_all(parts.reshape(2 * layers, height // layers, -1), ('layer',...]
where the time goes in v7:
time: 113 us; the launch traced here: 112 us
  blocking collectives  88.6 us (78%)
  starting transfers between devices  11.7 us (10%)
  waiting for transfers between devices  4.42 us (4%)
  Pallas kernels  3.45 us (3%)
  other arithmetic  2.93 us (3%)
    all_gather x2, blocking collectives, gather_z(): return lax.all_gather(x, AXES, axis=0, axis_index_groups=groups)  73.8 us
    all_to_all x1, blocking collectives, on_device(): lax.all_to_all(parts.reshape(2 * layers, height // layers, -1), ('layer',...  14.7 us
    ppermute x1, starting transfers between devices, on_device(): fisher_got = lax.ppermute(mine, 'xh', SWAP)  5.6 us
    pallas_call x3, Pallas kernels, in_vmem(): pl.pallas_call(kernel, out_shape=out_shape, in_specs=[spec] * len(operand...  3.45 us
    ppermute x1, starting transfers between devices, on_device(): other = lax.ppermute(own, 'c', SWAP)  2.29 us
    ppermute x1, waiting for transfers between devices, on_device(): other = lax.ppermute(own, 'c', SWAP)  2.26 us
  transfers between devices with their start and end apart: 4, of which 2 were waited for; matrix products, arithmetic and copies ran while one was open for 3% of the time, Pallas kernels for 1%

profile of v7, /device:TPU:1, one launch (start us, length us, event | category | flops | bytes accessed | tf_op | source)
XLA Modules:
  0.0 111.9 jit_solution(15631008605329499574)
XLA Ops:
  0.0 0.0 copy-start.1
  0.0 5.6 %collective-permute-start = (bf16[64,4096]{1,0:T(8,128)(2,1)}, bf16[64,4096]{1,0:T(8,128)(2,1)S(1)}, u32[]{:S(2)}, u32[]{:S(2)}) collective-permute-start(bf16[64,4096]{1,0:T(8,128)(2,1)} %bitcast.16), channel_id=1, source_target_pairs={{0,2},{2,0},{1,3},{3,1},{4,6},{6,4},{5,7},{7,5},{8,10},{10,8},{9,1... | collective-permute-start | bytes 1572872 | tf_op jit(solution)/shard_map/ppermute | solution.py:100
  5.6 1.9 %collective-permute-start.3 = (bf16[384,4096]{1,0:T(8,128)(2,1)}, bf16[384,4096]{1,0:T(8,128)(2,1)S(1)}, u32[]{:S(2)}, u32[]{:S(2)}) collective-permute-start(bf16[384,4096]{1,0:T(8,128)(2,1)} %bitcast.14), channel_id=1, source_target_pairs={{0,2},{2,0},{1,3},{3,1},{4,6},{6,4},{5,7},{7,5},{8,10},{10,8},{9,1... | collective-permute-start | bytes 9437192 | tf_op jit(solution)/shard_map/ppermute | solution.py:101
  7.5 1.0 fusion
  8.5 0.9 fusion.1
  9.5 0.1 broadcast_in_dim.2
  9.6 41.1 %all-gather.4 = f16[128,4224]{1,0:T(8,128)(2,1)S(1)} all-gather(f16[8,4224]{1,0:T(8,128)(2,1)S(1)} %pad_maximum_fusion), channel_id=2, replica_groups={{0,5,8,13,16,21,24,29,32,37,40,45,48,53,56,61},{1,4,9,12,17,20,25,28,33..., dimensions={0}, use_global_device_ids=true | all-gather | bytes 1148928 | tf_op jit(solution)/shard_map/all_gather | solution.py:21
  50.6 0.0 collective-permute-done.got
  50.6 0.1 exponential_reduce_fusion
  50.8 0.3 multiply_convert_fusion.1.rows
  51.0 1.9 %collective-permute-start.1 = (bf16[128,4096]{1,0:T(8,128)(2,1)S(1)}, bf16[128,4096]{1,0:T(8,128)(2,1)S(1)}, u32[]{:S(2)}, u32[]{:S(2)}) collective-permute-start(bf16[128,4096]{1,0:T(8,128)(2,1)S(1)} %multiply_convert_fusion.1.rows), channel_id=1, source_target_pairs={{0,1},{1,0},{2,3},{3,2},{4,5},{5,4},{6,7},{7,6},{8,9},{9,8},{10,11... | collective-permute-start | bytes 3145736 | tf_op jit(solution)/shard_map/ppermute | solution.py:111
  53.0 0.0 copy-done.1
  53.0 0.5 shard_map.37.near
  53.5 2.1 %collective-permute-done.1.rows = bf16[128,4096]{1,0:T(8,128)(2,1)S(1)} collective-permute-done((bf16[128,4096]{1,0:T(8,128)(2,1)S(1)}, bf16[128,4096]{1,0:T(8,128)(2,1)S(1)}, u32[]{:S(2)}, u32[]{:S(2)}) %collective-permute-start.1) | collective-permute-done | bytes 1048608 | tf_op jit(solution)/shard_map/ppermute | solution.py:111
  55.6 0.6 shard_map.38
  56.2 0.0 copy-start
  56.2 32.7 %all-gather.5 = f16[4224,128]{1,0:T(8,128)(2,1)S(1)} all-gather(f16[264,128]{1,0:T(8,128)(2,1)S(1)} %convert_element_type.47), channel_id=3, replica_groups={{0,5,8,13,16,21,24,29,32,37,40,45,48,53,56,61},{1,4,9,12,17,20,25,28,33..., dimensions={0}, use_global_device_ids=true | all-gather | bytes 1148928 | tf_op jit(solution)/shard_map/all_gather | solution.py:21
  89.0 0.2 fusion.5
  89.2 0.3 multiply_convert_fusion.own
  89.5 2.3 %collective-permute-start.2 = (bf16[16,256,128]{2,1,0:T(8,128)(2,1)S(1)}, bf16[16,256,128]{2,1,0:T(8,128)(2,1)S(1)}, u32[]{:S(2)}, u32[]{:S(2)}) collective-permute-start(bf16[16,256,128]{2,1,0:T(8,128)(2,1)S(1)} %multiply_convert_fusion.own), channel_id=1, source_target_pairs={{0,1},{1,0},{2,3},{3,2},{4,5},{5,4},{6,7},{7,6},{8,9},{9,8},{10,11... | collective-permute-start | bytes 3145736 | tf_op jit(solution)/shard_map/ppermute | solution.py:127
  91.8 2.3 %collective-permute-done.2.other = bf16[16,256,128]{2,1,0:T(8,128)(2,1)S(1)} collective-permute-done((bf16[16,256,128]{2,1,0:T(8,128)(2,1)S(1)}, bf16[16,256,128]{2,1,0:T(8,128)(2,1)S(1)}, u32[]{:S(2)}, u32[]{:S(2)}) %collective-permute-start.2) | collective-permute-done | bytes 1048608 | tf_op jit(solution)/shard_map/ppermute | solution.py:127
  94.1 0.0 collective-permute-done.3.got
  94.1 0.0 copy-done
  94.1 2.4 %shard_map.39 = bf16[8,2,32,384]{3,2,1,0:T(8,128)(2,1)S(1)} custom-call(bf16[16,256,128]{2,1,0:T(8,128)(2,1)S(1)} %multiply_convert_fusion.own, bf16[16,256,128]{2,1,0:T(8,128)(2,1)S(1)} %collective-permute-done.2.other, bf16[384,4096]{1,0:T(8,128)(2,1)S(1)} %bitcast.15, bf16[384,4096]{1,0:T(8,128)(2,1)S(1)} %collective-permute-done.3.got), custom_call_target="tpu_custom_call" | custom-call | flops 16777216 | bytes 1048576 | tf_op jit(solution)/shard_map/pallas_call | solution.py:83
  96.5 14.7 %all_to_all.5 = bf16[16,32,384]{2,1,0:T(8,128)(2,1)S(1)} all-to-all(bf16[16,32,384]{2,1,0:T(8,128)(2,1)S(1)} %bitcast.19), channel_id=1, replica_groups=mesh['layer'=8,'z'=16,'xh'=2,'c'=2] {'layer','xh'}, dimensions={0} | all-to-all | bytes 786432 | tf_op jit(solution)/shard_map/all_to_all | solution.py:131
  111.2 0.1 convert_reduce_fusion
  111.3 0.6 copy.5
  (3 shorter events, 0.1 us)
Async XLA Ops:
  0.0 53.0 %copy-start.1 = (bf16[1,4096,64]{1,2,0:T(8,128)(2,1)S(1)}, bf16[1,4096,64]{1,2,0:T(8,128)(2,1)}, u32[]{:S(2)}) copy-start(bf16[1,4096,64]{1,2,0:T(8,128)(2,1)} %param.4) | copy-start | bytes 1572868
  0.0 50.6 %collective-permute-start = (bf16[64,4096]{1,0:T(8,128)(2,1)}, bf16[64,4096]{1,0:T(8,128)(2,1)S(1)}, u32[]{:S(2)}, u32[]{:S(2)}) collective-permute-start(bf16[64,4096]{1,0:T(8,128)(2,1)} %bitcast.16), channel_id=1, source_target_pairs={{0,2},{2,0},{1,3},{3,1},{4,6},{6,4},{5,7},{7,5},{8,10},{10,8},{9,1... | collective-permute-start | bytes 1572872 | tf_op jit(solution)/shard_map/ppermute | solution.py:100
  5.6 88.5 %collective-permute-start.3 = (bf16[384,4096]{1,0:T(8,128)(2,1)}, bf16[384,4096]{1,0:T(8,128)(2,1)S(1)}, u32[]{:S(2)}, u32[]{:S(2)}) collective-permute-start(bf16[384,4096]{1,0:T(8,128)(2,1)} %bitcast.14), channel_id=1, source_target_pairs={{0,2},{2,0},{1,3},{3,1},{4,6},{6,4},{5,7},{7,5},{8,10},{10,8},{9,1... | collective-permute-start | bytes 9437192 | tf_op jit(solution)/shard_map/ppermute | solution.py:101
  51.0 4.6 %collective-permute-start.1 = (bf16[128,4096]{1,0:T(8,128)(2,1)S(1)}, bf16[128,4096]{1,0:T(8,128)(2,1)S(1)}, u32[]{:S(2)}, u32[]{:S(2)}) collective-permute-start(bf16[128,4096]{1,0:T(8,128)(2,1)S(1)} %multiply_convert_fusion.1.rows), channel_id=1, source_target_pairs={{0,1},{1,0},{2,3},{3,2},{4,5},{5,4},{6,7},{7,6},{8,9},{9,8},{10,11... | collective-permute-start | bytes 3145736 | tf_op jit(solution)/shard_map/ppermute | solution.py:111
  56.2 37.9 %copy-start = (bf16[1,384,4096]{2,1,0:T(8,128)(2,1)S(1)}, bf16[1,384,4096]{2,1,0:T(8,128)(2,1)}, u32[]{:S(2)}) copy-start(bf16[1,384,4096]{2,1,0:T(8,128)(2,1)} %param.5) | copy-start | bytes 9437188
  89.5 4.6 %collective-permute-start.2 = (bf16[16,256,128]{2,1,0:T(8,128)(2,1)S(1)}, bf16[16,256,128]{2,1,0:T(8,128)(2,1)S(1)}, u32[]{:S(2)}, u32[]{:S(2)}) collective-permute-start(bf16[16,256,128]{2,1,0:T(8,128)(2,1)S(1)} %multiply_convert_fusion.own), channel_id=1, source_target_pairs={{0,1},{1,0},{2,3},{3,2},{4,5},{5,4},{6,7},{7,6},{8,9},{9,8},{10,11... | collective-permute-start | bytes 3145736 | tf_op jit(solution)/shard_map/ppermute | solution.py:127

commit v8 on v7

--- a/solution.py
+++ b/solution.py
@@ -33,6 +33,24 @@
 def rounded_product(rows, columns):
     value = lax.dot_general(rows[...], columns, NT, preferred_element_type=jnp.float32)
     return value.astype(jnp.bfloat16).astype(jnp.float32)
+
+
+def scale_kernel(rows, out):
+    value = rows[...].astype(jnp.float32)
+    exponent = exponent_of(jnp.max(jnp.abs(value), axis=1, keepdims=True))
+    out[:, : value.shape[1]] = value * jnp.exp2(TOP - exponent)
+    out[:, value.shape[1] :] = jnp.broadcast_to(exponent, (value.shape[0], 128))
+
+
+def sum_kernel(parts, out):
+    span = out.shape[0] // 4
+    for z in range(2):
+        for chip in range(2):
+            piece = parts[chip, z * span : (z + 1) * span].astype(jnp.float32)
+            for layer in range(1, parts.shape[0] // 2):
+                piece = piece + parts[2 * layer + chip, z * span : (z + 1) * span].astype(jnp.float32)
+            begin = (2 * z + chip) * span
+            out[begin : begin + span] = piece
 
 
 def near_kernel(rows, mine, got, out):
@@ -78,7 +96,7 @@
 
 
 def in_vmem(kernel, out_shape, *operands, scratch=()):
-    flops = 2 * operands[0].size * operands[1].shape[0]
+    flops = 2 * operands[0].size * operands[-1].shape[0]
     spec = pl.BlockSpec(memory_space=pltpu.VMEM)
     return pl.pallas_call(
         kernel,
@@ -100,11 +118,8 @@
     fisher_got = lax.ppermute(mine, "xh", SWAP)
     train_got = lax.ppermute(train, "xh", SWAP)
 
-    wide = queries[0].astype(jnp.float32)
-    exponent = exponent_of(jnp.max(jnp.abs(wide), axis=1, keepdims=True))
-    scaled = (wide * jnp.exp2(TOP - exponent)).astype(jnp.float16)
-    tail = jnp.broadcast_to(exponent, (group, 128)).astype(jnp.float16)
-    rows = gather_z(jnp.concatenate([scaled, tail], axis=1), groups).reshape(slots * group, width + 128)
+    scaled = in_vmem(scale_kernel, jax.ShapeDtypeStruct((group, width + 128), jnp.float32), queries[0])
+    rows = gather_z(scaled.astype(jnp.float16), groups).reshape(slots * group, width + 128)
     rows, fisher_got = lax.optimization_barrier((rows, fisher_got))
     back = jnp.exp2(rows[:, width : width + 1].astype(jnp.float32) - TOP)
     rows = (rows[:, :width].astype(jnp.float32) * back).astype(jnp.bfloat16)
@@ -129,9 +144,7 @@
     parts = in_vmem(score_kernel, parts_shape, own, other, train, train_got)
 
     parts = lax.all_to_all(parts.reshape(2 * layers, height // layers, -1), ("layer", "xh"), 0, 0)
-    parts = parts.reshape(layers, 2, -1, 2 * group, parts.shape[-1])
-    total = jnp.sum(parts.astype(jnp.float32), axis=0)
-    return jnp.swapaxes(total, 0, 1).reshape(-1, parts.shape[-1])
+    return in_vmem(sum_kernel, jax.ShapeDtypeStruct((2 * height // layers, parts.shape[2]), jnp.float32), parts)
 
 
 def solution(mesh):

time: 113 us -> 112 us (level)
  other arithmetic: 2.93 us -> 0.95 us
    pallas_call x3 -> x5, Pallas kernels: 3.45 us -> 4.24 us  [in_vmem(): pl.pallas_call(kernel, out_shape=out_shape, in_specs=[spec] * len(operand...]
  transfers between devices with their start and end apart: 4 -> 4, of which waited for: 2 -> 2; matrix products, arithmetic and copies ran while one was open for 3% -> 1% of each run, Pallas kernels for 1% -> 1%
where the time goes in v8:
time: 112 us; the launch traced here: 111 us
  blocking collectives  88.6 us (79%)
  starting transfers between devices  11.7 us (10%)
  waiting for transfers between devices  4.42 us (4%)
  Pallas kernels  4.24 us (4%)
    all_gather x2, blocking collectives, gather_z(): return lax.all_gather(x, AXES, axis=0, axis_index_groups=groups)  73.8 us
    all_to_all x1, blocking collectives, on_device(): lax.all_to_all(parts.reshape(2 * layers, height // layers, -1), ('layer',...  14.8 us
    ppermute x1, starting transfers between devices, on_device(): fisher_got = lax.ppermute(mine, 'xh', SWAP)  5.6 us
    pallas_call x5, Pallas kernels, in_vmem(): pl.pallas_call(kernel, out_shape=out_shape, in_specs=[spec] * len(operand...  4.24 us
    ppermute x1, starting transfers between devices, on_device(): other = lax.ppermute(own, 'c', SWAP)  2.29 us
    ppermute x1, waiting for transfers between devices, on_device(): other = lax.ppermute(own, 'c', SWAP)  2.26 us
  transfers between devices with their start and end apart: 4, of which 2 were waited for; matrix products, arithmetic and copies ran while one was open for 1% of the time, Pallas kernels for 1%

profile of v8, /device:TPU:1, one launch (start us, length us, event | category | flops | bytes accessed | tf_op | source)
XLA Modules:
  0.0 110.9 jit_solution(2136651512193305943)
XLA Ops:
  0.0 0.0 copy-start.1
  0.0 5.6 %collective-permute-start = (bf16[64,4096]{1,0:T(8,128)(2,1)}, bf16[64,4096]{1,0:T(8,128)(2,1)S(1)}, u32[]{:S(2)}, u32[]{:S(2)}) collective-permute-start(bf16[64,4096]{1,0:T(8,128)(2,1)} %bitcast.9), channel_id=1, source_target_pairs={{0,2},{2,0},{1,3},{3,1},{4,6},{6,4},{5,7},{7,5},{8,10},{10,8},{9,1... | collective-permute-start | bytes 1572872 | tf_op jit(solution)/shard_map/ppermute | solution.py:118
  5.6 1.9 %collective-permute-start.3 = (bf16[384,4096]{1,0:T(8,128)(2,1)}, bf16[384,4096]{1,0:T(8,128)(2,1)S(1)}, u32[]{:S(2)}, u32[]{:S(2)}) collective-permute-start(bf16[384,4096]{1,0:T(8,128)(2,1)} %bitcast.7), channel_id=1, source_target_pairs={{0,2},{2,0},{1,3},{3,1},{4,6},{6,4},{5,7},{7,5},{8,10},{10,8},{9,1... | collective-permute-start | bytes 9437192 | tf_op jit(solution)/shard_map/ppermute | solution.py:119
  7.5 0.0 copy-start.2
  7.6 0.8 copy-done.2
  8.4 0.1 shard_map.37
  8.5 41.1 %all-gather.4 = f16[128,4224]{1,0:T(8,128)(2,1)S(1)} all-gather(f16[8,4224]{1,0:T(8,128)(2,1)S(1)} %convert_element_type.24), channel_id=2, replica_groups={{0,5,8,13,16,21,24,29,32,37,40,45,48,53,56,61},{1,4,9,12,17,20,25,28,33..., dimensions={0}, use_global_device_ids=true | all-gather | bytes 1148928 | tf_op jit(solution)/shard_map/all_gather | solution.py:21
  49.6 0.0 collective-permute-done.got
  49.6 0.1 exponential_reduce_fusion
  49.7 0.3 multiply_convert_fusion.1.rows
  50.0 1.9 %collective-permute-start.1 = (bf16[128,4096]{1,0:T(8,128)(2,1)S(1)}, bf16[128,4096]{1,0:T(8,128)(2,1)S(1)}, u32[]{:S(2)}, u32[]{:S(2)}) collective-permute-start(bf16[128,4096]{1,0:T(8,128)(2,1)S(1)} %multiply_convert_fusion.1.rows), channel_id=1, source_target_pairs={{0,1},{1,0},{2,3},{3,2},{4,5},{5,4},{6,7},{7,6},{8,9},{9,8},{10,11... | collective-permute-start | bytes 3145736 | tf_op jit(solution)/shard_map/ppermute | solution.py:126
  51.9 0.0 copy-done.1
  51.9 0.5 shard_map.38.near
  52.4 2.1 %collective-permute-done.1.rows = bf16[128,4096]{1,0:T(8,128)(2,1)S(1)} collective-permute-done((bf16[128,4096]{1,0:T(8,128)(2,1)S(1)}, bf16[128,4096]{1,0:T(8,128)(2,1)S(1)}, u32[]{:S(2)}, u32[]{:S(2)}) %collective-permute-start.1) | collective-permute-done | bytes 1048608 | tf_op jit(solution)/shard_map/ppermute | solution.py:126
  54.6 0.6 shard_map.39
  55.2 0.0 copy-start
  55.2 32.7 %all-gather.5 = f16[4224,128]{1,0:T(8,128)(2,1)S(1)} all-gather(f16[264,128]{1,0:T(8,128)(2,1)S(1)} %convert_element_type.28), channel_id=3, replica_groups={{0,5,8,13,16,21,24,29,32,37,40,45,48,53,56,61},{1,4,9,12,17,20,25,28,33..., dimensions={0}, use_global_device_ids=true | all-gather | bytes 1148928 | tf_op jit(solution)/shard_map/all_gather | solution.py:21
  87.9 0.2 fusion.3
  88.1 0.3 multiply_convert_fusion.own
  88.5 2.3 %collective-permute-start.2 = (bf16[16,256,128]{2,1,0:T(8,128)(2,1)S(1)}, bf16[16,256,128]{2,1,0:T(8,128)(2,1)S(1)}, u32[]{:S(2)}, u32[]{:S(2)}) collective-permute-start(bf16[16,256,128]{2,1,0:T(8,128)(2,1)S(1)} %multiply_convert_fusion.own), channel_id=1, source_target_pairs={{0,1},{1,0},{2,3},{3,2},{4,5},{5,4},{6,7},{7,6},{8,9},{9,8},{10,11... | collective-permute-start | bytes 3145736 | tf_op jit(solution)/shard_map/ppermute | solution.py:142
  90.8 2.3 %collective-permute-done.2.other = bf16[16,256,128]{2,1,0:T(8,128)(2,1)S(1)} collective-permute-done((bf16[16,256,128]{2,1,0:T(8,128)(2,1)S(1)}, bf16[16,256,128]{2,1,0:T(8,128)(2,1)S(1)}, u32[]{:S(2)}, u32[]{:S(2)}) %collective-permute-start.2) | collective-permute-done | bytes 1048608 | tf_op jit(solution)/shard_map/ppermute | solution.py:142
  93.0 0.0 collective-permute-done.3.got
  93.0 0.0 copy-done
  93.0 2.4 %shard_map.40 = bf16[8,2,32,384]{3,2,1,0:T(8,128)(2,1)S(1)} custom-call(bf16[16,256,128]{2,1,0:T(8,128)(2,1)S(1)} %multiply_convert_fusion.own, bf16[16,256,128]{2,1,0:T(8,128)(2,1)S(1)} %collective-permute-done.2.other, bf16[384,4096]{1,0:T(8,128)(2,1)S(1)} %bitcast.8, bf16[384,4096]{1,0:T(8,128)(2,1)S(1)} %collective-permute-done.3.got), custom_call_target="tpu_custom_call" | custom-call | flops 402653184 | bytes 1048576 | tf_op jit(solution)/shard_map/pallas_call | solution.py:101
  95.4 14.8 %all_to_all.5.parts = bf16[16,32,384]{2,1,0:T(8,128)(2,1)S(1)} all-to-all(bf16[16,32,384]{2,1,0:T(8,128)(2,1)S(1)} %bitcast.12), channel_id=1, replica_groups=mesh['layer'=8,'z'=16,'xh'=2,'c'=2] {'layer','xh'}, dimensions={0} | all-to-all | bytes 786432 | tf_op jit(solution)/shard_map/all_to_all | solution.py:146
  110.2 0.7 shard_map.41
  (2 shorter events, 0.0 us)
Async XLA Ops:
  0.0 51.9 %copy-start.1 = (bf16[1,4096,64]{1,2,0:T(8,128)(2,1)S(1)}, bf16[1,4096,64]{1,2,0:T(8,128)(2,1)}, u32[]{:S(2)}) copy-start(bf16[1,4096,64]{1,2,0:T(8,128)(2,1)} %param.4) | copy-start | bytes 1572868
  0.0 49.6 %collective-permute-start = (bf16[64,4096]{1,0:T(8,128)(2,1)}, bf16[64,4096]{1,0:T(8,128)(2,1)S(1)}, u32[]{:S(2)}, u32[]{:S(2)}) collective-permute-start(bf16[64,4096]{1,0:T(8,128)(2,1)} %bitcast.9), channel_id=1, source_target_pairs={{0,2},{2,0},{1,3},{3,1},{4,6},{6,4},{5,7},{7,5},{8,10},{10,8},{9,1... | collective-permute-start | bytes 1572872 | tf_op jit(solution)/shard_map/ppermute | solution.py:118
  5.6 87.4 %collective-permute-start.3 = (bf16[384,4096]{1,0:T(8,128)(2,1)}, bf16[384,4096]{1,0:T(8,128)(2,1)S(1)}, u32[]{:S(2)}, u32[]{:S(2)}) collective-permute-start(bf16[384,4096]{1,0:T(8,128)(2,1)} %bitcast.7), channel_id=1, source_target_pairs={{0,2},{2,0},{1,3},{3,1},{4,6},{6,4},{5,7},{7,5},{8,10},{10,8},{9,1... | collective-permute-start | bytes 9437192 | tf_op jit(solution)/shard_map/ppermute | solution.py:119
  7.5 0.8 copy-start.2
  50.0 4.6 %collective-permute-start.1 = (bf16[128,4096]{1,0:T(8,128)(2,1)S(1)}, bf16[128,4096]{1,0:T(8,128)(2,1)S(1)}, u32[]{:S(2)}, u32[]{:S(2)}) collective-permute-start(bf16[128,4096]{1,0:T(8,128)(2,1)S(1)} %multiply_convert_fusion.1.rows), channel_id=1, source_target_pairs={{0,1},{1,0},{2,3},{3,2},{4,5},{5,4},{6,7},{7,6},{8,9},{9,8},{10,11... | collective-permute-start | bytes 3145736 | tf_op jit(solution)/shard_map/ppermute | solution.py:126
  55.2 37.9 %copy-start = (bf16[1,384,4096]{2,1,0:T(8,128)(2,1)S(1)}, bf16[1,384,4096]{2,1,0:T(8,128)(2,1)}, u32[]{:S(2)}) copy-start(bf16[1,384,4096]{2,1,0:T(8,128)(2,1)} %param.5) | copy-start | bytes 9437188
  88.5 4.6 %collective-permute-start.2 = (bf16[16,256,128]{2,1,0:T(8,128)(2,1)S(1)}, bf16[16,256,128]{2,1,0:T(8,128)(2,1)S(1)}, u32[]{:S(2)}, u32[]{:S(2)}) collective-permute-start(bf16[16,256,128]{2,1,0:T(8,128)(2,1)S(1)} %multiply_convert_fusion.own), channel_id=1, source_target_pairs={{0,1},{1,0},{2,3},{3,2},{4,5},{5,4},{6,7},{7,6},{8,9},{9,8},{10,11... | collective-permute-start | bytes 3145736 | tf_op jit(solution)/shard_map/ppermute | solution.py:142

commit v9 on v8

--- a/solution.py
+++ b/solution.py
@@ -74,25 +74,32 @@
     out[...] = jnp.concatenate([value * jnp.exp2(TOP - exponent), tail], axis=0)
 
 
-def score_kernel(own, other, train, got, out):
-    side, chip = side_of(), lax.axis_index("xh")
-    layers, _, rows, count = out.shape
+def scores(own, other, train):
+    side = side_of()
     half = own.shape[2] // 2
-    here = jnp.zeros((own.shape[1], count), jnp.float32)
-    there = here
+    total = jnp.zeros((own.shape[1], train.shape[0]), jnp.float32)
     for z in range(own.shape[0]):
         mixed = lax.rem(side + z, 2) == 0
         one = jnp.where(mixed, own[z], other[z])
         two = jnp.where(mixed, other[z], own[z])
         left = jnp.concatenate([one[:, :half], two[:, :half], one[:, half:], two[:, half:]], axis=1)
-        span = left.shape[1]
-        right = train[:, z * span : (z + 1) * span]
-        here = here + lax.dot_general(left, right, NT, preferred_element_type=jnp.float32)
-        right = got[:, z * span : (z + 1) * span]
-        there = there + lax.dot_general(left, right, NT, preferred_element_type=jnp.float32)
+        right = train[:, z * left.shape[1] : (z + 1) * left.shape[1]]
+        total = total + lax.dot_general(left, right, NT, preferred_element_type=jnp.float32)
+    return total
+
+
+def here_kernel(own, other, train, out):
+    out[...] = scores(own, other, train).astype(out.dtype)
+
+
+def there_kernel(own, other, here, train, out):
+    chip = lax.axis_index("xh")
+    layers, _, rows, _ = out.shape
+    there = scores(own, other, train).astype(out.dtype)
     for layer in range(layers):
-        out[layer, chip] = here[layer * rows : (layer + 1) * rows].astype(out.dtype)
-        out[layer, 1 - chip] = there[layer * rows : (layer + 1) * rows].astype(out.dtype)
+        piece = slice(layer * rows, (layer + 1) * rows)
+        out[layer, chip] = here[piece]
+        out[layer, 1 - chip] = there[piece]
 
 
 def in_vmem(kernel, out_shape, *operands, scratch=()):
@@ -140,8 +147,9 @@
     back = jnp.exp2(blocks[:, height : height + 1, :1].astype(jnp.float32) - TOP)
     own = (blocks[:, :height].astype(jnp.float32) * back).astype(jnp.bfloat16)
     other = lax.ppermute(own, "c", SWAP)
+    here = in_vmem(here_kernel, jax.ShapeDtypeStruct((height, train.shape[0]), jnp.bfloat16), own, other, train)
     parts_shape = jax.ShapeDtypeStruct((layers, 2, height // layers, train.shape[0]), jnp.bfloat16)
-    parts = in_vmem(score_kernel, parts_shape, own, other, train, train_got)
+    parts = in_vmem(there_kernel, parts_shape, own, other, here, train_got)
 
     parts = lax.all_to_all(parts.reshape(2 * layers, height // layers, -1), ("layer", "xh"), 0, 0)
     return in_vmem(sum_kernel, jax.ShapeDtypeStruct((2 * height // layers, parts.shape[2]), jnp.float32), parts)

time: 112 us -> 112 us (level)
    pallas_call x5 -> x6, Pallas kernels: 4.24 us -> 4.47 us  [in_vmem(): pl.pallas_call(kernel, out_shape=out_shape, in_specs=[spec] * len(operand...]
  transfers between devices with their start and end apart: 4 -> 4, of which waited for: 2 -> 2; matrix products, arithmetic and copies ran while one was open for 1% -> 1% of each run, Pallas kernels for 1% -> 2%
where the time goes in v9:
time: 112 us; the launch traced here: 111 us
  blocking collectives  88.6 us (79%)
  starting transfers between devices  11.7 us (10%)
  Pallas kernels  4.47 us (4%)
  waiting for transfers between devices  4.42 us (4%)
    all_gather x2, blocking collectives, gather_z(): return lax.all_gather(x, AXES, axis=0, axis_index_groups=groups)  73.8 us
    all_to_all x1, blocking collectives, on_device(): lax.all_to_all(parts.reshape(2 * layers, height // layers, -1), ('layer',...  14.8 us
    ppermute x1, starting transfers between devices, on_device(): fisher_got = lax.ppermute(mine, 'xh', SWAP)  5.6 us
    pallas_call x6, Pallas kernels, in_vmem(): pl.pallas_call(kernel, out_shape=out_shape, in_specs=[spec] * len(operand...  4.47 us
    ppermute x1, starting transfers between devices, on_device(): other = lax.ppermute(own, 'c', SWAP)  2.29 us
    ppermute x1, waiting for transfers between devices, on_device(): other = lax.ppermute(own, 'c', SWAP)  2.26 us
  transfers between devices with their start and end apart: 4, of which 2 were waited for; matrix products, arithmetic and copies ran while one was open for 1% of the time, Pallas kernels for 2%

profile of v9, /device:TPU:1, one launch (start us, length us, event | category | flops | bytes accessed | tf_op | source)
XLA Modules:
  0.0 111.1 jit_solution(10614316459069827796)
XLA Ops:
  0.0 0.0 copy-start.1
  0.0 5.6 %collective-permute-start = (bf16[64,4096]{1,0:T(8,128)(2,1)}, bf16[64,4096]{1,0:T(8,128)(2,1)S(1)}, u32[]{:S(2)}, u32[]{:S(2)}) collective-permute-start(bf16[64,4096]{1,0:T(8,128)(2,1)} %bitcast.9), channel_id=1, source_target_pairs={{0,2},{2,0},{1,3},{3,1},{4,6},{6,4},{5,7},{7,5},{8,10},{10,8},{9,1... | collective-permute-start | bytes 1572872 | tf_op jit(solution)/shard_map/ppermute | solution.py:125
  5.6 1.9 %collective-permute-start.3 = (bf16[384,4096]{1,0:T(8,128)(2,1)}, bf16[384,4096]{1,0:T(8,128)(2,1)S(1)}, u32[]{:S(2)}, u32[]{:S(2)}) collective-permute-start(bf16[384,4096]{1,0:T(8,128)(2,1)} %bitcast.7), channel_id=1, source_target_pairs={{0,2},{2,0},{1,3},{3,1},{4,6},{6,4},{5,7},{7,5},{8,10},{10,8},{9,1... | collective-permute-start | bytes 9437192 | tf_op jit(solution)/shard_map/ppermute | solution.py:126
  7.5 0.0 copy-start.2
  7.6 0.8 copy-done.2
  8.4 0.1 shard_map.37
  8.5 41.1 %all-gather.4 = f16[128,4224]{1,0:T(8,128)(2,1)S(1)} all-gather(f16[8,4224]{1,0:T(8,128)(2,1)S(1)} %convert_element_type.24), channel_id=2, replica_groups={{0,5,8,13,16,21,24,29,32,37,40,45,48,53,56,61},{1,4,9,12,17,20,25,28,33..., dimensions={0}, use_global_device_ids=true | all-gather | bytes 1148928 | tf_op jit(solution)/shard_map/all_gather | solution.py:21
  49.6 0.0 collective-permute-done.got
  49.6 0.1 exponential_reduce_fusion
  49.7 0.3 multiply_convert_fusion.1.rows
  50.0 1.9 %collective-permute-start.1 = (bf16[128,4096]{1,0:T(8,128)(2,1)S(1)}, bf16[128,4096]{1,0:T(8,128)(2,1)S(1)}, u32[]{:S(2)}, u32[]{:S(2)}) collective-permute-start(bf16[128,4096]{1,0:T(8,128)(2,1)S(1)} %multiply_convert_fusion.1.rows), channel_id=1, source_target_pairs={{0,1},{1,0},{2,3},{3,2},{4,5},{5,4},{6,7},{7,6},{8,9},{9,8},{10,11... | collective-permute-start | bytes 3145736 | tf_op jit(solution)/shard_map/ppermute | solution.py:133
  51.9 0.0 copy-done.1
  51.9 0.5 shard_map.38.near
  52.4 2.1 %collective-permute-done.1.rows = bf16[128,4096]{1,0:T(8,128)(2,1)S(1)} collective-permute-done((bf16[128,4096]{1,0:T(8,128)(2,1)S(1)}, bf16[128,4096]{1,0:T(8,128)(2,1)S(1)}, u32[]{:S(2)}, u32[]{:S(2)}) %collective-permute-start.1) | collective-permute-done | bytes 1048608 | tf_op jit(solution)/shard_map/ppermute | solution.py:133
  54.6 0.6 shard_map.39
  55.2 0.0 copy-start
  55.2 32.7 %all-gather.5 = f16[4224,128]{1,0:T(8,128)(2,1)S(1)} all-gather(f16[264,128]{1,0:T(8,128)(2,1)S(1)} %convert_element_type.28), channel_id=3, replica_groups={{0,5,8,13,16,21,24,29,32,37,40,45,48,53,56,61},{1,4,9,12,17,20,25,28,33..., dimensions={0}, use_global_device_ids=true | all-gather | bytes 1148928 | tf_op jit(solution)/shard_map/all_gather | solution.py:21
  87.9 0.2 fusion.3
  88.1 0.3 multiply_convert_fusion.own
  88.5 2.3 %collective-permute-start.2 = (bf16[16,256,128]{2,1,0:T(8,128)(2,1)S(1)}, bf16[16,256,128]{2,1,0:T(8,128)(2,1)S(1)}, u32[]{:S(2)}, u32[]{:S(2)}) collective-permute-start(bf16[16,256,128]{2,1,0:T(8,128)(2,1)S(1)} %multiply_convert_fusion.own), channel_id=1, source_target_pairs={{0,1},{1,0},{2,3},{3,2},{4,5},{5,4},{6,7},{7,6},{8,9},{9,8},{10,11... | collective-permute-start | bytes 3145736 | tf_op jit(solution)/shard_map/ppermute | solution.py:149
  90.8 2.3 %collective-permute-done.2.other = bf16[16,256,128]{2,1,0:T(8,128)(2,1)S(1)} collective-permute-done((bf16[16,256,128]{2,1,0:T(8,128)(2,1)S(1)}, bf16[16,256,128]{2,1,0:T(8,128)(2,1)S(1)}, u32[]{:S(2)}, u32[]{:S(2)}) %collective-permute-start.2) | collective-permute-done | bytes 1048608 | tf_op jit(solution)/shard_map/ppermute | solution.py:149
  93.0 0.0 copy-done
  93.0 1.3 %shard_map.40.here = bf16[256,384]{1,0:T(8,128)(2,1)S(1)} custom-call(bf16[16,256,128]{2,1,0:T(8,128)(2,1)S(1)} %multiply_convert_fusion.own, bf16[16,256,128]{2,1,0:T(8,128)(2,1)S(1)} %collective-permute-done.2.other, bf16[384,4096]{1,0:T(8,128)(2,1)S(1)} %bitcast.8), custom_call_target="tpu_custom_call" | custom-call | flops 402653184 | bytes 1048576 | tf_op jit(solution)/shard_map/pallas_call | solution.py:108
  94.4 0.0 collective-permute-done.3.train
  94.4 1.3 %shard_map.41 = bf16[8,2,32,384]{3,2,1,0:T(8,128)(2,1)S(1)} custom-call(bf16[16,256,128]{2,1,0:T(8,128)(2,1)S(1)} %multiply_convert_fusion.own, bf16[16,256,128]{2,1,0:T(8,128)(2,1)S(1)} %collective-permute-done.2.other, bf16[256,384]{1,0:T(8,128)(2,1)S(1)} %shard_map.40.here, bf16[384,4096]{1,0:T(8,128)(2,1)S(1)} %collective-permute-done.3.train), custom_call_target="tpu_custom_call" | custom-call | flops 402653184 | bytes 1048576 | tf_op jit(solution)/shard_map/pallas_call | solution.py:108
  95.7 14.8 %all_to_all.5.parts = bf16[16,32,384]{2,1,0:T(8,128)(2,1)S(1)} all-to-all(bf16[16,32,384]{2,1,0:T(8,128)(2,1)S(1)} %bitcast.12), channel_id=1, replica_groups=mesh['layer'=8,'z'=16,'xh'=2,'c'=2] {'layer','xh'}, dimensions={0} | all-to-all | bytes 786432 | tf_op jit(solution)/shard_map/all_to_all | solution.py:154
  110.4 0.7 shard_map.42
  (2 shorter events, 0.0 us)
Async XLA Ops:
  0.0 51.9 %copy-start.1 = (bf16[1,4096,64]{1,2,0:T(8,128)(2,1)S(1)}, bf16[1,4096,64]{1,2,0:T(8,128)(2,1)}, u32[]{:S(2)}) copy-start(bf16[1,4096,64]{1,2,0:T(8,128)(2,1)} %param.4) | copy-start | bytes 1572868
  0.0 49.6 %collective-permute-start = (bf16[64,4096]{1,0:T(8,128)(2,1)}, bf16[64,4096]{1,0:T(8,128)(2,1)S(1)}, u32[]{:S(2)}, u32[]{:S(2)}) collective-permute-start(bf16[64,4096]{1,0:T(8,128)(2,1)} %bitcast.9), channel_id=1, source_target_pairs={{0,2},{2,0},{1,3},{3,1},{4,6},{6,4},{5,7},{7,5},{8,10},{10,8},{9,1... | collective-permute-start | bytes 1572872 | tf_op jit(solution)/shard_map/ppermute | solution.py:125
  5.6 88.8 %collective-permute-start.3 = (bf16[384,4096]{1,0:T(8,128)(2,1)}, bf16[384,4096]{1,0:T(8,128)(2,1)S(1)}, u32[]{:S(2)}, u32[]{:S(2)}) collective-permute-start(bf16[384,4096]{1,0:T(8,128)(2,1)} %bitcast.7), channel_id=1, source_target_pairs={{0,2},{2,0},{1,3},{3,1},{4,6},{6,4},{5,7},{7,5},{8,10},{10,8},{9,1... | collective-permute-start | bytes 9437192 | tf_op jit(solution)/shard_map/ppermute | solution.py:126
  7.5 0.8 copy-start.2
  50.0 4.6 %collective-permute-start.1 = (bf16[128,4096]{1,0:T(8,128)(2,1)S(1)}, bf16[128,4096]{1,0:T(8,128)(2,1)S(1)}, u32[]{:S(2)}, u32[]{:S(2)}) collective-permute-start(bf16[128,4096]{1,0:T(8,128)(2,1)S(1)} %multiply_convert_fusion.1.rows), channel_id=1, source_target_pairs={{0,1},{1,0},{2,3},{3,2},{4,5},{5,4},{6,7},{7,6},{8,9},{9,8},{10,11... | collective-permute-start | bytes 3145736 | tf_op jit(solution)/shard_map/ppermute | solution.py:133
  55.2 37.9 %copy-start = (bf16[1,384,4096]{2,1,0:T(8,128)(2,1)S(1)}, bf16[1,384,4096]{2,1,0:T(8,128)(2,1)}, u32[]{:S(2)}) copy-start(bf16[1,384,4096]{2,1,0:T(8,128)(2,1)} %param.5) | copy-start | bytes 9437188
  88.5 4.6 %collective-permute-start.2 = (bf16[16,256,128]{2,1,0:T(8,128)(2,1)S(1)}, bf16[16,256,128]{2,1,0:T(8,128)(2,1)S(1)}, u32[]{:S(2)}, u32[]{:S(2)}) collective-permute-start(bf16[16,256,128]{2,1,0:T(8,128)(2,1)S(1)} %multiply_convert_fusion.own), channel_id=1, source_target_pairs={{0,1},{1,0},{2,3},{3,2},{4,5},{5,4},{6,7},{7,6},{8,9},{9,8},{10,11... | collective-permute-start | bytes 3145736 | tf_op jit(solution)/shard_map/ppermute | solution.py:149

commit v10 on v9

--- a/solution.py
+++ b/solution.py
@@ -21,8 +21,8 @@
     return lax.all_gather(x, AXES, axis=0, axis_index_groups=groups)
 
 
-def side_of():
-    return lax.rem(lax.axis_index("c") + lax.axis_index("z"), 2)
+def core_at(entry, z):
+    return lax.rem(entry + lax.axis_index("z") + z, 2)
 
 
 def columns_of(mine, got):
@@ -53,20 +53,38 @@
             out[begin : begin + span] = piece
 
 
+def scale_kernel(rows, out):
+    value = rows[...].astype(jnp.float32)
+    exponent = exponent_of(jnp.max(jnp.abs(value), axis=1, keepdims=True))
+    out[:, : value.shape[1]] = value * jnp.exp2(TOP - exponent)
+    out[:, value.shape[1] :] = jnp.broadcast_to(exponent, (value.shape[0], 128))
+
+
+def sum_kernel(parts, out):
+    span = out.shape[0] // 4
+    for z in range(2):
+        for chip in range(2):
+            piece = parts[chip, z * span : (z + 1) * span].astype(jnp.float32)
+            for layer in range(1, parts.shape[0] // 2):
+                piece = piece + parts[2 * layer + chip, z * span : (z + 1) * span].astype(jnp.float32)
+            begin = (2 * z + chip) * span
+            out[begin : begin + span] = piece
+
+
 def near_kernel(rows, mine, got, out):
     out[...] = rounded_product(rows, columns_of(mine, got))
 
 
-def chunk_kernel(near, rows, mine, got, out, order):
-    side = side_of()
-    far = rounded_product(rows, columns_of(mine, got))
+def chunk_kernel(rows, mine, got, out, order):
+    product = rounded_product(rows, columns_of(mine, got))
     height = order.shape[0]
     group = out.shape[0] - height
-    for z in range(height // (2 * group)):
-        first = lax.rem(side + z, 2)
-        piece = slice(z * group, (z + 1) * group)
-        order[pl.ds(pl.multiple_of((2 * z + first) * group, group), group)] = near[piece]
-        order[pl.ds(pl.multiple_of((2 * z + 1 - first) * group, group), group)] = far[piece]
+    slots = height // (2 * group)
+    for entry in range(2):
+        for z in range(slots):
+            begin = (entry * slots + z) * group
+            place = pl.multiple_of((2 * z + core_at(entry, z)) * group, group)
+            order[pl.ds(place, group)] = product[begin : begin + group]
     value = order[...]
     peak = jnp.max(jnp.max(jnp.abs(value), axis=0, keepdims=True), axis=1, keepdims=True)
     exponent = exponent_of(peak)
@@ -74,28 +92,27 @@
     out[...] = jnp.concatenate([value * jnp.exp2(TOP - exponent), tail], axis=0)
 
 
-def scores(own, other, train):
-    side = side_of()
-    half = own.shape[2] // 2
-    total = jnp.zeros((own.shape[1], train.shape[0]), jnp.float32)
-    for z in range(own.shape[0]):
-        mixed = lax.rem(side + z, 2) == 0
-        one = jnp.where(mixed, own[z], other[z])
-        two = jnp.where(mixed, other[z], own[z])
+def scores(blocks, train):
+    half = blocks.shape[3] // 2
+    total = jnp.zeros((blocks.shape[2], train.shape[0]), jnp.float32)
+    for z in range(blocks.shape[1]):
+        straight = core_at(0, z) == 0
+        one = jnp.where(straight, blocks[0, z], blocks[1, z])
+        two = jnp.where(straight, blocks[1, z], blocks[0, z])
         left = jnp.concatenate([one[:, :half], two[:, :half], one[:, half:], two[:, half:]], axis=1)
         right = train[:, z * left.shape[1] : (z + 1) * left.shape[1]]
         total = total + lax.dot_general(left, right, NT, preferred_element_type=jnp.float32)
     return total
 
 
-def here_kernel(own, other, train, out):
-    out[...] = scores(own, other, train).astype(out.dtype)
+def here_kernel(blocks, train, out):
+    out[...] = scores(blocks, train).astype(out.dtype)
 
 
-def there_kernel(own, other, here, train, out):
+def there_kernel(blocks, here, train, out):
     chip = lax.axis_index("xh")
     layers, _, rows, _ = out.shape
-    there = scores(own, other, train).astype(out.dtype)
+    there = scores(blocks, train).astype(out.dtype)
     for layer in range(layers):
         piece = slice(layer * rows, (layer + 1) * rows)
         out[layer, chip] = here[piece]
@@ -127,29 +144,26 @@
 
     scaled = in_vmem(scale_kernel, jax.ShapeDtypeStruct((group, width + 128), jnp.float32), queries[0])
     rows = gather_z(scaled.astype(jnp.float16), groups).reshape(slots * group, width + 128)
+    rows = lax.all_gather(rows, "c", axis=0, tiled=True)
     rows, fisher_got = lax.optimization_barrier((rows, fisher_got))
     back = jnp.exp2(rows[:, width : width + 1].astype(jnp.float32) - TOP)
     rows = (rows[:, :width].astype(jnp.float32) * back).astype(jnp.bfloat16)
-    rows_got = lax.ppermute(rows, "c", SWAP)
 
     height, span = slots * 2 * group, 2 * mine.shape[0]
-    near = in_vmem(near_kernel, jax.ShapeDtypeStruct((height // 2, span), jnp.float32), rows, mine, fisher_got)
     chunk = in_vmem(
         chunk_kernel,
         jax.ShapeDtypeStruct((height + group, span), jnp.float32),
-        near,
-        rows_got,
+        rows,
         mine,
         fisher_got,
         scratch=[pltpu.VMEM((height, span), jnp.float32)],
     )
-    blocks = gather_z(chunk.astype(jnp.float16), groups)
-    back = jnp.exp2(blocks[:, height : height + 1, :1].astype(jnp.float32) - TOP)
-    own = (blocks[:, :height].astype(jnp.float32) * back).astype(jnp.bfloat16)
-    other = lax.ppermute(own, "c", SWAP)
-    here = in_vmem(here_kernel, jax.ShapeDtypeStruct((height, train.shape[0]), jnp.bfloat16), own, other, train)
+    blocks = lax.all_gather(gather_z(chunk.astype(jnp.float16), groups), "c", axis=0)
+    back = jnp.exp2(blocks[:, :, height : height + 1, :1].astype(jnp.float32) - TOP)
+    blocks = (blocks[:, :, :height].astype(jnp.float32) * back).astype(jnp.bfloat16)
+    here = in_vmem(here_kernel, jax.ShapeDtypeStruct((height, train.shape[0]), jnp.bfloat16), blocks, train)
     parts_shape = jax.ShapeDtypeStruct((layers, 2, height // layers, train.shape[0]), jnp.bfloat16)
-    parts = in_vmem(there_kernel, parts_shape, own, other, here, train_got)
+    parts = in_vmem(there_kernel, parts_shape, blocks, here, train_got)
 
     parts = lax.all_to_all(parts.reshape(2 * layers, height // layers, -1), ("layer", "xh"), 0, 0)
     return in_vmem(sum_kernel, jax.ShapeDtypeStruct((2 * height // layers, parts.shape[2]), jnp.float32), parts)

time: 112 us -> 112 us (level)
  blocking collectives: 88.6 us -> 95.1 us
  waiting for transfers between devices: 4.42 us -> 0.01 us
  starting transfers between devices: 11.7 us -> 7.39 us
  local copies, waits for them, and re-layouts: 0.84 us -> 2.26 us
    all_gather x0 -> x2, blocking collectives: none -> 6.7 us  [the longest x1 3.36 us: on_device(): lax.all_gather(gather_z(chunk.astype(jnp.float16), groups), 'c', axis=0)]
    ppermute x2 -> x0, waiting for transfers between devices: 4.41 us -> none  [the longest x1 2.26 us: on_device(): other = lax.ppermute(own, 'c', SWAP)]
    ppermute x2 -> x0, starting transfers between devices: 4.21 us -> none  [the longest x1 2.29 us: on_device(): other = lax.ppermute(own, 'c', SWAP)]
    unnamed x6, local copies, waits for them, and re-layouts: 0.84 us -> 2.26 us
    pallas_call x6 -> x5, Pallas kernels: 4.47 us -> 4.25 us  [in_vmem(): pl.pallas_call(kernel, out_shape=out_shape, in_specs=[spec] * len(operand...]
  transfers between devices with their start and end apart: 4 -> 2, of which waited for: 2 -> 0; matrix products, arithmetic and copies ran while one was open for 1% -> 1% of each run, Pallas kernels for 2% -> 2%
where the time goes in v10:
time: 112 us; the launch traced here: 111 us
  blocking collectives  95.1 us (85%)
  starting transfers between devices  7.39 us (7%)
  Pallas kernels  4.25 us (4%)
  local copies, waits for them, and re-layouts  2.26 us (2%)
  other arithmetic  1.5 us (1%)
    all_gather x2, blocking collectives, gather_z(): return lax.all_gather(x, AXES, axis=0, axis_index_groups=groups)  73.7 us
    all_to_all x1, blocking collectives, on_device(): lax.all_to_all(parts.reshape(2 * layers, height // layers, -1), ('layer',...  14.7 us
    ppermute x1, starting transfers between devices, on_device(): fisher_got = lax.ppermute(mine, 'xh', SWAP)  5.47 us
    pallas_call x5, Pallas kernels, in_vmem(): pl.pallas_call(kernel, out_shape=out_shape, in_specs=[spec] * len(operand...  4.25 us
    all_gather x1, blocking collectives, on_device(): lax.all_gather(gather_z(chunk.astype(jnp.float16), groups), 'c', axis=0)  3.36 us
    all_gather x1, blocking collectives, on_device(): rows = lax.all_gather(rows, 'c', axis=0, tiled=True)  3.34 us
    unnamed x6, local copies, waits for them, and re-layouts  2.26 us
  transfers between devices with their start and end apart: 2, of which 0 were waited for; matrix products, arithmetic and copies ran while one was open for 1% of the time, Pallas kernels for 2%

profile of v10, /device:TPU:1, one launch (start us, length us, event | category | flops | bytes accessed | tf_op | source)
XLA Modules:
  0.0 110.7 jit_solution(17076144666045221102)
XLA Ops:
  0.0 5.5 %collective-permute-start = (bf16[64,4096]{1,0:T(8,128)(2,1)}, bf16[64,4096]{1,0:T(8,128)(2,1)S(1)}, u32[]{:S(2)}, u32[]{:S(2)}) collective-permute-start(bf16[64,4096]{1,0:T(8,128)(2,1)} %bitcast.11), channel_id=1, source_target_pairs={{0,2},{2,0},{1,3},{3,1},{4,6},{6,4},{5,7},{7,5},{8,10},{10,8},{9,1... | collective-permute-start | bytes 1572872 | tf_op jit(solution)/shard_map/ppermute | solution.py:142
  5.5 1.9 %collective-permute-start.1 = (bf16[384,4096]{1,0:T(8,128)(2,1)}, bf16[384,4096]{1,0:T(8,128)(2,1)S(1)}, u32[]{:S(2)}, u32[]{:S(2)}) collective-permute-start(bf16[384,4096]{1,0:T(8,128)(2,1)} %bitcast.8), channel_id=1, source_target_pairs={{0,2},{2,0},{1,3},{3,1},{4,6},{6,4},{5,7},{7,5},{8,10},{10,8},{9,1... | collective-permute-start | bytes 9437192 | tf_op jit(solution)/shard_map/ppermute | solution.py:143
  7.4 0.0 copy-start.2
  7.4 0.8 copy-done.2
  8.3 0.1 shard_map.37
  8.4 41.1 %all-gather.7 = f16[128,4224]{1,0:T(8,128)(2,1)S(1)} all-gather(f16[8,4224]{1,0:T(8,128)(2,1)S(1)} %convert_element_type.24), channel_id=2, replica_groups={{0,5,8,13,16,21,24,29,32,37,40,45,48,53,56,61},{1,4,9,12,17,20,25,28,33..., dimensions={0}, use_global_device_ids=true | all-gather | bytes 1148928 | tf_op jit(solution)/shard_map/all_gather | solution.py:21
  49.5 3.3 %all-gather.8 = f16[256,4224]{1,0:T(8,128)(2,1)S(1)} all-gather(f16[128,4224]{1,0:T(8,128)(2,1)S(1)} %all-gather.7), channel_id=1, replica_groups=mesh['layer'=8,'z'=16,'xh'=2,'c'=2] {'c'}, dimensions={0}, use_global_device_ids=true | all-gather | bytes 3244032 | tf_op jit(solution)/shard_map/all_gather | solution.py:147
  52.8 0.0 copy-start.1
  52.8 0.0 collective-permute-done.got
  52.8 0.1 exponential_reduce_fusion
  52.9 0.5 multiply_convert_fusion.1.rows
  53.5 0.4 copy-done.1
  53.8 0.8 shard_map.38
  54.7 32.6 %all-gather.9 = f16[4224,128]{1,0:T(8,128)(2,1)S(1)} all-gather(f16[264,128]{1,0:T(8,128)(2,1)S(1)} %convert_element_type.28), channel_id=3, replica_groups={{0,5,8,13,16,21,24,29,32,37,40,45,48,53,56,61},{1,4,9,12,17,20,25,28,33..., dimensions={0}, use_global_device_ids=true | all-gather | bytes 1148928 | tf_op jit(solution)/shard_map/all_gather | solution.py:21
  87.3 3.4 %all-gather.10 = f16[32,264,128]{2,1,0:T(8,128)(2,1)S(1)} all-gather(f16[16,264,128]{2,1,0:T(8,128)(2,1)S(1)} %bitcast.16), channel_id=4, replica_groups=mesh['layer'=8,'z'=16,'xh'=2,'c'=2] {'c'}, dimensions={0}, use_global_device_ids=true | all-gather | bytes 3244032 | tf_op jit(solution)/shard_map/all_gather | solution.py:161
  90.7 0.0 copy-start
  90.7 0.2 fusion.3
  90.9 0.6 multiply_convert_fusion.blocks
  91.5 1.1 copy-done
  92.6 1.3 %shard_map.39.here = bf16[256,384]{1,0:T(8,128)(2,1)S(1)} custom-call(bf16[2,16,256,128]{3,2,1,0:T(8,128)(2,1)S(1)} %multiply_convert_fusion.blocks, bf16[384,4096]{1,0:T(8,128)(2,1)S(1)} %bitcast.9), custom_call_target="tpu_custom_call" | custom-call | flops 805306368 | bytes 1048576 | tf_op jit(solution)/shard_map/pallas_call | solution.py:125
  93.9 0.0 collective-permute-done.1.train
  93.9 1.3 %shard_map.40 = bf16[8,2,32,384]{3,2,1,0:T(8,128)(2,1)S(1)} custom-call(bf16[2,16,256,128]{3,2,1,0:T(8,128)(2,1)S(1)} %multiply_convert_fusion.blocks, bf16[256,384]{1,0:T(8,128)(2,1)S(1)} %shard_map.39.here, bf16[384,4096]{1,0:T(8,128)(2,1)S(1)} %collective-permute-done.1.train), custom_call_target="tpu_custom_call" | custom-call | flops 805306368 | bytes 1048576 | tf_op jit(solution)/shard_map/pallas_call | solution.py:125
  95.2 14.7 %all_to_all.5.parts = bf16[16,32,384]{2,1,0:T(8,128)(2,1)S(1)} all-to-all(bf16[16,32,384]{2,1,0:T(8,128)(2,1)S(1)} %bitcast.10), channel_id=1, replica_groups=mesh['layer'=8,'z'=16,'xh'=2,'c'=2] {'layer','xh'}, dimensions={0} | all-to-all | bytes 786432 | tf_op jit(solution)/shard_map/all_to_all | solution.py:168
  110.0 0.7 shard_map.41
  (2 shorter events, 0.0 us)
Async XLA Ops:
  0.0 52.8 %collective-permute-start = (bf16[64,4096]{1,0:T(8,128)(2,1)}, bf16[64,4096]{1,0:T(8,128)(2,1)S(1)}, u32[]{:S(2)}, u32[]{:S(2)}) collective-permute-start(bf16[64,4096]{1,0:T(8,128)(2,1)} %bitcast.11), channel_id=1, source_target_pairs={{0,2},{2,0},{1,3},{3,1},{4,6},{6,4},{5,7},{7,5},{8,10},{10,8},{9,1... | collective-permute-start | bytes 1572872 | tf_op jit(solution)/shard_map/ppermute | solution.py:142
  5.5 88.4 %collective-permute-start.1 = (bf16[384,4096]{1,0:T(8,128)(2,1)}, bf16[384,4096]{1,0:T(8,128)(2,1)S(1)}, u32[]{:S(2)}, u32[]{:S(2)}) collective-permute-start(bf16[384,4096]{1,0:T(8,128)(2,1)} %bitcast.8), channel_id=1, source_target_pairs={{0,2},{2,0},{1,3},{3,1},{4,6},{6,4},{5,7},{7,5},{8,10},{10,8},{9,1... | collective-permute-start | bytes 9437192 | tf_op jit(solution)/shard_map/ppermute | solution.py:143
  7.4 0.8 copy-start.2
  52.8 1.0 copy-start.1
  90.7 1.9 %copy-start = (bf16[1,384,4096]{2,1,0:T(8,128)(2,1)S(1)}, bf16[1,384,4096]{2,1,0:T(8,128)(2,1)}, u32[]{:S(2)}) copy-start(bf16[1,384,4096]{2,1,0:T(8,128)(2,1)} %param.5) | copy-start | bytes 9437188

commit v11 on v10

--- a/solution.py
+++ b/solution.py
@@ -92,10 +92,11 @@
     out[...] = jnp.concatenate([value * jnp.exp2(TOP - exponent), tail], axis=0)
 
 
-def scores(blocks, train):
+def scores(blocks, train, arrive=lambda z: None):
     half = blocks.shape[3] // 2
     total = jnp.zeros((blocks.shape[2], train.shape[0]), jnp.float32)
     for z in range(blocks.shape[1]):
+        arrive(z)
         straight = core_at(0, z) == 0
         one = jnp.where(straight, blocks[0, z], blocks[1, z])
         two = jnp.where(straight, blocks[1, z], blocks[0, z])
@@ -105,8 +106,21 @@
     return total
 
 
-def here_kernel(blocks, train, out):
-    out[...] = scores(blocks, train).astype(out.dtype)
+def here_kernel(blocks, train, out, held, done):
+    count = done.shape[0]
+    span = train.shape[1] // count
+    copies = []
+    for part in range(count):
+        columns = pl.ds(part * span, span)
+        copies.append(pltpu.make_async_copy(train.at[:, columns], held.at[:, columns], done.at[part]))
+        copies[-1].start()
+    each = blocks.shape[1] // count
+
+    def arrive(z):
+        if z % each == 0:
+            copies[z // each].wait()
+
+    out[...] = scores(blocks, held, arrive).astype(out.dtype)
 
 
 def there_kernel(blocks, here, train, out):
@@ -119,16 +133,16 @@
         out[layer, 1 - chip] = there[piece]
 
 
-def in_vmem(kernel, out_shape, *operands, scratch=()):
+def in_vmem(kernel, out_shape, *operands, scratch=(), outside=None, room=40):
     flops = 2 * operands[0].size * operands[-1].shape[0]
     spec = pl.BlockSpec(memory_space=pltpu.VMEM)
     return pl.pallas_call(
         kernel,
         out_shape=out_shape,
-        in_specs=[spec] * len(operands),
+        in_specs=[pl.BlockSpec(memory_space=pl.ANY) if i == outside else spec for i in range(len(operands))],
         out_specs=spec,
         scratch_shapes=scratch,
-        compiler_params=pltpu.CompilerParams(vmem_limit_bytes=40 * 2**20),
+        compiler_params=pltpu.CompilerParams(vmem_limit_bytes=room * 2**20),
         cost_estimate=pl.CostEstimate(flops=flops, bytes_accessed=2**20, transcendentals=0),
     )(*operands)
 
@@ -161,7 +175,15 @@
     blocks = lax.all_gather(gather_z(chunk.astype(jnp.float16), groups), "c", axis=0)
     back = jnp.exp2(blocks[:, :, height : height + 1, :1].astype(jnp.float32) - TOP)
     blocks = (blocks[:, :, :height].astype(jnp.float32) * back).astype(jnp.bfloat16)
-    here = in_vmem(here_kernel, jax.ShapeDtypeStruct((height, train.shape[0]), jnp.bfloat16), blocks, train)
+    here = in_vmem(
+        here_kernel,
+        jax.ShapeDtypeStruct((height, train.shape[0]), jnp.bfloat16),
+        blocks,
+        train,
+        scratch=[pltpu.VMEM(train.shape, train.dtype), pltpu.SemaphoreType.DMA((4,))],
+        outside=1,
+        room=51,
+    )
     parts_shape = jax.ShapeDtypeStruct((layers, 2, height // layers, train.shape[0]), jnp.bfloat16)
     parts = in_vmem(there_kernel, parts_shape, blocks, here, train_got)
 

time: 112 us -> 112 us (level)
  Pallas kernels: 4.25 us -> 5.77 us
    pallas_call x5, Pallas kernels: 4.25 us -> 5.77 us  [in_vmem(): pl.pallas_call(kernel, out_shape=out_shape, in_specs=[pl.BlockSpec(memory...]
    unnamed x6 -> x4, local copies, waits for them, and re-layouts: 2.26 us -> 1.2 us
  transfers between devices with their start and end apart: 2 -> 2, of which waited for: 0 -> 0; matrix products, arithmetic and copies ran while one was open for 1% -> 1% of each run, Pallas kernels for 2% -> 3%
where the time goes in v11:
time: 112 us; the launch traced here: 111 us
  blocking collectives  95.1 us (85%)
  starting transfers between devices  7.39 us (7%)
  Pallas kernels  5.77 us (5%)
  other arithmetic  1.5 us (1%)
  local copies, waits for them, and re-layouts  1.2 us (1%)
    all_gather x2, blocking collectives, gather_z(): return lax.all_gather(x, AXES, axis=0, axis_index_groups=groups)  73.7 us
    all_to_all x1, blocking collectives, on_device(): lax.all_to_all(parts.reshape(2 * layers, height // layers, -1), ('layer',...  14.8 us
    pallas_call x5, Pallas kernels, in_vmem(): pl.pallas_call(kernel, out_shape=out_shape, in_specs=[pl.BlockSpec(memory...  5.77 us
    ppermute x1, starting transfers between devices, on_device(): fisher_got = lax.ppermute(mine, 'xh', SWAP)  5.47 us
    all_gather x1, blocking collectives, on_device(): lax.all_gather(gather_z(chunk.astype(jnp.float16), groups), 'c', axis=0)  3.36 us
    all_gather x1, blocking collectives, on_device(): rows = lax.all_gather(rows, 'c', axis=0, tiled=True)  3.34 us
  transfers between devices with their start and end apart: 2, of which 0 were waited for; matrix products, arithmetic and copies ran while one was open for 1% of the time, Pallas kernels for 3%

profile of v11, /device:TPU:1, one launch (start us, length us, event | category | flops | bytes accessed | tf_op | source)
XLA Modules:
  0.0 111.1 jit_solution(8672675748866597681)
XLA Ops:
  0.0 5.5 %collective-permute-start = (bf16[64,4096]{1,0:T(8,128)(2,1)}, bf16[64,4096]{1,0:T(8,128)(2,1)S(1)}, u32[]{:S(2)}, u32[]{:S(2)}) collective-permute-start(bf16[64,4096]{1,0:T(8,128)(2,1)} %bitcast.9), channel_id=1, source_target_pairs={{0,2},{2,0},{1,3},{3,1},{4,6},{6,4},{5,7},{7,5},{8,10},{10,8},{9,1... | collective-permute-start | bytes 1572872 | tf_op jit(solution)/shard_map/ppermute | solution.py:156
  5.5 1.9 %collective-permute-start.1 = (bf16[384,4096]{1,0:T(8,128)(2,1)}, bf16[384,4096]{1,0:T(8,128)(2,1)S(1)}, u32[]{:S(2)}, u32[]{:S(2)}) collective-permute-start(bf16[384,4096]{1,0:T(8,128)(2,1)} %bitcast.15), channel_id=1, source_target_pairs={{0,2},{2,0},{1,3},{3,1},{4,6},{6,4},{5,7},{7,5},{8,10},{10,8},{9,1... | collective-permute-start | bytes 9437192 | tf_op jit(solution)/shard_map/ppermute | solution.py:157
  7.4 0.0 copy-start.1
  7.4 0.8 copy-done.1
  8.3 0.1 shard_map.37
  8.4 41.1 %all-gather.7 = f16[128,4224]{1,0:T(8,128)(2,1)S(1)} all-gather(f16[8,4224]{1,0:T(8,128)(2,1)S(1)} %convert_element_type.24), channel_id=2, replica_groups={{0,5,8,13,16,21,24,29,32,37,40,45,48,53,56,61},{1,4,9,12,17,20,25,28,33..., dimensions={0}, use_global_device_ids=true | all-gather | bytes 1148928 | tf_op jit(solution)/shard_map/all_gather | solution.py:21
  49.5 3.3 %all-gather.8 = f16[256,4224]{1,0:T(8,128)(2,1)S(1)} all-gather(f16[128,4224]{1,0:T(8,128)(2,1)S(1)} %all-gather.7), channel_id=1, replica_groups=mesh['layer'=8,'z'=16,'xh'=2,'c'=2] {'c'}, dimensions={0}, use_global_device_ids=true | all-gather | bytes 3244032 | tf_op jit(solution)/shard_map/all_gather | solution.py:161
  52.8 0.0 copy-start
  52.8 0.0 collective-permute-done.got
  52.8 0.1 exponential_reduce_fusion
  52.9 0.5 multiply_convert_fusion.1.rows
  53.5 0.4 copy-done
  53.8 0.8 shard_map.38
  54.7 32.6 %all-gather.9 = f16[4224,128]{1,0:T(8,128)(2,1)S(1)} all-gather(f16[264,128]{1,0:T(8,128)(2,1)S(1)} %convert_element_type.28), channel_id=3, replica_groups={{0,5,8,13,16,21,24,29,32,37,40,45,48,53,56,61},{1,4,9,12,17,20,25,28,33..., dimensions={0}, use_global_device_ids=true | all-gather | bytes 1148928 | tf_op jit(solution)/shard_map/all_gather | solution.py:21
  87.3 3.4 %all-gather.10 = f16[32,264,128]{2,1,0:T(8,128)(2,1)S(1)} all-gather(f16[16,264,128]{2,1,0:T(8,128)(2,1)S(1)} %bitcast.14), channel_id=4, replica_groups=mesh['layer'=8,'z'=16,'xh'=2,'c'=2] {'c'}, dimensions={0}, use_global_device_ids=true | all-gather | bytes 3244032 | tf_op jit(solution)/shard_map/all_gather | solution.py:175
  90.7 0.2 fusion.3
  90.9 0.6 multiply_convert_fusion.blocks
  91.5 2.8 %shard_map.39.here = bf16[256,384]{1,0:T(8,128)(2,1)S(1)} custom-call(bf16[2,16,256,128]{3,2,1,0:T(8,128)(2,1)S(1)} %multiply_convert_fusion.blocks, bf16[384,4096]{1,0:T(8,128)(2,1)} %bitcast.16), custom_call_target="tpu_custom_call" | custom-call | flops 805306368 | bytes 1048576 | tf_op jit(solution)/shard_map/pallas_call | solution.py:139
  94.3 0.0 collective-permute-done.1.train
  94.4 1.3 %shard_map.40 = bf16[8,2,32,384]{3,2,1,0:T(8,128)(2,1)S(1)} custom-call(bf16[2,16,256,128]{3,2,1,0:T(8,128)(2,1)S(1)} %multiply_convert_fusion.blocks, bf16[256,384]{1,0:T(8,128)(2,1)S(1)} %shard_map.39.here, bf16[384,4096]{1,0:T(8,128)(2,1)S(1)} %collective-permute-done.1.train), custom_call_target="tpu_custom_call" | custom-call | flops 805306368 | bytes 1048576 | tf_op jit(solution)/shard_map/pallas_call | solution.py:139
  95.7 14.8 %all_to_all.5.parts = bf16[16,32,384]{2,1,0:T(8,128)(2,1)S(1)} all-to-all(bf16[16,32,384]{2,1,0:T(8,128)(2,1)S(1)} %bitcast.8), channel_id=1, replica_groups=mesh['layer'=8,'z'=16,'xh'=2,'c'=2] {'layer','xh'}, dimensions={0} | all-to-all | bytes 786432 | tf_op jit(solution)/shard_map/all_to_all | solution.py:190
  110.4 0.7 shard_map.41
  (2 shorter events, 0.0 us)
Async XLA Ops:
  0.0 52.8 %collective-permute-start = (bf16[64,4096]{1,0:T(8,128)(2,1)}, bf16[64,4096]{1,0:T(8,128)(2,1)S(1)}, u32[]{:S(2)}, u32[]{:S(2)}) collective-permute-start(bf16[64,4096]{1,0:T(8,128)(2,1)} %bitcast.9), channel_id=1, source_target_pairs={{0,2},{2,0},{1,3},{3,1},{4,6},{6,4},{5,7},{7,5},{8,10},{10,8},{9,1... | collective-permute-start | bytes 1572872 | tf_op jit(solution)/shard_map/ppermute | solution.py:156
  5.5 88.9 %collective-permute-start.1 = (bf16[384,4096]{1,0:T(8,128)(2,1)}, bf16[384,4096]{1,0:T(8,128)(2,1)S(1)}, u32[]{:S(2)}, u32[]{:S(2)}) collective-permute-start(bf16[384,4096]{1,0:T(8,128)(2,1)} %bitcast.15), channel_id=1, source_target_pairs={{0,2},{2,0},{1,3},{3,1},{4,6},{6,4},{5,7},{7,5},{8,10},{10,8},{9,1... | collective-permute-start | bytes 9437192 | tf_op jit(solution)/shard_map/ppermute | solution.py:157
  7.4 0.8 copy-start.1
  52.8 1.0 copy-start

commit v12 on v11

--- a/solution.py
+++ b/solution.py
@@ -113,12 +113,15 @@
     for part in range(count):
         columns = pl.ds(part * span, span)
         copies.append(pltpu.make_async_copy(train.at[:, columns], held.at[:, columns], done.at[part]))
-        copies[-1].start()
     each = blocks.shape[1] // count
+    for copy in copies[:2]:
+        copy.start()
 
     def arrive(z):
         if z % each == 0:
             copies[z // each].wait()
+            for copy in copies[z // each + 2 : z // each + 3]:
+                copy.start()
 
     out[...] = scores(blocks, held, arrive).astype(out.dtype)
 
@@ -180,7 +183,7 @@
         jax.ShapeDtypeStruct((height, train.shape[0]), jnp.bfloat16),
         blocks,
         train,
-        scratch=[pltpu.VMEM(train.shape, train.dtype), pltpu.SemaphoreType.DMA((4,))],
+        scratch=[pltpu.VMEM(train.shape, train.dtype), pltpu.SemaphoreType.DMA((min(8, slots),))],
         outside=1,
         room=51,
     )

time: 112 us -> 114 us (1.018)
  Pallas kernels: 5.77 us -> 7.69 us
    pallas_call x5, Pallas kernels: 5.77 us -> 7.69 us  [in_vmem(): pl.pallas_call(kernel, out_shape=out_shape, in_specs=[pl.BlockSpec(memory...]
  transfers between devices with their start and end apart: 2 -> 2, of which waited for: 0 -> 0; matrix products, arithmetic and copies ran while one was open for 1% -> 1% of each run, Pallas kernels for 3% -> 5%
where the time goes in v12:
time: 114 us; the launch traced here: 113 us
  blocking collectives  95.1 us (83%)
  Pallas kernels  7.69 us (7%)
  starting transfers between devices  7.39 us (6%)
  other arithmetic  1.5 us (1%)
  local copies, waits for them, and re-layouts  1.2 us (1%)
    all_gather x2, blocking collectives, gather_z(): return lax.all_gather(x, AXES, axis=0, axis_index_groups=groups)  73.7 us
    all_to_all x1, blocking collectives, on_device(): lax.all_to_all(parts.reshape(2 * layers, height // layers, -1), ('layer',...  14.7 us
    pallas_call x5, Pallas kernels, in_vmem(): pl.pallas_call(kernel, out_shape=out_shape, in_specs=[pl.BlockSpec(memory...  7.69 us
    ppermute x1, starting transfers between devices, on_device(): fisher_got = lax.ppermute(mine, 'xh', SWAP)  5.47 us
    all_gather x1, blocking collectives, on_device(): lax.all_gather(gather_z(chunk.astype(jnp.float16), groups), 'c', axis=0)  3.36 us
    all_gather x1, blocking collectives, on_device(): rows = lax.all_gather(rows, 'c', axis=0, tiled=True)  3.34 us
  transfers between devices with their start and end apart: 2, of which 0 were waited for; matrix products, arithmetic and copies ran while one was open for 1% of the time, Pallas kernels for 5%

profile of v12, /device:TPU:1, one launch (start us, length us, event | category | flops | bytes accessed | tf_op | source)
XLA Modules:
  0.0 113.0 jit_solution(17669997426992892313)
XLA Ops:
  0.0 5.5 %collective-permute-start = (bf16[64,4096]{1,0:T(8,128)(2,1)}, bf16[64,4096]{1,0:T(8,128)(2,1)S(1)}, u32[]{:S(2)}, u32[]{:S(2)}) collective-permute-start(bf16[64,4096]{1,0:T(8,128)(2,1)} %bitcast.9), channel_id=1, source_target_pairs={{0,2},{2,0},{1,3},{3,1},{4,6},{6,4},{5,7},{7,5},{8,10},{10,8},{9,1... | collective-permute-start | bytes 1572872 | tf_op jit(solution)/shard_map/ppermute | solution.py:159
  5.5 1.9 %collective-permute-start.1 = (bf16[384,4096]{1,0:T(8,128)(2,1)}, bf16[384,4096]{1,0:T(8,128)(2,1)S(1)}, u32[]{:S(2)}, u32[]{:S(2)}) collective-permute-start(bf16[384,4096]{1,0:T(8,128)(2,1)} %bitcast.15), channel_id=1, source_target_pairs={{0,2},{2,0},{1,3},{3,1},{4,6},{6,4},{5,7},{7,5},{8,10},{10,8},{9,1... | collective-permute-start | bytes 9437192 | tf_op jit(solution)/shard_map/ppermute | solution.py:160
  7.4 0.0 copy-start.1
  7.4 0.8 copy-done.1
  8.3 0.1 shard_map.37
  8.4 41.1 %all-gather.7 = f16[128,4224]{1,0:T(8,128)(2,1)S(1)} all-gather(f16[8,4224]{1,0:T(8,128)(2,1)S(1)} %convert_element_type.24), channel_id=2, replica_groups={{0,5,8,13,16,21,24,29,32,37,40,45,48,53,56,61},{1,4,9,12,17,20,25,28,33..., dimensions={0}, use_global_device_ids=true | all-gather | bytes 1148928 | tf_op jit(solution)/shard_map/all_gather | solution.py:21
  49.5 3.3 %all-gather.8 = f16[256,4224]{1,0:T(8,128)(2,1)S(1)} all-gather(f16[128,4224]{1,0:T(8,128)(2,1)S(1)} %all-gather.7), channel_id=1, replica_groups=mesh['layer'=8,'z'=16,'xh'=2,'c'=2] {'c'}, dimensions={0}, use_global_device_ids=true | all-gather | bytes 3244032 | tf_op jit(solution)/shard_map/all_gather | solution.py:164
  52.8 0.0 copy-start
  52.8 0.0 collective-permute-done.got
  52.8 0.1 exponential_reduce_fusion
  52.9 0.5 multiply_convert_fusion.1.rows
  53.5 0.4 copy-done
  53.8 0.8 shard_map.38
  54.7 32.6 %all-gather.9 = f16[4224,128]{1,0:T(8,128)(2,1)S(1)} all-gather(f16[264,128]{1,0:T(8,128)(2,1)S(1)} %convert_element_type.28), channel_id=3, replica_groups={{0,5,8,13,16,21,24,29,32,37,40,45,48,53,56,61},{1,4,9,12,17,20,25,28,33..., dimensions={0}, use_global_device_ids=true | all-gather | bytes 1148928 | tf_op jit(solution)/shard_map/all_gather | solution.py:21
  87.3 3.4 %all-gather.10 = f16[32,264,128]{2,1,0:T(8,128)(2,1)S(1)} all-gather(f16[16,264,128]{2,1,0:T(8,128)(2,1)S(1)} %bitcast.14), channel_id=4, replica_groups=mesh['layer'=8,'z'=16,'xh'=2,'c'=2] {'c'}, dimensions={0}, use_global_device_ids=true | all-gather | bytes 3244032 | tf_op jit(solution)/shard_map/all_gather | solution.py:178
  90.7 0.2 fusion.3
  90.9 0.6 multiply_convert_fusion.blocks
  91.5 4.7 %shard_map.39.here = bf16[256,384]{1,0:T(8,128)(2,1)S(1)} custom-call(bf16[2,16,256,128]{3,2,1,0:T(8,128)(2,1)S(1)} %multiply_convert_fusion.blocks, bf16[384,4096]{1,0:T(8,128)(2,1)} %bitcast.16), custom_call_target="tpu_custom_call" | custom-call | flops 805306368 | bytes 1048576 | tf_op jit(solution)/shard_map/pallas_call | solution.py:142
  96.3 0.0 collective-permute-done.1.train
  96.3 1.3 %shard_map.40 = bf16[8,2,32,384]{3,2,1,0:T(8,128)(2,1)S(1)} custom-call(bf16[2,16,256,128]{3,2,1,0:T(8,128)(2,1)S(1)} %multiply_convert_fusion.blocks, bf16[256,384]{1,0:T(8,128)(2,1)S(1)} %shard_map.39.here, bf16[384,4096]{1,0:T(8,128)(2,1)S(1)} %collective-permute-done.1.train), custom_call_target="tpu_custom_call" | custom-call | flops 805306368 | bytes 1048576 | tf_op jit(solution)/shard_map/pallas_call | solution.py:142
  97.6 14.7 %all_to_all.5.parts = bf16[16,32,384]{2,1,0:T(8,128)(2,1)S(1)} all-to-all(bf16[16,32,384]{2,1,0:T(8,128)(2,1)S(1)} %bitcast.8), channel_id=1, replica_groups=mesh['layer'=8,'z'=16,'xh'=2,'c'=2] {'layer','xh'}, dimensions={0} | all-to-all | bytes 786432 | tf_op jit(solution)/shard_map/all_to_all | solution.py:193
  112.3 0.7 shard_map.41
  (2 shorter events, 0.0 us)
Async XLA Ops:
  0.0 52.8 %collective-permute-start = (bf16[64,4096]{1,0:T(8,128)(2,1)}, bf16[64,4096]{1,0:T(8,128)(2,1)S(1)}, u32[]{:S(2)}, u32[]{:S(2)}) collective-permute-start(bf16[64,4096]{1,0:T(8,128)(2,1)} %bitcast.9), channel_id=1, source_target_pairs={{0,2},{2,0},{1,3},{3,1},{4,6},{6,4},{5,7},{7,5},{8,10},{10,8},{9,1... | collective-permute-start | bytes 1572872 | tf_op jit(solution)/shard_map/ppermute | solution.py:159
  5.5 90.8 %collective-permute-start.1 = (bf16[384,4096]{1,0:T(8,128)(2,1)}, bf16[384,4096]{1,0:T(8,128)(2,1)S(1)}, u32[]{:S(2)}, u32[]{:S(2)}) collective-permute-start(bf16[384,4096]{1,0:T(8,128)(2,1)} %bitcast.15), channel_id=1, source_target_pairs={{0,2},{2,0},{1,3},{3,1},{4,6},{6,4},{5,7},{7,5},{8,10},{10,8},{9,1... | collective-permute-start | bytes 9437192 | tf_op jit(solution)/shard_map/ppermute | solution.py:160
  7.4 0.8 copy-start.1
  52.8 1.0 copy-start
